TPU v7x, 32 devices: a whole 2x2x4 slice. The times are simulated.
32 devices in a mesh: section: 8 (over y, x, core), inner: 4 (over z).
Axes of the slice: x: 2, y: 2, z: 4, core: 2. Of those that a mesh axis runs over, the one named last changes fastest.
Arguments:
- tokens: bfloat16 [2, 128, 3072], P(None, 'section'), may hold values from -6 to 6
- norm_gain: float32 [3072], replicated, may hold values from 0.5 to 1.5
- router: bfloat16 [3072, 8], replicated, may hold values from -0.21875 to 0.21875
- expert_in: bfloat16 [8, 2, 1024, 3072], P('section', None, 'inner'), may hold values from -0.109375 to 0.109375
- expert_out: bfloat16 [8, 1024, 3072], P('section', 'inner'), may hold values from -0.375 to 0.375
- choices: int32 [2, 128, 2], P(None, 'section'), may hold values from 0 to 7, all different within a row; in each aligned block of 16 rows (0 to 15, 16 to 31, ..., all dimensions but the last counted through in order) at most 8 rows name the same one
Outputs:
- layer_outputs: bfloat16 [2, 128, 3072], P(None, 'section', 'inner')
Inputs may be any that keep to these rules, and one draw needn't show every extreme that they name: `choices`: the two experts of a row differ; in each micro-batch the 16 rows of one section name any expert at most 8 times.
All inputs are finite; a program needn't handle non-finite values.
Results may differ from a plain program's by a relative error of at most 0.019.
Values may be sent and summed in bfloat16 or wider, within the bound.
No kernel may reach another device: no remote copies, remote signals or barrier semaphores. Data moves between devices by JAX's collectives and lax.ppermute only.
A program may use at most 128 MiB of HBM per device.

v0:
```python
import jax
import jax.numpy as jnp
from jax import lax
from jax.sharding import PartitionSpec as P

epsilon = 1e-05


def prepare(row_block, chosen, norm_scale, router_w, sections, capacity):
    experts = router_w.shape[1]
    model_width = row_block.shape[1]
    values = row_block.astype(jnp.float32)
    inv_rms = lax.rsqrt(jnp.mean(values * values, axis=-1, keepdims=True) + epsilon)
    normed = (values * inv_rms * norm_scale).astype(jnp.bfloat16)
    logits = jnp.dot(normed, router_w, preferred_element_type=jnp.float32)
    expert_ids = jnp.arange(experts, dtype=jnp.int32)
    first_hot = (chosen[:, 0:1] == expert_ids[None, :]).astype(jnp.float32)
    second_hot = (chosen[:, 1:2] == expert_ids[None, :]).astype(jnp.float32)
    lead_logit = jnp.sum(logits * first_hot, axis=1, keepdims=True)
    trail_logit = jnp.sum(logits * second_hot, axis=1, keepdims=True)
    weight_a = 1.0 / (1.0 + jnp.exp(trail_logit - lead_logit))
    weight_b = 1.0 / (1.0 + jnp.exp(lead_logit - trail_logit))
    mixing = weight_a * first_hot + weight_b * second_hot
    hot_count = (chosen[:, 0:1] == expert_ids[None, :]).astype(jnp.int32) + (
        chosen[:, 1:2] == expert_ids[None, :]
    ).astype(jnp.int32)
    slot_rank = jnp.cumsum(hot_count, axis=0) - hot_count
    slot_ids = jnp.arange(capacity, dtype=jnp.int32)
    placed = (
        hot_count[:, :, None] * (slot_rank[:, :, None] == slot_ids[None, None, :]).astype(jnp.int32)
    ).astype(jnp.float32)
    picked = jnp.einsum(
        "rec,rd->ecd", placed.astype(jnp.bfloat16), normed, preferred_element_type=jnp.float32
    ).astype(jnp.bfloat16)
    per_expert = sections // experts
    outgoing = jnp.broadcast_to(picked[:, None], (experts, per_expert, capacity, model_width))
    outgoing = outgoing.reshape(sections, capacity, model_width)
    slot_weights = mixing[:, :, None] * placed
    return (values, outgoing, slot_weights)


def combine(returned_part, slot_weights):
    experts = slot_weights.shape[1]
    capacity = slot_weights.shape[2]
    per_expert = returned_part.shape[0] // experts
    merged = jnp.sum(
        returned_part.astype(jnp.float32).reshape(
            experts, per_expert, capacity, returned_part.shape[2]
        ),
        axis=1,
    )
    return jnp.einsum("rec,ecx->rx", slot_weights, merged, precision=lax.Precision.HIGHEST)


def body(tokens, norm_gain, router, expert_in, expert_out, choices):
    sections = lax.axis_size("section")
    inner_count = lax.axis_size("inner")
    member = lax.axis_index("inner")
    micro_count = tokens.shape[0]
    row_count = tokens.shape[1]
    model_width = tokens.shape[2]
    capacity = row_count // 2
    width_part = model_width // inner_count
    hidden_dev = expert_in.shape[2]
    stacked_in = expert_in[0].reshape(2 * hidden_dev, model_width)
    down_rows = expert_out[0]
    prepared = [
        prepare(tokens[micro_idx], choices[micro_idx], norm_gain, router, sections, capacity)
        for micro_idx in range(micro_count)
    ]
    groups = [[micro_idx] for micro_idx in range(micro_count)]
    results = []
    for batch_group in groups:
        outgoing = jnp.concatenate([prepared[micro_idx][1] for micro_idx in batch_group], axis=1)
        received = lax.all_to_all(outgoing, "section", split_axis=0, concat_axis=0, tiled=True)
        source_count = received.shape[0]
        slot_count = received.shape[1]
        flat_rows = received.reshape(source_count * slot_count, model_width)
        gate_up = lax.dot_general(
            flat_rows, stacked_in, (((1,), (1,)), ((), ())), preferred_element_type=jnp.float32
        )
        active = (jax.nn.silu(gate_up[:, :hidden_dev]) * gate_up[:, hidden_dev:]).astype(
            jnp.bfloat16
        )
        partial_value = jnp.dot(active, down_rows, preferred_element_type=jnp.float32).astype(
            jnp.bfloat16
        )
        partial_value = partial_value.reshape(source_count, slot_count, model_width)
        returned = lax.all_to_all(partial_value, "section", split_axis=0, concat_axis=0, tiled=True)
        combined = jnp.stack(
            [
                combine(returned, prepared[micro_idx][2])
                for index_pos, micro_idx in enumerate(batch_group)
            ]
        )
        moe_part = lax.psum_scatter(
            combined.astype(jnp.bfloat16), "inner", scatter_dimension=2, tiled=True
        ).astype(jnp.float32)
        for index_pos, micro_idx in enumerate(batch_group):
            residual = lax.dynamic_slice_in_dim(
                prepared[micro_idx][0], member * width_part, width_part, 1
            )
            results.append((residual + moe_part[index_pos]).astype(jnp.bfloat16))
    return jnp.stack(results)


def solution(mesh):
    return jax.shard_map(
        body,
        mesh=mesh,
        in_specs=(
            P(None, "section", None),
            P(),
            P(),
            P("section", None, "inner", None),
            P("section", "inner", None),
            P(None, "section", None),
        ),
        out_specs=P(None, "section", "inner"),
        check_vma=False,
    )
```

profile of v0, /device:TPU:0, one launch (start us, length us, event | category | flops | bytes accessed | tf_op | source)
XLA Modules:
  0.0 113.1 jit_solution(4731805229870882505)
XLA Ops:
  6.5 1.8 %fusion.17 = (f32[16]{0:T(128)S(1)}, f32[16]{0:T(128)}) fusion(bf16[2,16,3072]{2,1,0:T(8,128)(2,1)} %param.6), kind=kLoop, calls=%fused_computation.27 | loop fusion | flops 294880 | bytes 196736 | tf_op jit(solution)/shard_map/reduce_sum | solution.py:13
  8.3 0.7 slice_bitcast_fusion.1
  9.8 2.0 %convolution_convert_fusion.3 = bf16[8,8,3072]{2,1,0:T(8,128)(2,1)} fusion(bf16[16,8,8]{0,1,2:T(8,128)(2,1)S(1)} %convert_convert_fusion.1, f32[3072]{0:T(1024)} %param.7, f32[16]{0:T(128)S(1)} %add_rsqrt_fusion.1, bf16[2,16,3072]{2,1,0:T(8,128)(2,1)} %param.6), kind=kOutput, calls=%fused_computation.3 | convolution fusion | flops 6684672 | bytes 505920 | tf_op jit(solution)/shard_map/rec,rd->ecd/dot_general | solution.py:32
  11.8 5.2 %all-to-all-start = ((bf16[8,8,3072]{2,1,0:T(8,128)(2,1)}), bf16[8,8,3072]{2,1,0:T(8,128)(2,1)S(1)}, u32[]{:S(2)}, u32[]{:S(2)}) async-start(bf16[8,8,3072]{2,1,0:T(8,128)(2,1)} %convolution_convert_fusion.3), calls=%async_computation | async-start | bytes 786432 | tf_op jit(solution)/shard_map/all_to_all | solution.py:75
  16.9 1.7 %slice_convert_fusion.1 = (f32[1,16,3072]{2,1,0:T(8,128)}, f32[1,16,3072]{2,1,0:T(8,128)}) fusion(bf16[2,16,3072]{2,1,0:T(8,128)(2,1)} %param.6), kind=kLoop, calls=%fused_computation.33 | loop fusion | flops 98304 | bytes 589824 | tf_op jit(solution)/shard_map/convert_element_type | solution.py:12
  19.3 1.7 %select_reduce_fusion.3 = (f32[16]{0:T(128)}, f32[16]{0:T(128)}) fusion(s32[16]{0:T(128)S(1)} %get-tuple-element.23, s32[16]{0:T(128)} %copy-done.5, bf16[3072,8]{0,1:T(8,128)(2,1)} %param.8, f32[3072]{0:T(1024)} %param.7, f32[16]{0:T(128)} %copy-done.6, bf16[2,16,3072]{2,1,0:T(8,128)(2,1)} %param.6), kind=kOutput, calls=%fused_computation.74 | convolution fusion | flops 983776 | bytes 160960 | tf_op jit(solution)/shard_map/dot_general | solution.py:15
  21.0 0.7 convert_add_fusion
  21.7 1.7 %select_reduce_fusion.1 = (f32[16]{0:T(128)}, f32[16]{0:T(128)}) fusion(s32[16]{0:T(128)} %get-tuple-element.22, s32[16]{0:T(128)} %get-tuple-element.21, bf16[3072,8]{0,1:T(8,128)(2,1)} %param.8, f32[16]{0:T(128)S(1)} %add_rsqrt_fusion, f32[3072]{0:T(1024)} %param.7, bf16[2,16,3072]{2,1,0:T(8,128)(2,1)} %param.6), kind=kOutput, calls=%fused_computation.68 | convolution fusion | flops 983776 | bytes 160960 | tf_op jit(solution)/shard_map/dot_general | solution.py:15
  24.1 1.3 %reduce_window_sum.18 = s32[16,8]{1,0:T(8,128)} reduce-window(s32[16,8]{1,0:T(8,128)} %copy.19, s32[]{:T(128)} %constant.31.clone.1), window={size=16x1 pad=15_0x0_0}, to_apply=%region_8.9 | reduce-window | flops 1920 | bytes 1028 | tf_op jit(solution)/shard_map/jit(cumsum)/reduce_window_sum | solution.py:27
  25.4 1.4 %copy.20 = s32[16,8]{0,1:T(8,128)} copy(s32[16,8]{1,0:T(8,128)} %reduce_window_sum.18) | data formatting | bytes 1024 | tf_op jit(solution)/shard_map/jit(cumsum)/reduce_window_sum | solution.py:27
  26.8 0.7 fusion.51
  28.1 1.3 %select_add_fusion.1 = f32[16,8]{0,1:T(8,128)} fusion(f32[16]{0:T(128)S(1)} %get-tuple-element.16, f32[16]{0:T(128)S(1)} %get-tuple-element.15, s32[16]{0:T(128)} %copy-done.4, s32[16]{0:T(128)} %copy-done.5), kind=kLoop, calls=%fused_computation.72 | loop fusion | flops 640 | bytes 768 | tf_op jit(solution)/shard_map/add | solution.py:23
  29.4 1.3 %add_divide_fusion.1 = (f32[16]{0:T(128)}, f32[16]{0:T(128)}) fusion(f32[16]{0:T(128)} %get-tuple-element.9, f32[16]{0:T(128)} %get-tuple-element.10), kind=kLoop, calls=%fused_computation.82 | loop fusion | flops 96 | bytes 256 | tf_op jit(solution)/shard_map/div | solution.py:21
  30.7 2.0 %convolution_convert_fusion.2 = bf16[8,8,3072]{2,1,0:T(8,128)(2,1)} fusion(bf16[16,8,8]{0,1,2:T(8,128)(2,1)S(1)} %convert_convert_fusion, f32[16]{0:T(128)} %copy-done.7, f32[3072]{0:T(1024)} %param.7, bf16[2,16,3072]{2,1,0:T(8,128)(2,1)} %param.6), kind=kOutput, calls=%fused_computation.2 | convolution fusion | flops 6684672 | bytes 506368 | tf_op jit(solution)/shard_map/rec,rd->ecd/dot_general | solution.py:32
  32.7 4.2 %all-to-all-start.2 = ((bf16[8,8,3072]{2,1,0:T(8,128)(2,1)}), bf16[8,8,3072]{2,1,0:T(8,128)(2,1)}, u32[]{:S(2)}, u32[]{:S(2)}) async-start(bf16[8,8,3072]{2,1,0:T(8,128)(2,1)} %convolution_convert_fusion.2), calls=%async_computation.3 | async-start | bytes 786432 | tf_op jit(solution)/shard_map/all_to_all | solution.py:75
  36.9 1.1 fusion.10
  38.3 1.1 fusion
  39.4 5.9 %all-to-all-done.2 = bf16[8,8,3072]{2,1,0:T(8,128)(2,1)} async-done(((bf16[8,8,3072]{2,1,0:T(8,128)(2,1)}), bf16[8,8,3072]{2,1,0:T(8,128)(2,1)}, u32[]{:S(2)}, u32[]{:S(2)}) %all-to-all-start.2) | async-done | bytes 393248 | tf_op jit(solution)/shard_map/all_to_all | solution.py:75
  45.3 3.5 %all-to-all-start.1 = ((bf16[8,8,3072]{2,1,0:T(8,128)(2,1)}), bf16[8,8,3072]{2,1,0:T(8,128)(2,1)S(1)}, u32[]{:S(2)}, u32[]{:S(2)}) async-start(bf16[8,8,3072]{2,1,0:T(8,128)(2,1)} %fusion), calls=%async_computation.1 | async-start | bytes 786432 | tf_op jit(solution)/shard_map/all_to_all | solution.py:89
  48.8 2.2 %fusion.8 = f32[64,512]{1,0:T(8,128)S(1)} fusion(bf16[512,3072]{1,0:T(8,128)(2,1)S(1)} %bitcast.85, bf16[8,8,3072]{2,1,0:T(8,128)(2,1)} %all-to-all-done.2), kind=kOutput, calls=%fused_computation.14 | convolution fusion | flops 201326592 | bytes 3670016 | tf_op jit(solution)/shard_map/dot_general | solution.py:79
  51.0 1.1 fusion.1
  52.1 4.9 %all-to-all-done.1 = bf16[8,8,3072]{2,1,0:T(8,128)(2,1)S(1)} async-done(((bf16[8,8,3072]{2,1,0:T(8,128)(2,1)}), bf16[8,8,3072]{2,1,0:T(8,128)(2,1)S(1)}, u32[]{:S(2)}, u32[]{:S(2)}) %all-to-all-start.1) | async-done | bytes 393248 | tf_op jit(solution)/shard_map/all_to_all | solution.py:89
  57.1 0.7 copy-done.3
  57.8 3.5 %all-to-all-start.3 = ((bf16[8,8,3072]{2,1,0:T(8,128)(2,1)}), bf16[8,8,3072]{2,1,0:T(8,128)(2,1)S(1)}, u32[]{:S(2)}, u32[]{:S(2)}) async-start(bf16[8,8,3072]{2,1,0:T(8,128)(2,1)} %fusion.1), calls=%async_computation.4 | async-start | bytes 786432 | tf_op jit(solution)/shard_map/all_to_all | solution.py:89
  61.3 2.1 %fusion.5 = bf16[1,16,3072]{2,1,0:T(8,128)(2,1)} fusion(bf16[8,8,3072]{2,1,0:T(8,128)(2,1)} %copy-done.3, s32[16,8]{0,1:T(8,128)S(1)} %convert_add_fusion.1, s32[16,8]{0,1:T(8,128)S(1)} %fusion.50, f32[16,8]{0,1:T(8,128)} %select_add_fusion.1), kind=kOutput, calls=%fused_computation.11 | convolution fusion | flops 37801984 | bytes 493056 | tf_op jit(solution)/shard_map/rec,ecx->rx/dot_general | solution.py:52
  63.5 0.7 select_add_fusion
  64.2 5.3 %all-to-all-done.3 = bf16[8,8,3072]{2,1,0:T(8,128)(2,1)S(1)} async-done(((bf16[8,8,3072]{2,1,0:T(8,128)(2,1)}), bf16[8,8,3072]{2,1,0:T(8,128)(2,1)S(1)}, u32[]{:S(2)}, u32[]{:S(2)}) %all-to-all-start.3) | async-done | bytes 393248 | tf_op jit(solution)/shard_map/all_to_all | solution.py:89
  69.5 1.1 fusion.4
  70.7 14.4 %reduce-scatter.3.cloned.1.call-done = bf16[1,16,768]{2,1,0:T(8,128)(2,1)} async-done(((bf16[1,16,3072]{2,1,0:T(8,128)(2,1)}), bf16[1,16,768]{2,1,0:T(8,128)(2,1)}) %reduce-scatter.3.cloned.1.call-update) | async-done | bytes 24592 | tf_op jit(solution)/shard_map/reduce_scatter | solution.py:96
  85.1 0.8 add_convert_fusion.1
  85.9 18.9 %reduce-scatter.5.cloned.1.call-done = bf16[1,16,768]{2,1,0:T(8,128)(2,1)} async-done(((bf16[1,16,3072]{2,1,0:T(8,128)(2,1)}), bf16[1,16,768]{2,1,0:T(8,128)(2,1)}) %reduce-scatter.5.cloned.1.call-update) | async-done | bytes 24592 | tf_op jit(solution)/shard_map/reduce_scatter | solution.py:96
  104.8 0.8 add_convert_fusion
  (33 shorter events, 3.9 us)
Async XLA Ops:
  6.5 30.4 %copy-start = (bf16[1,2,256,3072]{3,2,1,0:T(8,128)(2,1)S(1)}, bf16[1,2,256,3072]{3,2,1,0:T(8,128)(2,1)}, u32[]{:S(2)}) copy-start(bf16[1,2,256,3072]{3,2,1,0:T(8,128)(2,1)} %param.9) | copy-start | bytes 9437188
  8.3 3.5 %copy-start.6 = (f32[16]{0:T(128)}, f32[16]{0:T(128)S(1)}, u32[]{:S(2)}) copy-start(f32[16]{0:T(128)S(1)} %add_rsqrt_fusion.1) | copy-start | bytes 196
  9.6 2.2 %copy-start.5 = (s32[16]{0:T(128)}, s32[16]{0:T(128)S(1)}, u32[]{:S(2)}) copy-start(s32[16]{0:T(128)S(1)} %get-tuple-element.24) | copy-start | bytes 196
  9.6 11.5 %copy-start.4 = (s32[16]{0:T(128)}, s32[16]{0:T(128)S(1)}, u32[]{:S(2)}) copy-start(s32[16]{0:T(128)S(1)} %get-tuple-element.23) | copy-start | bytes 196
  11.8 20.9 %all-to-all-start = ((bf16[8,8,3072]{2,1,0:T(8,128)(2,1)}), bf16[8,8,3072]{2,1,0:T(8,128)(2,1)S(1)}, u32[]{:S(2)}, u32[]{:S(2)}) async-start(bf16[8,8,3072]{2,1,0:T(8,128)(2,1)} %convolution_convert_fusion.3), calls=%async_computation | async-start | bytes 786432 | tf_op jit(solution)/shard_map/all_to_all | solution.py:75
  19.3 6.1 %copy-start.7 = (f32[16]{0:T(128)}, f32[16]{0:T(128)S(1)}, u32[]{:S(2)}) copy-start(f32[16]{0:T(128)S(1)} %add_rsqrt_fusion) | copy-start | bytes 196
  32.7 12.6 %all-to-all-start.2 = ((bf16[8,8,3072]{2,1,0:T(8,128)(2,1)}), bf16[8,8,3072]{2,1,0:T(8,128)(2,1)}, u32[]{:S(2)}, u32[]{:S(2)}) async-start(bf16[8,8,3072]{2,1,0:T(8,128)(2,1)} %convolution_convert_fusion.2), calls=%async_computation.3 | async-start | bytes 786432 | tf_op jit(solution)/shard_map/all_to_all | solution.py:75
  36.9 1.4 %copy-start.1 = (bf16[1,256,3072]{2,1,0:T(8,128)(2,1)S(1)}, bf16[1,256,3072]{2,1,0:T(8,128)(2,1)}, u32[]{:S(2)}) copy-start(bf16[1,256,3072]{2,1,0:T(8,128)(2,1)} %param.10) | copy-start | bytes 4718596
  45.3 11.7 %all-to-all-start.1 = ((bf16[8,8,3072]{2,1,0:T(8,128)(2,1)}), bf16[8,8,3072]{2,1,0:T(8,128)(2,1)S(1)}, u32[]{:S(2)}, u32[]{:S(2)}) async-start(bf16[8,8,3072]{2,1,0:T(8,128)(2,1)} %fusion), calls=%async_computation.1 | async-start | bytes 786432 | tf_op jit(solution)/shard_map/all_to_all | solution.py:89
  48.8 2.2 %copy-start.2 = (bf16[1,256,3072]{2,1,0:T(8,128)(2,1)S(1)}, bf16[1,256,3072]{2,1,0:T(8,128)(2,1)}, u32[]{:S(2)}) copy-start(bf16[1,256,3072]{2,1,0:T(8,128)(2,1)} %param.10) | copy-start | bytes 4718596
  57.1 0.8 copy-start.3
  57.8 11.7 %all-to-all-start.3 = ((bf16[8,8,3072]{2,1,0:T(8,128)(2,1)}), bf16[8,8,3072]{2,1,0:T(8,128)(2,1)S(1)}, u32[]{:S(2)}, u32[]{:S(2)}) async-start(bf16[8,8,3072]{2,1,0:T(8,128)(2,1)} %fusion.1), calls=%async_computation.4 | async-start | bytes 786432 | tf_op jit(solution)/shard_map/all_to_all | solution.py:89
  61.3 23.8 %reduce-scatter.3.cloned.1.call-start = ((), (), s32[]{:S(2)}) async-start(), calls=%async_computation.6 | async-start | bytes 122880 | tf_op jit(solution)/shard_map/reduce_scatter | solution.py:96
  63.5 41.3 %reduce-scatter.5.cloned.1.call-start = ((), (), s32[]{:S(2)}) async-start(), calls=%async_computation.7 | async-start | bytes 122880 | tf_op jit(solution)/shard_map/reduce_scatter | solution.py:96
Sparse Core Ops, SparseCore 0:
  64.4 20.6 reduce-scatter.2
  87.4 17.3 reduce-scatter.4
where the time goes:
time: 114 us; the launch traced here: 113 us
  waiting for transfers between devices  49.5 us (43%)
  starting transfers between devices  16.4 us (14%)
  matrix products  16.1 us (14%)
  between operations  13.5 us (12%)
  other arithmetic  13.1 us (11%)
  local copies, waits for them, and re-layouts  4.56 us (4%)
    reduce_scatter x2, waiting for transfers between devices, body(): lax.psum_scatter(combined.astype(jnp.bfloat16), 'inner', scatter_dimensio...  33.3 us
    all_to_all x2, waiting for transfers between devices, body(): lax.all_to_all(partial_value, 'section', split_axis=0, concat_axis=0, til...  10.3 us
    all_to_all x2, starting transfers between devices, body(): lax.all_to_all(outgoing, 'section', split_axis=0, concat_axis=0, tiled=True)  9.37 us
    all_to_all x2, starting transfers between devices, body(): lax.all_to_all(partial_value, 'section', split_axis=0, concat_axis=0, til...  6.9 us
    all_to_all x2, waiting for transfers between devices, body(): lax.all_to_all(outgoing, 'section', split_axis=0, concat_axis=0, tiled=True)  5.91 us
    dot_general x2, matrix products, prepare(): jnp.einsum('rec,rd->ecd', placed.astype(jnp.bfloat16), normed, preferred_...  3.93 us
    dot_general x2, matrix products, prepare(): logits = jnp.dot(normed, router_w, preferred_element_type=jnp.float32)  3.44 us
    dot_general x2, matrix products, body(): lax.dot_general(flat_rows, stacked_in, (((1,), (1,)), ((), ())), preferre...  3.26 us
  transfers between devices with their start and end apart: 6, of which 5 were waited for; matrix products, arithmetic and copies ran while one was open for 23% of the time, Pallas kernels for 0%

commit v1 on v0

v1 whole, which is shorter than its diff:
```python
import jax
import jax.numpy as jnp
from jax import lax
from jax.sharding import PartitionSpec as P

epsilon = 1e-05


def trade(value, axis, distance):
    count = lax.axis_size(axis)
    return lax.ppermute(value, axis, [(place, place ^ distance) for place in range(count)])


def mixing_of(normed, first, second, router, expert):
    logits = jnp.dot(normed, router, preferred_element_type=jnp.float32)
    ids = jnp.arange(router.shape[1], dtype=jnp.int32).astype(jnp.float32)
    first_hot = (first == ids[None, :]).astype(jnp.float32)
    second_hot = (second == ids[None, :]).astype(jnp.float32)
    lead = jnp.sum(logits * first_hot, axis=1, keepdims=True)
    trail = jnp.sum(logits * second_hot, axis=1, keepdims=True)
    weight_a = 1.0 / (1.0 + jnp.exp(trail - lead))
    weight_b = 1.0 / (1.0 + jnp.exp(lead - trail))
    mine = expert.astype(jnp.float32)
    return jnp.where(first == mine, weight_a, 0.0) + jnp.where(second == mine, weight_b, 0.0)


def body(tokens, norm_gain, router, expert_in, expert_out, choices):
    sections = lax.axis_size("section")
    inner_count = lax.axis_size("inner")
    member = lax.axis_index("inner")
    section = lax.axis_index("section")
    chips = sections // 2
    expert = section // (sections // router.shape[1])
    micro, row_count, width = tokens.shape
    rows = micro * row_count
    part = width // inner_count
    hidden = expert_in.shape[2]
    stacked_in = expert_in[0].reshape(2 * hidden, width)
    down = expert_out[0]

    own = tokens.reshape(rows, width)
    named = choices.reshape(rows, 2).astype(jnp.bfloat16)
    message = jnp.concatenate([own, named, jnp.zeros((rows, 126), jnp.bfloat16)], axis=1)
    here = jnp.stack([message] + [trade(message, "section", 2 * k) for k in range(1, chips)])
    there = trade(here, "section", 1)
    every = jnp.concatenate([here, there], axis=0).reshape(sections * rows, width + 128)

    values = every[:, :width].astype(jnp.float32)
    inv_rms = lax.rsqrt(jnp.mean(values * values, axis=-1, keepdims=True) + epsilon)
    normed = (values * inv_rms * norm_gain).astype(jnp.bfloat16)
    first = every[:, width : width + 1].astype(jnp.float32)
    second = every[:, width + 1 : width + 2].astype(jnp.float32)
    weight = mixing_of(normed, first, second, router, expert)
    gate_up = lax.dot_general(
        normed, stacked_in, (((1,), (1,)), ((), ())), preferred_element_type=jnp.float32
    )
    active = (jax.nn.silu(gate_up[:, :hidden]) * gate_up[:, hidden:]).astype(jnp.bfloat16)
    partial = jnp.dot(active, down, preferred_element_type=jnp.float32)
    weighted = (partial * weight).astype(jnp.bfloat16).reshape(2, chips, rows, width)
    back = trade(weighted[1], "section", 1)
    paired = (weighted[0].astype(jnp.float32) + back.astype(jnp.float32)).astype(jnp.bfloat16)
    total = paired[0].astype(jnp.float32)
    for k in range(1, chips):
        total = total + trade(paired[k], "section", 2 * k).astype(jnp.float32)
    mine = lax.dynamic_slice_in_dim(total, member * part, part, 1)
    rounded = total.astype(jnp.bfloat16)
    for k in range(1, inner_count):
        away = lax.dynamic_slice_in_dim(rounded, (member ^ k) * part, part, 1)
        mine = mine + trade(away, "inner", k).astype(jnp.float32)
    residual = lax.dynamic_slice_in_dim(own, member * part, part, 1).astype(jnp.float32)
    return (residual + mine).astype(jnp.bfloat16).reshape(micro, row_count, part)


def solution(mesh):
    return jax.shard_map(
        body,
        mesh=mesh,
        in_specs=(
            P(None, "section", None),
            P(),
            P(),
            P("section", None, "inner", None),
            P("section", "inner", None),
            P(None, "section", None),
        ),
        out_specs=P(None, "section", "inner"),
        check_vma=False,
    )
```

time: 114 us -> 55 us (0.48)
  waiting for transfers between devices: 49.5 us -> 24.8 us
  between operations: 13.5 us -> 0.19 us
  matrix products: 16.1 us -> 3.76 us
  other arithmetic: 13.1 us -> 6.73 us
  starting transfers between devices: 16.4 us -> 12.7 us
  local copies, waits for them, and re-layouts: 4.56 us -> 6.5 us
    reduce_scatter x2 -> x0, waiting for transfers between devices: 33.3 us -> none  [body(): lax.psum_scatter(combined.astype(jnp.bfloat16), 'inner', scatter_dimensio...]
    ppermute x0 -> x11, waiting for transfers between devices: none -> 24.8 us  [trade(): lax.ppermute(value, axis, [(place, place ^ distance) for place in range(c...]
    all_to_all x4 -> x0, starting transfers between devices: 16.3 us -> none  [the longest x2 9.37 us: body(): lax.all_to_all(outgoing, 'section', split_axis=0, concat_axis=0, tiled=True)]
    all_to_all x4 -> x0, waiting for transfers between devices: 16.2 us -> none  [the longest x2 10.3 us: body(): lax.all_to_all(partial_value, 'section', split_axis=0, concat_axis=0, til...]
    ppermute x0 -> x11, starting transfers between devices: none -> 12.7 us  [trade(): lax.ppermute(value, axis, [(place, place ^ distance) for place in range(c...]
    dot_general x10 -> x3, matrix products: 16.1 us -> 3.76 us  [the longest x1 2.54 us: body(): lax.dot_general(normed, stacked_in, (((1,), (1,)), ((), ())), preferred_e...]
    unnamed x16 -> x18, local copies, waits for them, and re-layouts: 1.1 us -> 3.51 us
    div x2 -> x1, other arithmetic: 1.93 us -> 0.01 us  [mixing_of(): weight_a = 1.0 / (1.0 + jnp.exp(trail - lead))]
  transfers between devices with their start and end apart: 6 -> 11, of which waited for: 5 -> 10; matrix products, arithmetic and copies ran while one was open for 23% -> 5% of each run, Pallas kernels for 0% -> 0%
where the time goes in v1:
time: 55 us; the launch traced here: 54.7 us
  waiting for transfers between devices  24.8 us (45%)
  starting transfers between devices  12.7 us (23%)
  other arithmetic  6.73 us (12%)
  local copies, waits for them, and re-layouts  6.5 us (12%)
  matrix products  3.76 us (7%)
    ppermute x11, waiting for transfers between devices, trade(): lax.ppermute(value, axis, [(place, place ^ distance) for place in range(c...  24.8 us
    ppermute x11, starting transfers between devices, trade(): lax.ppermute(value, axis, [(place, place ^ distance) for place in range(c...  12.7 us
    unnamed x18, local copies, waits for them, and re-layouts  3.51 us
    dot_general x1, matrix products, body(): lax.dot_general(normed, stacked_in, (((1,), (1,)), ((), ())), preferred_e...  2.54 us
    convert_element_type x1, other arithmetic, body(): (residual + mine).astype(jnp.bfloat16).reshape(micro, row_count, part)  1.52 us
    convert_element_type x1, other arithmetic, body(): rounded = total.astype(jnp.bfloat16)  1.32 us
    another operation x1, other arithmetic, body(): jnp.stack([message] + [trade(message, 'section', 2 * k) for k in range(1,...  1.15 us
    add x1, other arithmetic, mixing_of(): jnp.where(first == mine, weight_a, 0.0)  1.1 us
  transfers between devices with their start and end apart: 11, of which 10 were waited for; matrix products, arithmetic and copies ran while one was open for 5% of the time, Pallas kernels for 0%

profile of v1, /device:TPU:0, one launch (start us, length us, event | category | flops | bytes accessed | tf_op | source)
XLA Modules:
  0.0 54.7 jit_solution(14515984863154313560)
XLA Ops:
  0.0 0.8 %convert_element_type.84 = bf16[2,16,2]{1,2,0:T(2,128)(2,1)S(1)} convert(s32[2,16,2]{1,2,0:T(2,128)} %param.11) | non-fusion elementwise | flops 64 | bytes 384 | tf_op jit(solution)/shard_map/convert_element_type | solution.py:42
  0.9 1.0 %concatenate.7 = bf16[32,3200]{1,0:T(8,128)(2,1)S(1)} concatenate(bf16[32,3072]{1,0:T(8,128)(2,1)} %bitcast.45, bf16[32,2]{1,0:T(8,128)(2,1)S(1)} %bitcast.47, bf16[32,126]{1,0:T(8,128)(2,1)S(1)} %broadcast_in_dim.6), dimensions={1} | concatenate | bytes 409600 | tf_op jit(solution)/shard_map/concatenate | solution.py:43
  2.0 3.0 %collective-permute-start = (bf16[32,3200]{1,0:T(8,128)(2,1)S(1)}, bf16[32,3200]{1,0:T(8,128)(2,1)S(1)}, u32[]{:S(2)}, u32[]{:S(2)}) collective-permute-start(bf16[32,3200]{1,0:T(8,128)(2,1)S(1)} %concatenate.7), channel_id=1, source_target_pairs={{0,8},{4,12},{8,0},{12,4},{16,24},{20,28},{24,16},{28,20},{1,9},{5... | collective-permute-start | bytes 614408 | tf_op jit(solution)/shard_map/ppermute | solution.py:11
  5.0 1.5 %collective-permute-start.1 = (bf16[32,3200]{1,0:T(8,128)(2,1)S(1)}, bf16[32,3200]{1,0:T(8,128)(2,1)}, u32[]{:S(2)}, u32[]{:S(2)}) collective-permute-start(bf16[32,3200]{1,0:T(8,128)(2,1)S(1)} %concatenate.7), channel_id=1, source_target_pairs={{0,16},{4,20},{8,24},{12,28},{16,0},{20,4},{24,8},{28,12},{1,17},{... | collective-permute-start | bytes 614408 | tf_op jit(solution)/shard_map/ppermute | solution.py:11
  6.5 0.7 %constant_dynamic-update-slice_fusion.4 = bf16[8,32,3200]{2,1,0:T(8,128)(2,1)} fusion(bf16[32,3200]{1,0:T(8,128)(2,1)S(1)} %concatenate.7), kind=kLoop, calls=%fused_computation.33 | loop fusion | bytes 409600
  7.2 3.7 %collective-permute-done = bf16[32,3200]{1,0:T(8,128)(2,1)S(1)} collective-permute-done((bf16[32,3200]{1,0:T(8,128)(2,1)S(1)}, bf16[32,3200]{1,0:T(8,128)(2,1)S(1)}, u32[]{:S(2)}, u32[]{:S(2)}) %collective-permute-start) | collective-permute-done | bytes 204832 | tf_op jit(solution)/shard_map/ppermute | solution.py:11
  10.9 5.1 %collective-permute-done.1 = bf16[32,3200]{1,0:T(8,128)(2,1)} collective-permute-done((bf16[32,3200]{1,0:T(8,128)(2,1)S(1)}, bf16[32,3200]{1,0:T(8,128)(2,1)}, u32[]{:S(2)}, u32[]{:S(2)}) %collective-permute-start.1) | collective-permute-done | bytes 204832 | tf_op jit(solution)/shard_map/ppermute | solution.py:11
  16.0 1.2 %pad_maximum_fusion = bf16[4,32,3200]{2,1,0:T(8,128)(2,1)S(1)} fusion(bf16[1,32,3200]{2,1,0:T(8,128)(2,1)} %bitcast.5, bf16[1,32,3200]{2,1,0:T(8,128)(2,1)} %bitcast.4, bf16[1,32,3200]{2,1,0:T(8,128)(2,1)S(1)} %bitcast.43, bf16[1,32,3200]{2,1,0:T(8,128)(2,1)S(1)} %bitcast.42), kind=kLoop, calls=%fused_computation.10 | loop fusion | flops 1228800 | bytes 1638400 | tf_op jit(solution)/shard_map/stack | solution.py:44
  17.3 1.0 %constant_dynamic-update-slice_fusion.2 = bf16[8,32,3200]{2,1,0:T(8,128)(2,1)S(1)} fusion(bf16[8,32,3200]{2,1,0:T(8,128)(2,1)S(1)} %constant_dynamic-update-slice_fusion.3, bf16[32,3200]{1,0:T(8,128)(2,1)} %collective-permute-done.1), kind=kLoop, calls=%fused_computation.31 | loop fusion | bytes 409600
  18.2 1.0 %constant_dynamic-update-slice_fusion.1 = bf16[8,32,3200]{2,1,0:T(8,128)(2,1)S(1)} fusion(bf16[8,32,3200]{2,1,0:T(8,128)(2,1)S(1)} %constant_dynamic-update-slice_fusion.2, bf16[32,3200]{1,0:T(8,128)(2,1)} %collective-permute-done.2), kind=kLoop, calls=%fused_computation.30 | loop fusion | bytes 409600
  19.9 0.4 fusion.1
  20.3 0.6 %select_reduce_fusion.1 = (f32[256]{0:T(256)S(1)}, f32[256]{0:T(256)S(1)}) fusion(f32[256]{0:T(256)S(1)} %get-tuple-element.5, f32[8]{0:T(128)S(1)} %iota_convert_fusion, f32[256]{0:T(256)S(1)} %get-tuple-element.6, bf16[3072,8]{0,1:T(8,128)(2,1)S(1)} %copy-done.5, f32[3072]{0:T(1024)S(1)} %copy-done.6, f32[256]{0:T(256)S(1)} %add_rsqrt_fusion, ...), kind=kOutput, calls=%fused_computation.35 | convolution fusion | flops 15740416 | bytes 1639936 | tf_op jit(solution)/shard_map/dot_general | solution.py:15
  21.2 2.5 %fusion.10 = f32[256,512]{1,0:T(8,128)S(1)} fusion(bf16[512,3072]{1,0:T(8,128)(2,1)S(1)} %bitcast.35, f32[3072]{0:T(1024)S(1)} %copy-done.6, f32[256]{0:T(256)S(1)} %add_rsqrt_fusion, bf16[256,3200]{1,0:T(8,128)(2,1)} %bitcast.40), kind=kOutput, calls=%fused_computation.15 | convolution fusion | flops 808452096 | bytes 5256192 | tf_op jit(solution)/shard_map/dot_general | solution.py:54
  23.8 1.1 %add_reduce_fusion = f32[256]{0:T(256)S(1)} fusion(f32[256,1]{1,0:T(8,128)S(1)} %copy.15, f32[256,1]{1,0:T(8,128)S(1)} %copy.14, f32[]{:T(128)S(6)} %convert_element_type.90, bf16[256,3200]{1,0:T(8,128)(2,1)} %bitcast.41), kind=kLoop, calls=%fused_computation.26 | loop fusion | flops 1792 | bytes 4100 | tf_op jit(solution)/shard_map/add | solution.py:24
  24.9 0.6 %fusion = bf16[256,3072]{1,0:T(8,128)(2,1)S(1)} fusion(bf16[1,256,3072]{2,1,0:T(8,128)(2,1)S(1)} %copy-done.4, f32[256]{0:T(256)S(1)} %add_reduce_fusion, f32[256,512]{1,0:T(8,128)S(1)} %fusion.10), kind=kOutput, calls=%fused_computation.3 | convolution fusion | flops 404619264 | bytes 3671040 | tf_op jit(solution)/shard_map/dot_general | solution.py:58
  25.9 2.1 %collective-permute-done.4 = bf16[4,32,3072]{2,1,0:T(8,128)(2,1)S(1)} collective-permute-done((bf16[4,32,3072]{2,1,0:T(8,128)(2,1)S(1)}, bf16[4,32,3072]{2,1,0:T(8,128)(2,1)S(1)}, u32[]{:S(2)}, u32[]{:S(2)}) %collective-permute-start.4) | collective-permute-done | bytes 786464 | tf_op jit(solution)/shard_map/ppermute | solution.py:11
  28.2 0.9 %copy-done.1 = bf16[4,32,3072]{2,1,0:T(8,128)(2,1)} copy-done((bf16[4,32,3072]{2,1,0:T(8,128)(2,1)}, bf16[4,32,3072]{2,1,0:T(8,128)(2,1)S(1)}, u32[]{:S(2)}) %copy-start.1) | copy-done | bytes 786456
  29.1 0.7 %slice_bitcast_fusion.2 = (bf16[32,3072]{1,0:T(8,128)(2,1)}, bf16[32,3072]{1,0:T(8,128)(2,1)S(1)}, bf16[32,3072]{1,0:T(8,128)(2,1)S(1)}) fusion(bf16[4,32,3072]{2,1,0:T(8,128)(2,1)S(1)} %fusion.4), kind=kLoop, calls=%fused_computation.20 | loop fusion | bytes 1179648 | tf_op jit(solution)/shard_map/squeeze | solution.py:64
  29.8 1.2 %collective-permute-start.5 = (bf16[32,3072]{1,0:T(8,128)(2,1)}, bf16[32,3072]{1,0:T(8,128)(2,1)}, u32[]{:S(2)}, u32[]{:S(2)}) collective-permute-start(bf16[32,3072]{1,0:T(8,128)(2,1)} %get-tuple-element.13), channel_id=1, source_target_pairs={{0,8},{4,12},{8,0},{12,4},{16,24},{20,28},{24,16},{28,20},{1,9},{5... | collective-permute-start | bytes 589832 | tf_op jit(solution)/shard_map/ppermute | solution.py:11
  31.0 0.8 %collective-permute-start.6 = (bf16[32,3072]{1,0:T(8,128)(2,1)S(1)}, bf16[32,3072]{1,0:T(8,128)(2,1)}, u32[]{:S(2)}, u32[]{:S(2)}) collective-permute-start(bf16[32,3072]{1,0:T(8,128)(2,1)S(1)} %get-tuple-element.15), channel_id=1, source_target_pairs={{0,16},{4,20},{8,24},{12,28},{16,0},{20,4},{24,8},{28,12},{1,17},{... | collective-permute-start | bytes 589832 | tf_op jit(solution)/shard_map/ppermute | solution.py:11
  31.8 1.4 %collective-permute-start.7 = (bf16[32,3072]{1,0:T(8,128)(2,1)S(1)}, bf16[32,3072]{1,0:T(8,128)(2,1)}, u32[]{:S(2)}, u32[]{:S(2)}) collective-permute-start(bf16[32,3072]{1,0:T(8,128)(2,1)S(1)} %get-tuple-element.14), channel_id=1, source_target_pairs={{0,24},{4,28},{8,16},{12,20},{16,8},{20,12},{24,0},{28,4},{1,25},{... | collective-permute-start | bytes 589832 | tf_op jit(solution)/shard_map/ppermute | solution.py:11
  33.3 4.6 %collective-permute-done.5 = bf16[32,3072]{1,0:T(8,128)(2,1)} collective-permute-done((bf16[32,3072]{1,0:T(8,128)(2,1)}, bf16[32,3072]{1,0:T(8,128)(2,1)}, u32[]{:S(2)}, u32[]{:S(2)}) %collective-permute-start.5) | collective-permute-done | bytes 196640 | tf_op jit(solution)/shard_map/ppermute | solution.py:11
  37.8 0.5 collective-permute-done.6
  38.3 3.9 %collective-permute-done.7 = bf16[32,3072]{1,0:T(8,128)(2,1)} collective-permute-done((bf16[32,3072]{1,0:T(8,128)(2,1)S(1)}, bf16[32,3072]{1,0:T(8,128)(2,1)}, u32[]{:S(2)}, u32[]{:S(2)}) %collective-permute-start.7) | collective-permute-done | bytes 196640 | tf_op jit(solution)/shard_map/ppermute | solution.py:11
  42.3 1.3 %fusion.16 = (bf16[32,3072]{1,0:T(8,128)(2,1)S(1)}, f32[32,3072]{1,0:T(8,128)S(1)}) fusion(bf16[32,3072]{1,0:T(8,128)(2,1)} %collective-permute-done.7, bf16[32,3072]{1,0:T(8,128)(2,1)} %collective-permute-done.6, bf16[32,3072]{1,0:T(8,128)(2,1)} %collective-permute-done.5, bf16[4,32,3072]{2,1,0:T(8,128)(2,1)} %copy-done.1), kind=kLoop, calls=%fused_computation.44 | loop fusion | flops 786432 | bytes 1376256 | tf_op jit(solution)/shard_map/convert_element_type | solution.py:66
  43.6 0.7 %constant_dynamic-slice_fusion.1 = (bf16[32,768]{1,0:T(8,128)(2,1)}, bf16[32,768]{1,0:T(8,128)(2,1)}, bf16[32,768]{1,0:T(8,128)(2,1)}) fusion(bf16[32,3072]{1,0:T(8,128)(2,1)S(1)} %get-tuple-element.9, s32[]{:T(128)S(6)} %select_n.26, s32[]{:T(128)S(6)} %select_n.28, s32[]{:T(128)S(6)} %select_n.27), kind=kLoop, calls=%fused_computation.37 | loop fusion | bytes 294924 | tf_op jit(solution)/shard_map/dynamic_slice | solution.py:68
  44.2 3.6 %collective-permute-start.10 = (bf16[32,768]{1,0:T(8,128)(2,1)}, bf16[32,768]{1,0:T(8,128)(2,1)}, u32[]{:S(2)}, u32[]{:S(2)}) collective-permute-start(bf16[32,768]{1,0:T(8,128)(2,1)} %get-tuple-element.17), channel_id=1, source_target_pairs={{0,3},{1,2},{2,1},{3,0},{4,7},{5,6},{6,5},{7,4},{8,11},{9,10},{10,... | collective-permute-start | bytes 147464 | tf_op jit(solution)/shard_map/ppermute | solution.py:11
  47.9 0.8 %collective-permute-start.9 = (bf16[32,768]{1,0:T(8,128)(2,1)}, bf16[32,768]{1,0:T(8,128)(2,1)}, u32[]{:S(2)}, u32[]{:S(2)}) collective-permute-start(bf16[32,768]{1,0:T(8,128)(2,1)} %get-tuple-element.18), channel_id=1, source_target_pairs={{0,2},{1,3},{2,0},{3,1},{4,6},{5,7},{6,4},{7,5},{8,10},{9,11},{10,... | collective-permute-start | bytes 147464 | tf_op jit(solution)/shard_map/ppermute | solution.py:11
  48.6 1.9 %collective-permute-done.10 = bf16[32,768]{1,0:T(8,128)(2,1)} collective-permute-done((bf16[32,768]{1,0:T(8,128)(2,1)}, bf16[32,768]{1,0:T(8,128)(2,1)}, u32[]{:S(2)}, u32[]{:S(2)}) %collective-permute-start.10) | collective-permute-done | bytes 49184 | tf_op jit(solution)/shard_map/ppermute | solution.py:11
  50.6 1.7 %collective-permute-done.8 = bf16[32,768]{1,0:T(8,128)(2,1)} collective-permute-done((bf16[32,768]{1,0:T(8,128)(2,1)}, bf16[32,768]{1,0:T(8,128)(2,1)}, u32[]{:S(2)}, u32[]{:S(2)}) %collective-permute-start.8) | collective-permute-done | bytes 49184 | tf_op jit(solution)/shard_map/ppermute | solution.py:11
  52.3 0.9 %collective-permute-done.9 = bf16[32,768]{1,0:T(8,128)(2,1)} collective-permute-done((bf16[32,768]{1,0:T(8,128)(2,1)}, bf16[32,768]{1,0:T(8,128)(2,1)}, u32[]{:S(2)}, u32[]{:S(2)}) %collective-permute-start.9) | collective-permute-done | bytes 49184 | tf_op jit(solution)/shard_map/ppermute | solution.py:11
  53.2 1.5 %add_convert_fusion = bf16[32,768]{1,0:T(8,128)(2,1)} fusion(bf16[32,768]{1,0:T(8,128)(2,1)} %collective-permute-done.10, bf16[32,768]{1,0:T(8,128)(2,1)} %collective-permute-done.9, bf16[32,768]{1,0:T(8,128)(2,1)} %collective-permute-done.8, f32[32,3072]{1,0:T(8,128)S(1)} %get-tuple-element.10, s32[]{:T(128)S(6)} %select_n.23, bf16[32,3072]{1,0:T(8,128)(2,1)} %bitcast.46), kind=kLoop, calls=%fused_computation.28 | loop fusion | flops 221184 | bytes 344068 | tf_op jit(solution)/shard_map/convert_element_type | solution.py:71
  (31 shorter events, 1.8 us)
Async XLA Ops:
  0.0 21.2 %copy-start = (bf16[1,2,256,3072]{3,2,1,0:T(8,128)(2,1)S(1)}, bf16[1,2,256,3072]{3,2,1,0:T(8,128)(2,1)}, u32[]{:S(2)}) copy-start(bf16[1,2,256,3072]{3,2,1,0:T(8,128)(2,1)} %param.9) | copy-start | bytes 9437188
  2.0 8.9 %collective-permute-start = (bf16[32,3200]{1,0:T(8,128)(2,1)S(1)}, bf16[32,3200]{1,0:T(8,128)(2,1)S(1)}, u32[]{:S(2)}, u32[]{:S(2)}) collective-permute-start(bf16[32,3200]{1,0:T(8,128)(2,1)S(1)} %concatenate.7), channel_id=1, source_target_pairs={{0,8},{4,12},{8,0},{12,4},{16,24},{20,28},{24,16},{28,20},{1,9},{5... | collective-permute-start | bytes 614408 | tf_op jit(solution)/shard_map/ppermute | solution.py:11
  5.0 11.0 %collective-permute-start.1 = (bf16[32,3200]{1,0:T(8,128)(2,1)S(1)}, bf16[32,3200]{1,0:T(8,128)(2,1)}, u32[]{:S(2)}, u32[]{:S(2)}) collective-permute-start(bf16[32,3200]{1,0:T(8,128)(2,1)S(1)} %concatenate.7), channel_id=1, source_target_pairs={{0,16},{4,20},{8,24},{12,28},{16,0},{20,4},{24,8},{28,12},{1,17},{... | collective-permute-start | bytes 614408 | tf_op jit(solution)/shard_map/ppermute | solution.py:11
  6.5 9.5 %collective-permute-start.2 = (bf16[32,3200]{1,0:T(8,128)(2,1)S(1)}, bf16[32,3200]{1,0:T(8,128)(2,1)}, u32[]{:S(2)}, u32[]{:S(2)}) collective-permute-start(bf16[32,3200]{1,0:T(8,128)(2,1)S(1)} %concatenate.7), channel_id=1, source_target_pairs={{0,24},{4,28},{8,16},{12,20},{16,8},{20,12},{24,0},{28,4},{1,25},{... | collective-permute-start | bytes 614408 | tf_op jit(solution)/shard_map/ppermute | solution.py:11
  7.2 10.0 %copy-start.2 = (bf16[8,32,3200]{2,1,0:T(8,128)(2,1)S(1)}, bf16[8,32,3200]{2,1,0:T(8,128)(2,1)}, u32[]{:S(2)}) copy-start(bf16[8,32,3200]{2,1,0:T(8,128)(2,1)} %constant_dynamic-update-slice_fusion.4) | copy-start | bytes 4915204
  17.2 2.4 %collective-permute-start.3 = (bf16[4,32,3200]{2,1,0:T(8,128)(2,1)S(1)}, bf16[4,32,3200]{2,1,0:T(8,128)(2,1)S(1)}, u32[]{:S(2)}, u32[]{:S(2)}) collective-permute-start(bf16[4,32,3200]{2,1,0:T(8,128)(2,1)S(1)} %pad_maximum_fusion), channel_id=1, source_target_pairs={{0,4},{4,0},{8,12},{12,8},{16,20},{20,16},{24,28},{28,24},{1,5},{5... | collective-permute-start | bytes 2457608 | tf_op jit(solution)/shard_map/ppermute | solution.py:11
  19.2 1.1 %copy-start.5 = (bf16[3072,8]{0,1:T(8,128)(2,1)S(1)}, bf16[3072,8]{0,1:T(8,128)(2,1)}, u32[]{:S(2)}) copy-start(bf16[3072,8]{0,1:T(8,128)(2,1)} %param.8) | copy-start | bytes 147460
  19.2 1.1 %copy-start.6 = (f32[3072]{0:T(1024)S(1)}, f32[3072]{0:T(1024)}, u32[]{:S(2)}) copy-start(f32[3072]{0:T(1024)} %param.7) | copy-start | bytes 36868
  19.7 1.2 %copy-start.3 = (bf16[8,32,3200]{2,1,0:T(8,128)(2,1)}, bf16[8,32,3200]{2,1,0:T(8,128)(2,1)S(1)}, u32[]{:S(2)}) copy-start(bf16[8,32,3200]{2,1,0:T(8,128)(2,1)S(1)} %constant_dynamic-update-slice_fusion) | copy-start | bytes 4915204
  21.2 3.7 %copy-start.4 = (bf16[1,256,3072]{2,1,0:T(8,128)(2,1)S(1)}, bf16[1,256,3072]{2,1,0:T(8,128)(2,1)}, u32[]{:S(2)}) copy-start(bf16[1,256,3072]{2,1,0:T(8,128)(2,1)} %param.10) | copy-start | bytes 4718596
  25.6 2.4 %collective-permute-start.4 = (bf16[4,32,3072]{2,1,0:T(8,128)(2,1)S(1)}, bf16[4,32,3072]{2,1,0:T(8,128)(2,1)S(1)}, u32[]{:S(2)}, u32[]{:S(2)}) collective-permute-start(bf16[4,32,3072]{2,1,0:T(8,128)(2,1)S(1)} %bitcast.44), channel_id=1, source_target_pairs={{0,4},{4,0},{8,12},{12,8},{16,20},{20,16},{24,28},{28,24},{1,5},{5... | collective-permute-start | bytes 2359304 | tf_op jit(solution)/shard_map/ppermute | solution.py:11
  28.2 0.9 %copy-start.1 = (bf16[4,32,3072]{2,1,0:T(8,128)(2,1)}, bf16[4,32,3072]{2,1,0:T(8,128)(2,1)S(1)}, u32[]{:S(2)}) copy-start(bf16[4,32,3072]{2,1,0:T(8,128)(2,1)S(1)} %fusion.4) | copy-start | bytes 2359300
  29.8 8.1 %collective-permute-start.5 = (bf16[32,3072]{1,0:T(8,128)(2,1)}, bf16[32,3072]{1,0:T(8,128)(2,1)}, u32[]{:S(2)}, u32[]{:S(2)}) collective-permute-start(bf16[32,3072]{1,0:T(8,128)(2,1)} %get-tuple-element.13), channel_id=1, source_target_pairs={{0,8},{4,12},{8,0},{12,4},{16,24},{20,28},{24,16},{28,20},{1,9},{5... | collective-permute-start | bytes 589832 | tf_op jit(solution)/shard_map/ppermute | solution.py:11
  31.0 7.3 %collective-permute-start.6 = (bf16[32,3072]{1,0:T(8,128)(2,1)S(1)}, bf16[32,3072]{1,0:T(8,128)(2,1)}, u32[]{:S(2)}, u32[]{:S(2)}) collective-permute-start(bf16[32,3072]{1,0:T(8,128)(2,1)S(1)} %get-tuple-element.15), channel_id=1, source_target_pairs={{0,16},{4,20},{8,24},{12,28},{16,0},{20,4},{24,8},{28,12},{1,17},{... | collective-permute-start | bytes 589832 | tf_op jit(solution)/shard_map/ppermute | solution.py:11
  31.8 10.4 %collective-permute-start.7 = (bf16[32,3072]{1,0:T(8,128)(2,1)S(1)}, bf16[32,3072]{1,0:T(8,128)(2,1)}, u32[]{:S(2)}, u32[]{:S(2)}) collective-permute-start(bf16[32,3072]{1,0:T(8,128)(2,1)S(1)} %get-tuple-element.14), channel_id=1, source_target_pairs={{0,24},{4,28},{8,16},{12,20},{16,8},{20,12},{24,0},{28,4},{1,25},{... | collective-permute-start | bytes 589832 | tf_op jit(solution)/shard_map/ppermute | solution.py:11
  44.2 6.3 %collective-permute-start.10 = (bf16[32,768]{1,0:T(8,128)(2,1)}, bf16[32,768]{1,0:T(8,128)(2,1)}, u32[]{:S(2)}, u32[]{:S(2)}) collective-permute-start(bf16[32,768]{1,0:T(8,128)(2,1)} %get-tuple-element.17), channel_id=1, source_target_pairs={{0,3},{1,2},{2,1},{3,0},{4,7},{5,6},{6,5},{7,4},{8,11},{9,10},{10,... | collective-permute-start | bytes 147464 | tf_op jit(solution)/shard_map/ppermute | solution.py:11
  47.8 4.4 %collective-permute-start.8 = (bf16[32,768]{1,0:T(8,128)(2,1)}, bf16[32,768]{1,0:T(8,128)(2,1)}, u32[]{:S(2)}, u32[]{:S(2)}) collective-permute-start(bf16[32,768]{1,0:T(8,128)(2,1)} %get-tuple-element.16), channel_id=1, source_target_pairs={{0,1},{1,0},{2,3},{3,2},{4,5},{5,4},{6,7},{7,6},{8,9},{9,8},{10,11... | collective-permute-start | bytes 147464 | tf_op jit(solution)/shard_map/ppermute | solution.py:11
  47.9 5.3 %collective-permute-start.9 = (bf16[32,768]{1,0:T(8,128)(2,1)}, bf16[32,768]{1,0:T(8,128)(2,1)}, u32[]{:S(2)}, u32[]{:S(2)}) collective-permute-start(bf16[32,768]{1,0:T(8,128)(2,1)} %get-tuple-element.18), channel_id=1, source_target_pairs={{0,2},{1,3},{2,0},{3,1},{4,6},{5,7},{6,4},{7,5},{8,10},{9,11},{10,... | collective-permute-start | bytes 147464 | tf_op jit(solution)/shard_map/ppermute | solution.py:11

commit v2 on v1

v2 whole, which is shorter than its diff:
```python
import functools

import jax
import jax.numpy as jnp
from jax import lax
from jax.experimental import pallas as pl
from jax.experimental.pallas import tpu as pltpu
from jax.sharding import PartitionSpec as P

epsilon = 1e-05
LANES = 128
NT = (((1,), (1,)), ((), ()))
VMEM = pl.BlockSpec(memory_space=pltpu.VMEM)
HBM = pl.BlockSpec(memory_space=pltpu.HBM)
SMEM = pl.BlockSpec(memory_space=pltpu.SMEM)
PARAMS = pltpu.CompilerParams(vmem_limit_bytes=20 * 1024 * 1024)


def trade(value, axis, distance):
    count = lax.axis_size(axis)
    return lax.ppermute(value, axis, [(place, place ^ distance) for place in range(count)])


def shaped(rows, width, dtype):
    return jax.ShapeDtypeStruct((rows, width), dtype)


def expert_at(section, distance, per_expert):
    return lax.div(section ^ (2 * distance), jnp.int32(per_expert))


def pack_kernel(chips, per_expert, experts, section_ref, tokens_ref, other_ref, named_ref, other_named_ref, gain_ref, *refs):
    out_refs, normed_ref, slots_ref, named_rows_ref = refs[:chips], refs[chips], refs[chips + 1], refs[chips + 2]
    micro, _, row_count = named_ref.shape
    rows = tokens_ref.shape[0]
    for place, ref in enumerate((tokens_ref, other_ref)):
        values = ref[...].astype(jnp.float32)
        inv_rms = lax.rsqrt(jnp.mean(values * values, axis=-1, keepdims=True) + epsilon)
        normed_ref[place * rows : (place + 1) * rows, :] = (
            values * inv_rms * gain_ref[...]
        ).astype(jnp.bfloat16)
    named = [
        jnp.concatenate(
            [ref[m, k : k + 1, :] for ref in (named_ref, other_named_ref) for m in range(micro)],
            axis=1,
        ).astype(jnp.float32)
        for k in range(2)
    ]
    every = 2 * rows
    capacity = row_count // 2
    ids = lax.broadcasted_iota(jnp.int32, (experts, every), 0).astype(jnp.float32)
    hit = (named[0] == ids) | (named[1] == ids)
    above = lax.broadcasted_iota(jnp.int32, (every, every), 0)
    column = lax.broadcasted_iota(jnp.int32, (every, every), 1)
    earlier = (above < column) & (above // row_count == column // row_count)
    rank = jnp.dot(
        hit.astype(jnp.bfloat16), earlier.astype(jnp.bfloat16), preferred_element_type=jnp.float32
    )
    group = lax.broadcasted_iota(jnp.int32, (experts, every), 1) // row_count
    slots = jnp.where(hit, (group * capacity).astype(jnp.float32) + rank, -1.0)
    slots_ref[...] = slots
    named_rows_ref[0:1, :] = named[0]
    named_rows_ref[1:2, :] = named[1]
    section = section_ref[0]
    slot_ids = lax.broadcasted_iota(jnp.int32, (rows, every), 0).astype(jnp.float32)
    picks = []
    for k in range(chips):
        expert = expert_at(section, k, per_expert).astype(jnp.float32)
        slot = jnp.sum(jnp.where(ids == expert, slots, 0.0), axis=0, keepdims=True)
        picks.append(jnp.where(slot == slot_ids, 1.0, 0.0))
    pick = jnp.concatenate(picks, axis=0).astype(jnp.bfloat16)
    packed = jnp.dot(pick, normed_ref[...], preferred_element_type=jnp.float32)
    for k, out_ref in enumerate(out_refs):
        out_ref[...] = packed[k * rows : (k + 1) * rows, :].astype(jnp.bfloat16)


def pack(section, tokens, other, named, other_named, gain, chips, per_expert, experts):
    rows, width = tokens.shape
    return pl.pallas_call(
        functools.partial(pack_kernel, chips, per_expert, experts),
        out_shape=[shaped(rows, width, jnp.bfloat16)] * chips
        + [
            shaped(2 * rows, width, jnp.bfloat16),
            shaped(experts, 2 * rows, jnp.float32),
            shaped(2, 2 * rows, jnp.float32),
        ],
        in_specs=[SMEM] + [VMEM] * 5,
        out_specs=[VMEM] * (chips + 3),
        compiler_params=PARAMS,
        name="pack",
    )(section, tokens, other, named, other_named, gain)


def mix_kernel(sets, per_expert, section_ref, normed_ref, slots_ref, named_ref, router_ref, *outs):
    experts, every = slots_ref.shape
    rows = every // 2
    logits = lax.dot_general(
        normed_ref[...], router_ref[...], NT, preferred_element_type=jnp.float32
    )
    diagonal = lax.broadcasted_iota(jnp.int32, (every, every), 0) == (
        lax.broadcasted_iota(jnp.int32, (every, every), 1)
    )

    def upright(row):
        return jnp.sum(jnp.where(diagonal, row, 0.0), axis=1, keepdims=True)

    first, second = upright(named_ref[0:1, :]), upright(named_ref[1:2, :])
    ids = lax.broadcasted_iota(jnp.int32, logits.shape, 1).astype(jnp.float32)
    lead = jnp.sum(jnp.where(first == ids, logits, 0.0), axis=1, keepdims=True)
    trail = jnp.sum(jnp.where(second == ids, logits, 0.0), axis=1, keepdims=True)
    weight_a = 1.0 / (1.0 + jnp.exp(trail - lead))
    weight_b = 1.0 / (1.0 + jnp.exp(lead - trail))
    section = section_ref[0]
    tall = lax.broadcasted_iota(jnp.int32, (experts, every), 0).astype(jnp.float32)
    for place, ks in enumerate(sets):
        shape = (every, len(ks) * rows)
        lanes = lax.broadcasted_iota(jnp.int32, shape, 1).astype(jnp.float32)
        spread = jnp.zeros(shape, jnp.float32)
        for at, k in enumerate(ks):
            expert = expert_at(section, k, per_expert).astype(jnp.float32)
            slot = jnp.sum(jnp.where(tall == expert, slots_ref[...], 0.0), axis=0, keepdims=True)
            weight = jnp.where(first == expert, weight_a, 0.0) + jnp.where(
                second == expert, weight_b, 0.0
            )
            spread = spread + jnp.where(upright(slot) + at * rows == lanes, weight, 0.0)
        high = spread.astype(jnp.bfloat16)
        outs[2 * place][...] = high
        outs[2 * place + 1][...] = (spread - high.astype(jnp.float32)).astype(jnp.bfloat16)


def mix(section, normed, slots, named, router, sets, per_expert):
    every = normed.shape[0]
    shapes = [shaped(every, len(ks) * every // 2, jnp.bfloat16) for ks in sets for _ in range(2)]
    return pl.pallas_call(
        functools.partial(mix_kernel, sets, per_expert),
        out_shape=shapes,
        in_specs=[SMEM] + [VMEM] * 4,
        out_specs=[VMEM] * len(shapes),
        compiler_params=PARAMS,
        name="mix",
    )(section, normed, slots, named, router)


def fetch_kernel(count, *refs):
    sources, targets, sems = refs[:count], refs[-1 - count : -1], refs[-1]
    copies = [
        pltpu.make_async_copy(source, target, sems.at[k])
        for k, (source, target) in enumerate(zip(sources, targets))
    ]
    for copy in copies:
        copy.start()
    for copy in copies:
        copy.wait()


def fetch(arrays, after=()):
    count = len(arrays)
    return pl.pallas_call(
        functools.partial(fetch_kernel, count),
        out_shape=[jax.ShapeDtypeStruct(a.shape, a.dtype) for a in arrays],
        in_specs=[HBM] * count + [VMEM] * len(after),
        out_specs=[VMEM] * count,
        scratch_shapes=[pltpu.SemaphoreType.DMA((count,))],
        compiler_params=PARAMS,
        name="fetch",
    )(*[pltpu.with_memory_space_constraint(a, pltpu.HBM) for a in arrays], *after)


def expert_kernel(count, in_ref, down_ref, *refs):
    blocks, out_refs, every_ref = refs[:count], refs[-1 - count : -1], refs[-1]
    rows = blocks[0].shape[0]
    for place, block in enumerate(blocks):
        every_ref[place * rows : (place + 1) * rows, :] = block[...]
    gate_up = lax.dot_general(
        every_ref[...], in_ref[...], NT, preferred_element_type=jnp.float32
    )
    hidden = gate_up.shape[1] // 2
    gate = gate_up[:, :hidden]
    active = (gate / (1.0 + jnp.exp(-gate)) * gate_up[:, hidden:]).astype(jnp.bfloat16)
    partial = jnp.dot(active, down_ref[...], preferred_element_type=jnp.float32)
    for place, out_ref in enumerate(out_refs):
        out_ref[...] = partial[place * rows : (place + 1) * rows, :].astype(jnp.bfloat16)


def run_expert(blocks, stacked_in, down, after=()):
    count = len(blocks)
    rows, width = blocks[0].shape
    return pl.pallas_call(
        functools.partial(expert_kernel, count),
        out_shape=[shaped(rows, width, jnp.bfloat16)] * count,
        in_specs=[VMEM] * (2 + count) + [pl.BlockSpec(memory_space=pl.ANY)] * len(after),
        out_specs=[VMEM] * count,
        scratch_shapes=[pltpu.VMEM((count * rows, width), jnp.bfloat16)],
        compiler_params=PARAMS,
        name="expert",
    )(stacked_in, down, *blocks, *after)


def gathered(blocks, every_ref):
    rows = blocks[0].shape[0]
    for place, block in enumerate(blocks):
        every_ref[place * rows : (place + 1) * rows, :] = block[...]
    return every_ref[...]


def begin_kernel(count, high_ref, low_ref, *refs):
    blocks, out_ref, every_ref = refs[:count], refs[count], refs[-1]
    every = gathered(blocks, every_ref)
    total = jnp.dot(low_ref[...], every, preferred_element_type=jnp.float32)
    out_ref[...] = total + jnp.dot(high_ref[...], every, preferred_element_type=jnp.float32)


def begin(high, low, blocks):
    count = len(blocks)
    rows, width = blocks[0].shape
    return pl.pallas_call(
        functools.partial(begin_kernel, count),
        out_shape=shaped(2 * rows, width, jnp.float32),
        in_specs=[VMEM] * (2 + count),
        out_specs=VMEM,
        scratch_shapes=[pltpu.VMEM((count * rows, width), jnp.bfloat16)],
        compiler_params=PARAMS,
        name="begin",
    )(high, low, *blocks)


def combine_kernel(count, high_ref, low_ref, begun_ref, *refs):
    blocks, keep_ref, send_ref, every_ref = refs[:count], refs[count], refs[count + 1], refs[-1]
    rows = blocks[0].shape[0]
    every = gathered(blocks, every_ref)
    total = begun_ref[...] + jnp.dot(low_ref[...], every, preferred_element_type=jnp.float32)
    total = total + jnp.dot(high_ref[...], every, preferred_element_type=jnp.float32)
    keep_ref[...] = total[:rows]
    send_ref[...] = total[rows:].astype(jnp.bfloat16)


def combine(high, low, begun, blocks):
    count = len(blocks)
    rows, width = blocks[0].shape
    return pl.pallas_call(
        functools.partial(combine_kernel, count),
        out_shape=[shaped(rows, width, jnp.float32), shaped(rows, width, jnp.bfloat16)],
        in_specs=[VMEM] * (3 + count),
        out_specs=[VMEM] * 2,
        scratch_shapes=[pltpu.VMEM((count * rows, width), jnp.bfloat16)],
        compiler_params=PARAMS,
        name="combine",
    )(high, low, begun, *blocks)


def split_kernel(member_ref, tokens_ref, keep_ref, back_ref, *outs):
    part = outs[0].shape[1]
    for k, out_ref in enumerate(outs):
        columns = pl.ds(pl.multiple_of((member_ref[0] ^ k) * part, LANES), part)
        total = keep_ref[:, columns] + back_ref[:, columns].astype(jnp.float32)
        if k == 0:
            total = total + tokens_ref[:, columns].astype(jnp.float32)
        out_ref[...] = total.astype(out_ref.dtype)


def split_up(keep, back, tokens, member, inner_count):
    rows, width = keep.shape
    part = width // inner_count
    if part % LANES:
        total = keep + back.astype(jnp.float32)
        rounded = total.astype(jnp.bfloat16)
        total = total + tokens.astype(jnp.float32)
        outs = [lax.dynamic_slice_in_dim(total, member * part, part, 1)]
        for k in range(1, inner_count):
            outs.append(lax.dynamic_slice_in_dim(rounded, (member ^ k) * part, part, 1))
        return outs
    kinds = [jnp.float32] + [jnp.bfloat16] * (inner_count - 1)
    return pl.pallas_call(
        split_kernel,
        out_shape=[shaped(rows, part, kind) for kind in kinds],
        in_specs=[SMEM] + [VMEM] * 3,
        out_specs=[VMEM] * inner_count,
        compiler_params=PARAMS,
        name="split",
    )(member.reshape(1), tokens, keep, back)


def final_kernel(*refs):
    out_ref = refs[-1]
    micro, row_count, _ = out_ref.shape
    total = refs[0][...]
    for ref in refs[1:-1]:
        total = total + ref[...].astype(jnp.float32)
    for m in range(micro):
        out_ref[m] = total[m * row_count : (m + 1) * row_count].astype(out_ref.dtype)


def finish(pieces, micro, row_count):
    part = pieces[0].shape[1]
    return pl.pallas_call(
        final_kernel,
        out_shape=jax.ShapeDtypeStruct((micro, row_count, part), jnp.bfloat16),
        in_specs=[VMEM] * len(pieces),
        out_specs=VMEM,
        compiler_params=PARAMS,
        name="finish",
    )(*pieces)


def body(tokens, norm_gain, router, expert_in, expert_out, choices):
    sections = lax.axis_size("section")
    inner_count = lax.axis_size("inner")
    member = lax.axis_index("inner").astype(jnp.int32)
    section = lax.axis_index("section").astype(jnp.int32).reshape(1)
    chips = sections // 2
    experts = router.shape[1]
    per_expert = sections // experts
    micro, row_count, width = tokens.shape
    rows = micro * row_count
    hidden = expert_in.shape[2]
    own = tokens.reshape(rows, width)
    named = choices.transpose(0, 2, 1)
    gain = norm_gain.reshape(1, width)

    other = trade(own, "section", 1)
    other_named = trade(named, "section", 1)
    own, named, gain = fetch((own, named, gain))
    *messages, normed, slots, names = pack(
        section, own, other, named, other_named, gain, chips, per_expert, experts
    )
    order = list(range(1, chips))
    arrived = {k: trade(messages[k], "section", 2 * k) for k in reversed(order)}
    router_rows, stacked_in, down = fetch(
        (router.T, expert_in[0].reshape(2 * hidden, width), expert_out[0]), (slots,)
    )
    far, near = order[-1], order[:-1]
    sets = ((0, far), tuple(near))
    high_a, low_a, high_b, low_b = mix(
        section, normed, slots, names, router_rows, sets, per_expert
    )
    here, away = run_expert([messages[0], arrived[far]], stacked_in, down)
    early = [here, trade(away, "section", 2 * far)]
    late = run_expert([arrived[k] for k in near], stacked_in, down, (here,))
    late = [trade(value, "section", 2 * k) for k, value in zip(near, late)]
    begun = begin(high_a, low_a, early)
    keep, send = combine(high_b, low_b, begun, late)
    back = trade(send, "section", 1)
    split = split_up(keep, back, own, member, inner_count)
    pieces = {k: trade(split[k], "inner", k) for k in reversed(range(1, inner_count))}
    pieces[0] = split[0]
    return finish([pieces[k] for k in [0] + list(reversed(range(1, inner_count)))], micro, row_count)


def solution(mesh):
    return jax.shard_map(
        body,
        mesh=mesh,
        in_specs=(
            P(None, "section", None),
            P(),
            P(),
            P("section", None, "inner", None),
            P("section", "inner", None),
            P(None, "section", None),
        ),
        out_specs=P(None, "section", "inner"),
        check_vma=False,
    )
```

time: 55 us -> 36.8 us (0.67)
  waiting for transfers between devices: 24.8 us -> 12.9 us
  Pallas kernels: 0 us -> 8.52 us
  other arithmetic: 6.73 us -> 0 us
  local copies, waits for them, and re-layouts: 6.5 us -> 0 us
  matrix products: 3.76 us -> 0 us
  starting transfers between devices: 12.7 us -> 15.1 us
    ppermute x11 -> x12, waiting for transfers between devices: 24.8 us -> 12.9 us  [trade(): lax.ppermute(value, axis, [(place, place ^ distance) for place in range(c...]
    pallas_call x0 -> x10, Pallas kernels: none -> 8.52 us  [the longest x2 3.36 us: fetch(): pl.pallas_call(functools.partial(fetch_kernel, count), out_shape=[jax.Sha...]
    convert_element_type x6 -> x0, other arithmetic: 4.06 us -> none  [the longest x1 1.52 us: body(): (residual + mine).astype(jnp.bfloat16).reshape(micro, row_count, part)]
    dot_general x3 -> x0, matrix products: 3.76 us -> none  [the longest x1 2.54 us: body(): lax.dot_general(normed, stacked_in, (((1,), (1,)), ((), ())), preferred_e...]
    unnamed x18 -> x0, local copies, waits for them, and re-layouts: 3.51 us -> none
    ppermute x11 -> x12, starting transfers between devices: 12.7 us -> 15.1 us  [trade(): lax.ppermute(value, axis, [(place, place ^ distance) for place in range(c...]
    another operation x1 -> x0, other arithmetic: 1.15 us -> none  [body(): jnp.stack([message] + [trade(message, 'section', 2 * k) for k in range(1,...]
    concatenate x2 -> x0, local copies, waits for them, and re-layouts: 1.12 us -> none  [the longest x1 1.03 us: body(): jnp.concatenate([own, named, jnp.zeros((rows, 126), jnp.bfloat16)], axis=1)]
  transfers between devices with their start and end apart: 11 -> 12, of which waited for: 10 -> 7; matrix products, arithmetic and copies ran while one was open for 5% -> 0% of each run, Pallas kernels for 0% -> 19%
where the time goes in v2:
time: 36.8 us; the launch traced here: 36.6 us
  starting transfers between devices  15.1 us (41%)
  waiting for transfers between devices  12.9 us (35%)
  Pallas kernels  8.52 us (23%)
    ppermute x12, starting transfers between devices, trade(): lax.ppermute(value, axis, [(place, place ^ distance) for place in range(c...  15.1 us
    ppermute x12, waiting for transfers between devices, trade(): lax.ppermute(value, axis, [(place, place ^ distance) for place in range(c...  12.9 us
    pallas_call x2, Pallas kernels, fetch(): pl.pallas_call(functools.partial(fetch_kernel, count), out_shape=[jax.Sha...  3.36 us
    pallas_call x2, Pallas kernels, run_expert(): pl.pallas_call(functools.partial(expert_kernel, count), out_shape=[shaped...  2.86 us
  transfers between devices with their start and end apart: 12, of which 7 were waited for; matrix products, arithmetic and copies ran while one was open for 0% of the time, Pallas kernels for 19%

profile of v2, /device:TPU:0, one launch (start us, length us, event | category | flops | bytes accessed | tf_op | source)
XLA Modules:
  0.0 36.6 jit_solution(11499759827358624211)
XLA Ops:
  0.0 0.5 %collective-permute-start = (bf16[32,3072]{1,0:T(8,128)(2,1)}, bf16[32,3072]{1,0:T(8,128)(2,1)S(1)}, u32[]{:S(2)}, u32[]{:S(2)}) collective-permute-start(bf16[32,3072]{1,0:T(8,128)(2,1)} %bitcast.10), channel_id=1, source_target_pairs={{0,4},{4,0},{8,12},{12,8},{16,20},{20,16},{24,28},{28,24},{1,5},{5... | collective-permute-start | bytes 589832 | tf_op jit(solution)/shard_map/ppermute | solution.py:21
  0.5 0.1 collective-permute-start.1
  0.5 1.0 %fetch.2 = (bf16[32,3072]{1,0:T(8,128)(2,1)S(1)}, s32[2,2,16]{2,1,0:T(2,128)S(1)}, f32[1,3072]{1,0:T(1,128)S(1)}) custom-call(bf16[32,3072]{1,0:T(8,128)(2,1)} %bitcast.11, s32[2,2,16]{2,1,0:T(2,128)} %bitcast.15, f32[1,3072]{1,0:T(1,128)} %bitcast.13), custom_call_target="tpu_custom_call" | custom-call | tf_op jit(solution)/shard_map/fetch/pallas_call | solution.py:158
  1.5 0.3 collective-permute-done.1.other_named_ref
  1.8 0.0 collective-permute-done.other_ref
  1.8 0.6 %pack.1 = (bf16[32,3072]{1,0:T(8,128)(2,1)S(1)}, bf16[32,3072]{1,0:T(8,128)(2,1)S(1)}, bf16[32,3072]{1,0:T(8,128)(2,1)S(1)}, bf16[32,3072]{1,0:T(8,128)(2,1)S(1)...) custom-call(s32[1]{0:T(128)} %bitcast.4.section_ref, ...), custom_call_target="tpu_custom_call" | custom-call | tf_op jit(solution)/shard_map/pack/pallas_call | solution.py:79
  2.4 3.8 %collective-permute-start.2 = (bf16[32,3072]{1,0:T(8,128)(2,1)S(1)}, bf16[32,3072]{1,0:T(8,128)(2,1)S(1)}, u32[]{:S(2)}, u32[]{:S(2)}) collective-permute-start(bf16[32,3072]{1,0:T(8,128)(2,1)S(1)} %get-tuple-element.46), channel_id=1, source_target_pairs={{0,24},{4,28},{8,16},{12,20},{16,8},{20,12},{24,0},{28,4},{1,25},{... | collective-permute-start | bytes 589832 | tf_op jit(solution)/shard_map/ppermute | solution.py:21
  6.2 0.5 %collective-permute-start.4 = (bf16[32,3072]{1,0:T(8,128)(2,1)S(1)}, bf16[32,3072]{1,0:T(8,128)(2,1)S(1)}, u32[]{:S(2)}, u32[]{:S(2)}) collective-permute-start(bf16[32,3072]{1,0:T(8,128)(2,1)S(1)} %get-tuple-element.49), channel_id=1, source_target_pairs={{0,8},{4,12},{8,0},{12,4},{16,24},{20,28},{24,16},{28,20},{1,9},{5... | collective-permute-start | bytes 589832 | tf_op jit(solution)/shard_map/ppermute | solution.py:21
  6.7 0.1 collective-permute-start.5
  6.8 2.4 %fetch.3 = (bf16[8,3072]{1,0:T(8,128)(2,1)S(1)}, bf16[512,3072]{1,0:T(8,128)(2,1)S(1)}, bf16[256,3072]{1,0:T(8,128)(2,1)S(1)}) custom-call(bf16[8,3072]{1,0:T(8,128)(2,1)} %bitcast.12, bf16[512,3072]{1,0:T(8,128)(2,1)} %bitcast.8, bf16[256,3072]{1,0:T(8,128)(2,1)} %bitcast.9, f32[8,64]{1,0:T(8,128)S(1)} %get-tuple-element.36.refs_3_.slots_ref), custom_call_target="tpu_custom_call" | custom-call | tf_op jit(solution)/shard_map/fetch/pallas_call | solution.py:158
  9.2 2.7 %collective-permute-done.2.refs_1_ = bf16[32,3072]{1,0:T(8,128)(2,1)S(1)} collective-permute-done((bf16[32,3072]{1,0:T(8,128)(2,1)S(1)}, bf16[32,3072]{1,0:T(8,128)(2,1)S(1)}, u32[]{:S(2)}, u32[]{:S(2)}) %collective-permute-start.2) | collective-permute-done | bytes 196640 | tf_op jit(solution)/shard_map/ppermute | solution.py:21
  11.9 1.4 %expert.2 = (bf16[32,3072]{1,0:T(8,128)(2,1)S(1)}, bf16[32,3072]{1,0:T(8,128)(2,1)S(1)}) custom-call(bf16[512,3072]{1,0:T(8,128)(2,1)S(1)} %get-tuple-element.43.in_ref, bf16[256,3072]{1,0:T(8,128)(2,1)S(1)} %get-tuple-element.44.down_ref, bf16[32,3072]{1,0:T(8,128)(2,1)S(1)} %get-tuple-element.45.refs_0_, bf16[32,3072]{1,0:T(8,128)(2,1)S(1)} %collective-permute-done.2.refs_1_), custom_call_target="tpu_custom_call" | custom-call | tf_op jit(solution)/shard_map/expert/pallas_call | solution.py:188
  13.3 3.0 %collective-permute-start.3 = (bf16[32,3072]{1,0:T(8,128)(2,1)S(1)}, bf16[32,3072]{1,0:T(8,128)(2,1)S(1)}, u32[]{:S(2)}, u32[]{:S(2)}) collective-permute-start(bf16[32,3072]{1,0:T(8,128)(2,1)S(1)} %get-tuple-element.48), channel_id=1, source_target_pairs={{0,24},{4,28},{8,16},{12,20},{16,8},{20,12},{24,0},{28,4},{1,25},{... | collective-permute-start | bytes 589832 | tf_op jit(solution)/shard_map/ppermute | solution.py:21
  16.4 0.0 collective-permute-done.4.refs_0_
  16.4 0.0 collective-permute-done.5.refs_1_
  16.4 1.4 %expert.3 = (bf16[32,3072]{1,0:T(8,128)(2,1)S(1)}, bf16[32,3072]{1,0:T(8,128)(2,1)S(1)}) custom-call(bf16[512,3072]{1,0:T(8,128)(2,1)S(1)} %get-tuple-element.43.in_ref, bf16[256,3072]{1,0:T(8,128)(2,1)S(1)} %get-tuple-element.44.down_ref, bf16[32,3072]{1,0:T(8,128)(2,1)S(1)} %collective-permute-done.4.refs_0_, ...), custom_call_target="tpu_custom_call" | custom-call | tf_op jit(solution)/shard_map/expert/pallas_call | solution.py:188
  17.8 1.2 %collective-permute-start.6 = (bf16[32,3072]{1,0:T(8,128)(2,1)S(1)}, bf16[32,3072]{1,0:T(8,128)(2,1)S(1)}, u32[]{:S(2)}, u32[]{:S(2)}) collective-permute-start(bf16[32,3072]{1,0:T(8,128)(2,1)S(1)} %get-tuple-element.51), channel_id=1, source_target_pairs={{0,8},{4,12},{8,0},{12,4},{16,24},{20,28},{24,16},{28,20},{1,9},{5... | collective-permute-start | bytes 589832 | tf_op jit(solution)/shard_map/ppermute | solution.py:21
  19.0 1.4 %collective-permute-start.7 = (bf16[32,3072]{1,0:T(8,128)(2,1)S(1)}, bf16[32,3072]{1,0:T(8,128)(2,1)S(1)}, u32[]{:S(2)}, u32[]{:S(2)}) collective-permute-start(bf16[32,3072]{1,0:T(8,128)(2,1)S(1)} %get-tuple-element.52), channel_id=1, source_target_pairs={{0,16},{4,20},{8,24},{12,28},{16,0},{20,4},{24,8},{28,12},{1,17},{... | collective-permute-start | bytes 589832 | tf_op jit(solution)/shard_map/ppermute | solution.py:21
  20.4 0.4 mix.1
  20.8 0.3 begin.1.begun_ref
  21.1 3.6 %collective-permute-done.6.refs_0_ = bf16[32,3072]{1,0:T(8,128)(2,1)S(1)} collective-permute-done((bf16[32,3072]{1,0:T(8,128)(2,1)S(1)}, bf16[32,3072]{1,0:T(8,128)(2,1)S(1)}, u32[]{:S(2)}, u32[]{:S(2)}) %collective-permute-start.6) | collective-permute-done | bytes 196640 | tf_op jit(solution)/shard_map/ppermute | solution.py:21
  24.7 0.7 %collective-permute-done.7.refs_1_ = bf16[32,3072]{1,0:T(8,128)(2,1)S(1)} collective-permute-done((bf16[32,3072]{1,0:T(8,128)(2,1)S(1)}, bf16[32,3072]{1,0:T(8,128)(2,1)S(1)}, u32[]{:S(2)}, u32[]{:S(2)}) %collective-permute-start.7) | collective-permute-done | bytes 196640 | tf_op jit(solution)/shard_map/ppermute | solution.py:21
  25.4 0.3 combine.1
  25.8 0.1 collective-permute-start.8
  25.8 1.4 %collective-permute-done.8.back_ref = bf16[32,3072]{1,0:T(8,128)(2,1)S(1)} collective-permute-done((bf16[32,3072]{1,0:T(8,128)(2,1)S(1)}, bf16[32,3072]{1,0:T(8,128)(2,1)S(1)}, u32[]{:S(2)}, u32[]{:S(2)}) %collective-permute-start.8) | collective-permute-done | bytes 196640 | tf_op jit(solution)/shard_map/ppermute | solution.py:21
  27.3 0.1 split.1
  27.3 3.7 %collective-permute-start.9 = (bf16[32,768]{1,0:T(8,128)(2,1)S(1)}, bf16[32,768]{1,0:T(8,128)(2,1)S(1)}, u32[]{:S(2)}, u32[]{:S(2)}) collective-permute-start(bf16[32,768]{1,0:T(8,128)(2,1)S(1)} %get-tuple-element.56), channel_id=1, source_target_pairs={{0,3},{1,2},{2,1},{3,0},{4,7},{5,6},{6,5},{7,4},{8,11},{9,10},{10,... | collective-permute-start | bytes 147464 | tf_op jit(solution)/shard_map/ppermute | solution.py:21
  31.0 0.8 %collective-permute-start.11 = (bf16[32,768]{1,0:T(8,128)(2,1)S(1)}, bf16[32,768]{1,0:T(8,128)(2,1)S(1)}, u32[]{:S(2)}, u32[]{:S(2)}) collective-permute-start(bf16[32,768]{1,0:T(8,128)(2,1)S(1)} %get-tuple-element.58), channel_id=1, source_target_pairs={{0,1},{1,0},{2,3},{3,2},{4,5},{5,4},{6,7},{7,6},{8,9},{9,8},{10,11... | collective-permute-start | bytes 147464 | tf_op jit(solution)/shard_map/ppermute | solution.py:21
  31.8 1.6 %collective-permute-done.9.refs_1_ = bf16[32,768]{1,0:T(8,128)(2,1)S(1)} collective-permute-done((bf16[32,768]{1,0:T(8,128)(2,1)S(1)}, bf16[32,768]{1,0:T(8,128)(2,1)S(1)}, u32[]{:S(2)}, u32[]{:S(2)}) %collective-permute-start.9) | collective-permute-done | bytes 49184 | tf_op jit(solution)/shard_map/ppermute | solution.py:21
  33.3 2.7 %collective-permute-done.10.refs_2_ = bf16[32,768]{1,0:T(8,128)(2,1)S(1)} collective-permute-done((bf16[32,768]{1,0:T(8,128)(2,1)S(1)}, bf16[32,768]{1,0:T(8,128)(2,1)S(1)}, u32[]{:S(2)}, u32[]{:S(2)}) %collective-permute-start.10) | collective-permute-done | bytes 49184 | tf_op jit(solution)/shard_map/ppermute | solution.py:21
  36.0 0.0 collective-permute-done.11.refs_3_
  36.0 0.6 %finish.1 = bf16[2,16,768]{2,1,0:T(8,128)(2,1)} custom-call(f32[32,768]{1,0:T(8,128)S(1)} %get-tuple-element.55.refs_0_, bf16[32,768]{1,0:T(8,128)(2,1)S(1)} %collective-permute-done.9.refs_1_, bf16[32,768]{1,0:T(8,128)(2,1)S(1)} %collective-permute-done.10.refs_2_, bf16[32,768]{1,0:T(8,128)(2,1)S(1)} %collective-permute-done.11.refs_3_), custom_call_target="tpu_custom_call" | custom-call | tf_op jit(solution)/shard_map/finish/pallas_call | solution.py:295
  (2 shorter events, 0.0 us)
Async XLA Ops:
  0.0 1.8 %collective-permute-start = (bf16[32,3072]{1,0:T(8,128)(2,1)}, bf16[32,3072]{1,0:T(8,128)(2,1)S(1)}, u32[]{:S(2)}, u32[]{:S(2)}) collective-permute-start(bf16[32,3072]{1,0:T(8,128)(2,1)} %bitcast.10), channel_id=1, source_target_pairs={{0,4},{4,0},{8,12},{12,8},{16,20},{20,16},{24,28},{28,24},{1,5},{5... | collective-permute-start | bytes 589832 | tf_op jit(solution)/shard_map/ppermute | solution.py:21
  0.5 1.4 %collective-permute-start.1 = (s32[2,2,16]{2,1,0:T(2,128)}, s32[2,2,16]{2,1,0:T(2,128)S(1)}, u32[]{:S(2)}, u32[]{:S(2)}) collective-permute-start(s32[2,2,16]{2,1,0:T(2,128)} %bitcast.14), channel_id=1, source_target_pairs={{0,4},{4,0},{8,12},{12,8},{16,20},{20,16},{24,28},{28,24},{1,5},{5... | collective-permute-start | bytes 776 | tf_op jit(solution)/shard_map/ppermute | solution.py:21
  2.4 9.5 %collective-permute-start.2 = (bf16[32,3072]{1,0:T(8,128)(2,1)S(1)}, bf16[32,3072]{1,0:T(8,128)(2,1)S(1)}, u32[]{:S(2)}, u32[]{:S(2)}) collective-permute-start(bf16[32,3072]{1,0:T(8,128)(2,1)S(1)} %get-tuple-element.46), channel_id=1, source_target_pairs={{0,24},{4,28},{8,16},{12,20},{16,8},{20,12},{24,0},{28,4},{1,25},{... | collective-permute-start | bytes 589832 | tf_op jit(solution)/shard_map/ppermute | solution.py:21
  6.2 10.2 %collective-permute-start.4 = (bf16[32,3072]{1,0:T(8,128)(2,1)S(1)}, bf16[32,3072]{1,0:T(8,128)(2,1)S(1)}, u32[]{:S(2)}, u32[]{:S(2)}) collective-permute-start(bf16[32,3072]{1,0:T(8,128)(2,1)S(1)} %get-tuple-element.49), channel_id=1, source_target_pairs={{0,8},{4,12},{8,0},{12,4},{16,24},{20,28},{24,16},{28,20},{1,9},{5... | collective-permute-start | bytes 589832 | tf_op jit(solution)/shard_map/ppermute | solution.py:21
  6.7 9.7 %collective-permute-start.5 = (bf16[32,3072]{1,0:T(8,128)(2,1)S(1)}, bf16[32,3072]{1,0:T(8,128)(2,1)S(1)}, u32[]{:S(2)}, u32[]{:S(2)}) collective-permute-start(bf16[32,3072]{1,0:T(8,128)(2,1)S(1)} %get-tuple-element.50), channel_id=1, source_target_pairs={{0,16},{4,20},{8,24},{12,28},{16,0},{20,4},{24,8},{28,12},{1,17},{... | collective-permute-start | bytes 589832 | tf_op jit(solution)/shard_map/ppermute | solution.py:21
  13.3 7.4 %collective-permute-start.3 = (bf16[32,3072]{1,0:T(8,128)(2,1)S(1)}, bf16[32,3072]{1,0:T(8,128)(2,1)S(1)}, u32[]{:S(2)}, u32[]{:S(2)}) collective-permute-start(bf16[32,3072]{1,0:T(8,128)(2,1)S(1)} %get-tuple-element.48), channel_id=1, source_target_pairs={{0,24},{4,28},{8,16},{12,20},{16,8},{20,12},{24,0},{28,4},{1,25},{... | collective-permute-start | bytes 589832 | tf_op jit(solution)/shard_map/ppermute | solution.py:21
  17.8 6.9 %collective-permute-start.6 = (bf16[32,3072]{1,0:T(8,128)(2,1)S(1)}, bf16[32,3072]{1,0:T(8,128)(2,1)S(1)}, u32[]{:S(2)}, u32[]{:S(2)}) collective-permute-start(bf16[32,3072]{1,0:T(8,128)(2,1)S(1)} %get-tuple-element.51), channel_id=1, source_target_pairs={{0,8},{4,12},{8,0},{12,4},{16,24},{20,28},{24,16},{28,20},{1,9},{5... | collective-permute-start | bytes 589832 | tf_op jit(solution)/shard_map/ppermute | solution.py:21
  19.0 6.4 %collective-permute-start.7 = (bf16[32,3072]{1,0:T(8,128)(2,1)S(1)}, bf16[32,3072]{1,0:T(8,128)(2,1)S(1)}, u32[]{:S(2)}, u32[]{:S(2)}) collective-permute-start(bf16[32,3072]{1,0:T(8,128)(2,1)S(1)} %get-tuple-element.52), channel_id=1, source_target_pairs={{0,16},{4,20},{8,24},{12,28},{16,0},{20,4},{24,8},{28,12},{1,17},{... | collective-permute-start | bytes 589832 | tf_op jit(solution)/shard_map/ppermute | solution.py:21
  25.8 1.5 %collective-permute-start.8 = (bf16[32,3072]{1,0:T(8,128)(2,1)S(1)}, bf16[32,3072]{1,0:T(8,128)(2,1)S(1)}, u32[]{:S(2)}, u32[]{:S(2)}) collective-permute-start(bf16[32,3072]{1,0:T(8,128)(2,1)S(1)} %get-tuple-element.54), channel_id=1, source_target_pairs={{0,4},{4,0},{8,12},{12,8},{16,20},{20,16},{24,28},{28,24},{1,5},{5... | collective-permute-start | bytes 589832 | tf_op jit(solution)/shard_map/ppermute | solution.py:21
  27.3 6.0 %collective-permute-start.9 = (bf16[32,768]{1,0:T(8,128)(2,1)S(1)}, bf16[32,768]{1,0:T(8,128)(2,1)S(1)}, u32[]{:S(2)}, u32[]{:S(2)}) collective-permute-start(bf16[32,768]{1,0:T(8,128)(2,1)S(1)} %get-tuple-element.56), channel_id=1, source_target_pairs={{0,3},{1,2},{2,1},{3,0},{4,7},{5,6},{6,5},{7,4},{8,11},{9,10},{10,... | collective-permute-start | bytes 147464 | tf_op jit(solution)/shard_map/ppermute | solution.py:21
  31.0 5.0 %collective-permute-start.10 = (bf16[32,768]{1,0:T(8,128)(2,1)S(1)}, bf16[32,768]{1,0:T(8,128)(2,1)S(1)}, u32[]{:S(2)}, u32[]{:S(2)}) collective-permute-start(bf16[32,768]{1,0:T(8,128)(2,1)S(1)} %get-tuple-element.57), channel_id=1, source_target_pairs={{0,2},{1,3},{2,0},{3,1},{4,6},{5,7},{6,4},{7,5},{8,10},{9,11},{10,... | collective-permute-start | bytes 147464 | tf_op jit(solution)/shard_map/ppermute | solution.py:21
  31.0 5.0 %collective-permute-start.11 = (bf16[32,768]{1,0:T(8,128)(2,1)S(1)}, bf16[32,768]{1,0:T(8,128)(2,1)S(1)}, u32[]{:S(2)}, u32[]{:S(2)}) collective-permute-start(bf16[32,768]{1,0:T(8,128)(2,1)S(1)} %get-tuple-element.58), channel_id=1, source_target_pairs={{0,1},{1,0},{2,3},{3,2},{4,5},{5,4},{6,7},{7,6},{8,9},{9,8},{10,11... | collective-permute-start | bytes 147464 | tf_op jit(solution)/shard_map/ppermute | solution.py:21

commit v3 on v2

--- a/solution.py
+++ b/solution.py
@@ -11,6 +11,7 @@
 LANES = 128
 NT = (((1,), (1,)), ((), ()))
 VMEM = pl.BlockSpec(memory_space=pltpu.VMEM)
+ANY = pl.BlockSpec(memory_space=pl.ANY)
 HBM = pl.BlockSpec(memory_space=pltpu.HBM)
 SMEM = pl.BlockSpec(memory_space=pltpu.SMEM)
 PARAMS = pltpu.CompilerParams(vmem_limit_bytes=20 * 1024 * 1024)
@@ -26,7 +27,7 @@
 
 
 def expert_at(section, distance, per_expert):
-    return lax.div(section ^ (2 * distance), jnp.int32(per_expert))
+    return lax.div(section ^ distance, jnp.int32(per_expert))
 
 
 def pack_kernel(chips, per_expert, experts, section_ref, tokens_ref, other_ref, named_ref, other_named_ref, gain_ref, *refs):
@@ -65,7 +66,7 @@
     slot_ids = lax.broadcasted_iota(jnp.int32, (rows, every), 0).astype(jnp.float32)
     picks = []
     for k in range(chips):
-        expert = expert_at(section, k, per_expert).astype(jnp.float32)
+        expert = expert_at(section, 2 * k, per_expert).astype(jnp.float32)
         slot = jnp.sum(jnp.where(ids == expert, slots, 0.0), axis=0, keepdims=True)
         picks.append(jnp.where(slot == slot_ids, 1.0, 0.0))
     pick = jnp.concatenate(picks, axis=0).astype(jnp.bfloat16)
@@ -112,27 +113,36 @@
     weight_b = 1.0 / (1.0 + jnp.exp(lead - trail))
     section = section_ref[0]
     tall = lax.broadcasted_iota(jnp.int32, (experts, every), 0).astype(jnp.float32)
-    for place, ks in enumerate(sets):
-        shape = (every, len(ks) * rows)
-        lanes = lax.broadcasted_iota(jnp.int32, shape, 1).astype(jnp.float32)
-        spread = jnp.zeros(shape, jnp.float32)
-        for at, k in enumerate(ks):
-            expert = expert_at(section, k, per_expert).astype(jnp.float32)
+    for place, distances in enumerate(sets):
+        high_ref, low_ref = outs[2 * place : 2 * place + 2]
+        count, width = high_ref.shape
+        each = width // len(distances)
+        lanes = lax.broadcasted_iota(jnp.int32, (count, width), 1).astype(jnp.float32)
+        spread = jnp.zeros((count, width), jnp.float32)
+        for at, distance in enumerate(distances):
+            expert = expert_at(section, distance, per_expert).astype(jnp.float32)
             slot = jnp.sum(jnp.where(tall == expert, slots_ref[...], 0.0), axis=0, keepdims=True)
             weight = jnp.where(first == expert, weight_a, 0.0) + jnp.where(
                 second == expert, weight_b, 0.0
             )
-            spread = spread + jnp.where(upright(slot) + at * rows == lanes, weight, 0.0)
+            spread = spread + jnp.where(
+                upright(slot)[:count] + at * each == lanes, weight[:count], 0.0
+            )
         high = spread.astype(jnp.bfloat16)
-        outs[2 * place][...] = high
-        outs[2 * place + 1][...] = (spread - high.astype(jnp.float32)).astype(jnp.bfloat16)
-
-
-def mix(section, normed, slots, named, router, sets, per_expert):
+        high_ref[...] = high
+        low_ref[...] = (spread - high.astype(jnp.float32)).astype(jnp.bfloat16)
+
+
+def mix(section, normed, slots, named, router, early, near, per_expert):
     every = normed.shape[0]
-    shapes = [shaped(every, len(ks) * every // 2, jnp.bfloat16) for ks in sets for _ in range(2)]
-    return pl.pallas_call(
-        functools.partial(mix_kernel, sets, per_expert),
+    rows = every // 2
+    shapes = [
+        shaped(rows, len(distances) * rows // 2, jnp.bfloat16)
+        for distances in (early, near)
+        for _ in range(2)
+    ]
+    return pl.pallas_call(
+        functools.partial(mix_kernel, (early, near), per_expert),
         out_shape=shapes,
         in_specs=[SMEM] + [VMEM] * 4,
         out_specs=[VMEM] * len(shapes),
@@ -166,34 +176,73 @@
     )(*[pltpu.with_memory_space_constraint(a, pltpu.HBM) for a in arrays], *after)
 
 
-def expert_kernel(count, in_ref, down_ref, *refs):
-    blocks, out_refs, every_ref = refs[:count], refs[-1 - count : -1], refs[-1]
-    rows = blocks[0].shape[0]
-    for place, block in enumerate(blocks):
-        every_ref[place * rows : (place + 1) * rows, :] = block[...]
-    gate_up = lax.dot_general(
-        every_ref[...], in_ref[...], NT, preferred_element_type=jnp.float32
-    )
+def load_kernel(count, in_ref, *refs):
+    sources, targets = refs[:count], refs[count + 2 : 2 * count + 2]
+    turned_ref, held_ref, sems = refs[count + 1], refs[-2], refs[-1]
+    pieces, rows, _ = held_ref.shape
+    copies = [
+        pltpu.make_async_copy(in_ref.at[pl.ds(k * rows, rows)], held_ref.at[k], sems.at[k])
+        for k in range(pieces)
+    ]
+    others = [
+        pltpu.make_async_copy(source, target, sems.at[pieces + k])
+        for k, (source, target) in enumerate(zip(sources, targets))
+    ]
+    for copy in copies + others:
+        copy.start()
+    for k in range(pieces):
+        copies[k].wait()
+        turned_ref[:, k * rows : (k + 1) * rows] = held_ref[k].T
+    for copy in others:
+        copy.wait()
+
+
+def load_weights(stacked_in, others, after):
+    count = len(others)
+    rows, width = stacked_in.shape
+    pieces = max(1, rows // LANES)
+    arrays = [stacked_in, *others]
+    return pl.pallas_call(
+        functools.partial(load_kernel, count),
+        out_shape=[shaped(width, rows, stacked_in.dtype)]
+        + [jax.ShapeDtypeStruct(a.shape, a.dtype) for a in others],
+        in_specs=[HBM] * (count + 1) + [VMEM],
+        out_specs=[VMEM] * (count + 1),
+        scratch_shapes=[
+            pltpu.VMEM((pieces, rows // pieces, width), stacked_in.dtype),
+            pltpu.SemaphoreType.DMA((pieces + count,)),
+        ],
+        compiler_params=PARAMS,
+        name="load_weights",
+    )(*[pltpu.with_memory_space_constraint(a, pltpu.HBM) for a in arrays], after)
+
+
+def expert_kernel(count, after, in_ref, down_ref, *refs):
+    blocks, every_ref = refs[:count], refs[-1]
+    out_refs = refs[count + after : -1]
+    every = gathered(blocks, every_ref)
+    gate_up = jnp.dot(every, in_ref[...], preferred_element_type=jnp.float32)
     hidden = gate_up.shape[1] // 2
     gate = gate_up[:, :hidden]
     active = (gate / (1.0 + jnp.exp(-gate)) * gate_up[:, hidden:]).astype(jnp.bfloat16)
     partial = jnp.dot(active, down_ref[...], preferred_element_type=jnp.float32)
+    rows = out_refs[0].shape[0]
     for place, out_ref in enumerate(out_refs):
         out_ref[...] = partial[place * rows : (place + 1) * rows, :].astype(jnp.bfloat16)
 
 
-def run_expert(blocks, stacked_in, down, after=()):
+def run_expert(blocks, turned_in, down, pieces, after=()):
     count = len(blocks)
     rows, width = blocks[0].shape
     return pl.pallas_call(
-        functools.partial(expert_kernel, count),
-        out_shape=[shaped(rows, width, jnp.bfloat16)] * count,
-        in_specs=[VMEM] * (2 + count) + [pl.BlockSpec(memory_space=pl.ANY)] * len(after),
-        out_specs=[VMEM] * count,
+        functools.partial(expert_kernel, count, len(after)),
+        out_shape=[shaped(rows // pieces, width, jnp.bfloat16)] * (count * pieces),
+        in_specs=[VMEM] * (2 + count) + [ANY] * len(after),
+        out_specs=[VMEM] * (count * pieces),
         scratch_shapes=[pltpu.VMEM((count * rows, width), jnp.bfloat16)],
         compiler_params=PARAMS,
         name="expert",
-    )(stacked_in, down, *blocks, *after)
+    )(turned_in, down, *blocks, *after)
 
 
 def gathered(blocks, every_ref):
@@ -212,72 +261,65 @@
 
 def begin(high, low, blocks):
     count = len(blocks)
-    rows, width = blocks[0].shape
+    each, width = blocks[0].shape
     return pl.pallas_call(
         functools.partial(begin_kernel, count),
-        out_shape=shaped(2 * rows, width, jnp.float32),
+        out_shape=shaped(high.shape[0], width, jnp.float32),
         in_specs=[VMEM] * (2 + count),
         out_specs=VMEM,
-        scratch_shapes=[pltpu.VMEM((count * rows, width), jnp.bfloat16)],
+        scratch_shapes=[pltpu.VMEM((count * each, width), jnp.bfloat16)],
         compiler_params=PARAMS,
         name="begin",
     )(high, low, *blocks)
 
 
-def combine_kernel(count, high_ref, low_ref, begun_ref, *refs):
-    blocks, keep_ref, send_ref, every_ref = refs[:count], refs[count], refs[count + 1], refs[-1]
-    rows = blocks[0].shape[0]
+def close_kernel(count, member_ref, tokens_ref, high_ref, low_ref, begun_ref, *refs):
+    blocks, outs, every_ref, total_ref = refs[:count], refs[count:-2], refs[-2], refs[-1]
     every = gathered(blocks, every_ref)
     total = begun_ref[...] + jnp.dot(low_ref[...], every, preferred_element_type=jnp.float32)
-    total = total + jnp.dot(high_ref[...], every, preferred_element_type=jnp.float32)
-    keep_ref[...] = total[:rows]
-    send_ref[...] = total[rows:].astype(jnp.bfloat16)
-
-
-def combine(high, low, begun, blocks):
-    count = len(blocks)
-    rows, width = blocks[0].shape
-    return pl.pallas_call(
-        functools.partial(combine_kernel, count),
-        out_shape=[shaped(rows, width, jnp.float32), shaped(rows, width, jnp.bfloat16)],
-        in_specs=[VMEM] * (3 + count),
-        out_specs=[VMEM] * 2,
-        scratch_shapes=[pltpu.VMEM((count * rows, width), jnp.bfloat16)],
-        compiler_params=PARAMS,
-        name="combine",
-    )(high, low, begun, *blocks)
-
-
-def split_kernel(member_ref, tokens_ref, keep_ref, back_ref, *outs):
+    total_ref[...] = total + jnp.dot(high_ref[...], every, preferred_element_type=jnp.float32)
+    if len(outs) == 1:
+        outs[0][...] = total_ref[...]
+        return
     part = outs[0].shape[1]
     for k, out_ref in enumerate(outs):
         columns = pl.ds(pl.multiple_of((member_ref[0] ^ k) * part, LANES), part)
-        total = keep_ref[:, columns] + back_ref[:, columns].astype(jnp.float32)
+        value = total_ref[:, columns]
         if k == 0:
-            total = total + tokens_ref[:, columns].astype(jnp.float32)
-        out_ref[...] = total.astype(out_ref.dtype)
-
-
-def split_up(keep, back, tokens, member, inner_count):
-    rows, width = keep.shape
+            value = value + tokens_ref[:, columns].astype(jnp.float32)
+        out_ref[...] = value.astype(out_ref.dtype)
+
+
+def close(high, low, begun, blocks, tokens, member, inner_count):
+    count = len(blocks)
+    each = blocks[0].shape[0]
+    rows, width = begun.shape
     part = width // inner_count
-    if part % LANES:
-        total = keep + back.astype(jnp.float32)
-        rounded = total.astype(jnp.bfloat16)
-        total = total + tokens.astype(jnp.float32)
-        outs = [lax.dynamic_slice_in_dim(total, member * part, part, 1)]
-        for k in range(1, inner_count):
-            outs.append(lax.dynamic_slice_in_dim(rounded, (member ^ k) * part, part, 1))
+    whole = part % LANES != 0
+    kinds = [jnp.float32] + [jnp.bfloat16] * (inner_count - 1)
+    shapes = [shaped(rows, part, kind) for kind in kinds]
+    if whole:
+        shapes = [shaped(rows, width, jnp.float32)]
+    outs = pl.pallas_call(
+        functools.partial(close_kernel, count),
+        out_shape=shapes,
+        in_specs=[SMEM] + [VMEM] * (4 + count),
+        out_specs=[VMEM] * len(shapes),
+        scratch_shapes=[
+            pltpu.VMEM((count * each, width), jnp.bfloat16),
+            pltpu.VMEM((rows, width), jnp.float32),
+        ],
+        compiler_params=PARAMS,
+        name="close",
+    )(member.reshape(1), tokens, high, low, begun, *blocks)
+    if not whole:
         return outs
-    kinds = [jnp.float32] + [jnp.bfloat16] * (inner_count - 1)
-    return pl.pallas_call(
-        split_kernel,
-        out_shape=[shaped(rows, part, kind) for kind in kinds],
-        in_specs=[SMEM] + [VMEM] * 3,
-        out_specs=[VMEM] * inner_count,
-        compiler_params=PARAMS,
-        name="split",
-    )(member.reshape(1), tokens, keep, back)
+    rounded = outs[0].astype(jnp.bfloat16)
+    total = outs[0] + tokens.astype(jnp.float32)
+    outs = [lax.dynamic_slice_in_dim(total, member * part, part, 1)]
+    for k in range(1, inner_count):
+        outs.append(lax.dynamic_slice_in_dim(rounded, (member ^ k) * part, part, 1))
+    return outs
 
 
 def final_kernel(*refs):
@@ -325,22 +367,30 @@
     )
     order = list(range(1, chips))
     arrived = {k: trade(messages[k], "section", 2 * k) for k in reversed(order)}
-    router_rows, stacked_in, down = fetch(
-        (router.T, expert_in[0].reshape(2 * hidden, width), expert_out[0]), (slots,)
+    turned_in, router_rows, down = load_weights(
+        expert_in[0].reshape(2 * hidden, width), (router.T, expert_out[0]), slots
     )
     far, near = order[-1], order[:-1]
-    sets = ((0, far), tuple(near))
+    early = (0, 1, 2 * far, 2 * far + 1)
+    late = tuple(distance for k in near for distance in (2 * k, 2 * k + 1))
     high_a, low_a, high_b, low_b = mix(
-        section, normed, slots, names, router_rows, sets, per_expert
-    )
-    here, away = run_expert([messages[0], arrived[far]], stacked_in, down)
-    early = [here, trade(away, "section", 2 * far)]
-    late = run_expert([arrived[k] for k in near], stacked_in, down, (here,))
-    late = [trade(value, "section", 2 * k) for k, value in zip(near, late)]
-    begun = begin(high_a, low_a, early)
-    keep, send = combine(high_b, low_b, begun, late)
-    back = trade(send, "section", 1)
-    split = split_up(keep, back, own, member, inner_count)
+        section, normed, slots, names, router_rows, early, late, per_expert
+    )
+
+    def come_back(blocks, distances):
+        return [
+            trade(block, "section", distance) if distance else block
+            for block, distance in zip(blocks, distances)
+        ]
+
+    early_blocks = run_expert([messages[0], arrived[far]], turned_in, down, 2)
+    late_blocks = run_expert(
+        [arrived[k] for k in near], turned_in, down, 2, (early_blocks[0],)
+    )
+    begun = begin(high_a, low_a, come_back(early_blocks, early))
+    split = close(
+        high_b, low_b, begun, come_back(late_blocks, late), own, member, inner_count
+    )
     pieces = {k: trade(split[k], "inner", k) for k in reversed(range(1, inner_count))}
     pieces[0] = split[0]
     return finish([pieces[k] for k in [0] + list(reversed(range(1, inner_count)))], micro, row_count)

time: 36.8 us -> 35.9 us (0.976)
  Pallas kernels: 8.52 us -> 7.47 us
  starting transfers between devices: 15.1 us -> 16.1 us
  waiting for transfers between devices: 12.9 us -> 12 us
    pallas_call x2 -> x1, Pallas kernels: 3.36 us -> 0.96 us  [fetch(): pl.pallas_call(functools.partial(fetch_kernel, count), out_shape=[jax.Sha...]
    pallas_call x6, Pallas kernels: 3.96 us -> 5.32 us  [the longest x1 2.43 us: load_weights(): pl.pallas_call(functools.partial(load_kernel, count), out_shape=[shaped(w...]
    ppermute x12 -> x15, starting transfers between devices: 15.1 us -> 16.1 us  [trade(): lax.ppermute(value, axis, [(place, place ^ distance) for place in range(c...]
    ppermute x12 -> x15, waiting for transfers between devices: 12.9 us -> 12 us  [trade(): lax.ppermute(value, axis, [(place, place ^ distance) for place in range(c...]
  transfers between devices with their start and end apart: 12 -> 15, of which waited for: 7 -> 8; matrix products, arithmetic and copies ran while one was open for 0% -> 0% of each run, Pallas kernels for 19% -> 17%
where the time goes in v3:
time: 35.9 us; the launch traced here: 35.7 us
  starting transfers between devices  16.1 us (45%)
  waiting for transfers between devices  12 us (33%)
  Pallas kernels  7.47 us (21%)
    ppermute x15, starting transfers between devices, trade(): lax.ppermute(value, axis, [(place, place ^ distance) for place in range(c...  16.1 us
    ppermute x15, waiting for transfers between devices, trade(): lax.ppermute(value, axis, [(place, place ^ distance) for place in range(c...  12 us
    pallas_call x1, Pallas kernels, load_weights(): pl.pallas_call(functools.partial(load_kernel, count), out_shape=[shaped(w...  2.43 us
    pallas_call x2, Pallas kernels, run_expert(): pl.pallas_call(functools.partial(expert_kernel, count, len(after)), out_s...  2.03 us
    pallas_call x1, Pallas kernels, fetch(): pl.pallas_call(functools.partial(fetch_kernel, count), out_shape=[jax.Sha...  0.96 us
  transfers between devices with their start and end apart: 15, of which 8 were waited for; matrix products, arithmetic and copies ran while one was open for 0% of the time, Pallas kernels for 17%

profile of v3, /device:TPU:0, one launch (start us, length us, event | category | flops | bytes accessed | tf_op | source)
XLA Modules:
  0.0 35.7 jit_solution(15856397118934367266)
XLA Ops:
  0.0 0.5 %collective-permute-start = (bf16[32,3072]{1,0:T(8,128)(2,1)}, bf16[32,3072]{1,0:T(8,128)(2,1)S(1)}, u32[]{:S(2)}, u32[]{:S(2)}) collective-permute-start(bf16[32,3072]{1,0:T(8,128)(2,1)} %bitcast.10), channel_id=1, source_target_pairs={{0,4},{4,0},{8,12},{12,8},{16,20},{20,16},{24,28},{28,24},{1,5},{5... | collective-permute-start | bytes 589832 | tf_op jit(solution)/shard_map/ppermute | solution.py:22
  0.5 0.1 collective-permute-start.1
  0.5 1.0 %fetch.1 = (bf16[32,3072]{1,0:T(8,128)(2,1)S(1)}, s32[2,2,16]{2,1,0:T(2,128)S(1)}, f32[1,3072]{1,0:T(1,128)S(1)}) custom-call(bf16[32,3072]{1,0:T(8,128)(2,1)} %bitcast.11, s32[2,2,16]{2,1,0:T(2,128)} %bitcast.15, f32[1,3072]{1,0:T(1,128)} %bitcast.13), custom_call_target="tpu_custom_call" | custom-call | tf_op jit(solution)/shard_map/fetch/pallas_call | solution.py:168
  1.5 0.3 collective-permute-done.1.other_named_ref
  1.8 0.6 %pack.1 = (bf16[32,3072]{1,0:T(8,128)(2,1)S(1)}, bf16[32,3072]{1,0:T(8,128)(2,1)S(1)}, bf16[32,3072]{1,0:T(8,128)(2,1)S(1)}, bf16[32,3072]{1,0:T(8,128)(2,1)S(1)...) custom-call(s32[1]{0:T(128)} %bitcast.4.section_ref, ...), custom_call_target="tpu_custom_call" | custom-call | tf_op jit(solution)/shard_map/pack/pallas_call | solution.py:80
  2.4 3.8 %collective-permute-start.2 = (bf16[32,3072]{1,0:T(8,128)(2,1)S(1)}, bf16[32,3072]{1,0:T(8,128)(2,1)S(1)}, u32[]{:S(2)}, u32[]{:S(2)}) collective-permute-start(bf16[32,3072]{1,0:T(8,128)(2,1)S(1)} %get-tuple-element.48), channel_id=1, source_target_pairs={{0,24},{4,28},{8,16},{12,20},{16,8},{20,12},{24,0},{28,4},{1,25},{... | collective-permute-start | bytes 589832 | tf_op jit(solution)/shard_map/ppermute | solution.py:22
  6.2 0.5 %collective-permute-start.6 = (bf16[32,3072]{1,0:T(8,128)(2,1)S(1)}, bf16[32,3072]{1,0:T(8,128)(2,1)S(1)}, u32[]{:S(2)}, u32[]{:S(2)}) collective-permute-start(bf16[32,3072]{1,0:T(8,128)(2,1)S(1)} %get-tuple-element.53), channel_id=1, source_target_pairs={{0,8},{4,12},{8,0},{12,4},{16,24},{20,28},{24,16},{28,20},{1,9},{5... | collective-permute-start | bytes 589832 | tf_op jit(solution)/shard_map/ppermute | solution.py:22
  6.7 0.1 collective-permute-start.7
  6.8 2.4 %load_weights.1 = (bf16[3072,512]{1,0:T(8,128)(2,1)S(1)}, bf16[8,3072]{1,0:T(8,128)(2,1)S(1)}, bf16[256,3072]{1,0:T(8,128)(2,1)S(1)}) custom-call(bf16[512,3072]{1,0:T(8,128)(2,1)} %bitcast.8, bf16[8,3072]{1,0:T(8,128)(2,1)} %bitcast.12, bf16[256,3072]{1,0:T(8,128)(2,1)} %bitcast.9, f32[8,64]{1,0:T(8,128)S(1)} %get-tuple-element.38.refs_2_.slots_ref), custom_call_target="tpu_custom_call" | custom-call | tf_op jit(solution)/shard_map/load_weights/pallas_call | solution.py:205
  9.3 2.6 %collective-permute-done.2.refs_1_ = bf16[32,3072]{1,0:T(8,128)(2,1)S(1)} collective-permute-done((bf16[32,3072]{1,0:T(8,128)(2,1)S(1)}, bf16[32,3072]{1,0:T(8,128)(2,1)S(1)}, u32[]{:S(2)}, u32[]{:S(2)}) %collective-permute-start.2) | collective-permute-done | bytes 196640 | tf_op jit(solution)/shard_map/ppermute | solution.py:22
  11.9 1.0 %expert.2 = (bf16[16,3072]{1,0:T(8,128)(2,1)S(1)}, bf16[16,3072]{1,0:T(8,128)(2,1)S(1)}, bf16[16,3072]{1,0:T(8,128)(2,1)S(1)}, bf16[16,3072]{1,0:T(8,128)(2,1)S(1)}) custom-call(bf16[3072,512]{1,0:T(8,128)(2,1)S(1)} %get-tuple-element.45.in_ref, bf16[256,3072]{1,0:T(8,128)(2,1)S(1)} %get-tuple-element.46.down_ref, ...), custom_call_target="tpu_custom_call" | custom-call | tf_op jit(solution)/shard_map/expert/pallas_call | solution.py:237
  12.9 0.1 collective-permute-start.3
  13.0 3.0 %collective-permute-start.4 = (bf16[16,3072]{1,0:T(8,128)(2,1)S(1)}, bf16[16,3072]{1,0:T(8,128)(2,1)S(1)}, u32[]{:S(2)}, u32[]{:S(2)}) collective-permute-start(bf16[16,3072]{1,0:T(8,128)(2,1)S(1)} %get-tuple-element.51), channel_id=1, source_target_pairs={{0,24},{4,28},{8,16},{12,20},{16,8},{20,12},{24,0},{28,4},{1,25},{... | collective-permute-start | bytes 294920 | tf_op jit(solution)/shard_map/ppermute | solution.py:22
  16.0 0.1 collective-permute-start.5
  16.1 1.0 %expert.3 = (bf16[16,3072]{1,0:T(8,128)(2,1)S(1)}, bf16[16,3072]{1,0:T(8,128)(2,1)S(1)}, bf16[16,3072]{1,0:T(8,128)(2,1)S(1)}, bf16[16,3072]{1,0:T(8,128)(2,1)S(1)}) custom-call(bf16[3072,512]{1,0:T(8,128)(2,1)S(1)} %get-tuple-element.45.in_ref, bf16[256,3072]{1,0:T(8,128)(2,1)S(1)} %get-tuple-element.46.down_ref, ...), custom_call_target="tpu_custom_call" | custom-call | tf_op jit(solution)/shard_map/expert/pallas_call | solution.py:237
  17.1 1.7 %collective-permute-start.8 = (bf16[16,3072]{1,0:T(8,128)(2,1)S(1)}, bf16[16,3072]{1,0:T(8,128)(2,1)S(1)}, u32[]{:S(2)}, u32[]{:S(2)}) collective-permute-start(bf16[16,3072]{1,0:T(8,128)(2,1)S(1)} %get-tuple-element.55), channel_id=1, source_target_pairs={{0,8},{4,12},{8,0},{12,4},{16,24},{20,28},{24,16},{28,20},{1,9},{5... | collective-permute-start | bytes 294920 | tf_op jit(solution)/shard_map/ppermute | solution.py:22
  18.8 0.0 collective-permute-start.9
  18.9 1.7 %collective-permute-start.10 = (bf16[16,3072]{1,0:T(8,128)(2,1)S(1)}, bf16[16,3072]{1,0:T(8,128)(2,1)S(1)}, u32[]{:S(2)}, u32[]{:S(2)}) collective-permute-start(bf16[16,3072]{1,0:T(8,128)(2,1)S(1)} %get-tuple-element.57), channel_id=1, source_target_pairs={{0,16},{4,20},{8,24},{12,28},{16,0},{20,4},{24,8},{28,12},{1,17},{... | collective-permute-start | bytes 294920 | tf_op jit(solution)/shard_map/ppermute | solution.py:22
  20.6 0.0 collective-permute-done.4.refs_2_
  20.6 0.1 collective-permute-start.11
  20.7 0.3 mix.1
  21.1 0.6 %collective-permute-done.5.refs_3_ = bf16[16,3072]{1,0:T(8,128)(2,1)S(1)} collective-permute-done((bf16[16,3072]{1,0:T(8,128)(2,1)S(1)}, bf16[16,3072]{1,0:T(8,128)(2,1)S(1)}, u32[]{:S(2)}, u32[]{:S(2)}) %collective-permute-start.5) | collective-permute-done | bytes 98336 | tf_op jit(solution)/shard_map/ppermute | solution.py:22
  21.7 0.2 begin.1.begun_ref
  21.9 2.4 %collective-permute-done.8.refs_0_ = bf16[16,3072]{1,0:T(8,128)(2,1)S(1)} collective-permute-done((bf16[16,3072]{1,0:T(8,128)(2,1)S(1)}, bf16[16,3072]{1,0:T(8,128)(2,1)S(1)}, u32[]{:S(2)}, u32[]{:S(2)}) %collective-permute-start.8) | collective-permute-done | bytes 98336 | tf_op jit(solution)/shard_map/ppermute | solution.py:22
  24.3 1.2 %collective-permute-done.9.refs_1_ = bf16[16,3072]{1,0:T(8,128)(2,1)S(1)} collective-permute-done((bf16[16,3072]{1,0:T(8,128)(2,1)S(1)}, bf16[16,3072]{1,0:T(8,128)(2,1)S(1)}, u32[]{:S(2)}, u32[]{:S(2)}) %collective-permute-start.9) | collective-permute-done | bytes 98336 | tf_op jit(solution)/shard_map/ppermute | solution.py:22
  25.5 0.5 %collective-permute-done.11.refs_3_ = bf16[16,3072]{1,0:T(8,128)(2,1)S(1)} collective-permute-done((bf16[16,3072]{1,0:T(8,128)(2,1)S(1)}, bf16[16,3072]{1,0:T(8,128)(2,1)S(1)}, u32[]{:S(2)}, u32[]{:S(2)}) %collective-permute-start.11) | collective-permute-done | bytes 98336 | tf_op jit(solution)/shard_map/ppermute | solution.py:22
  26.0 0.3 close.1
  26.3 3.7 %collective-permute-start.12 = (bf16[32,768]{1,0:T(8,128)(2,1)S(1)}, bf16[32,768]{1,0:T(8,128)(2,1)S(1)}, u32[]{:S(2)}, u32[]{:S(2)}) collective-permute-start(bf16[32,768]{1,0:T(8,128)(2,1)S(1)} %get-tuple-element.60), channel_id=1, source_target_pairs={{0,3},{1,2},{2,1},{3,0},{4,7},{5,6},{6,5},{7,4},{8,11},{9,10},{10,... | collective-permute-start | bytes 147464 | tf_op jit(solution)/shard_map/ppermute | solution.py:22
  30.1 0.7 %collective-permute-start.14 = (bf16[32,768]{1,0:T(8,128)(2,1)S(1)}, bf16[32,768]{1,0:T(8,128)(2,1)S(1)}, u32[]{:S(2)}, u32[]{:S(2)}) collective-permute-start(bf16[32,768]{1,0:T(8,128)(2,1)S(1)} %get-tuple-element.62), channel_id=1, source_target_pairs={{0,1},{1,0},{2,3},{3,2},{4,5},{5,4},{6,7},{7,6},{8,9},{9,8},{10,11... | collective-permute-start | bytes 147464 | tf_op jit(solution)/shard_map/ppermute | solution.py:22
  30.8 1.6 %collective-permute-done.12.refs_1_ = bf16[32,768]{1,0:T(8,128)(2,1)S(1)} collective-permute-done((bf16[32,768]{1,0:T(8,128)(2,1)S(1)}, bf16[32,768]{1,0:T(8,128)(2,1)S(1)}, u32[]{:S(2)}, u32[]{:S(2)}) %collective-permute-start.12) | collective-permute-done | bytes 49184 | tf_op jit(solution)/shard_map/ppermute | solution.py:22
  32.3 2.7 %collective-permute-done.13.refs_2_ = bf16[32,768]{1,0:T(8,128)(2,1)S(1)} collective-permute-done((bf16[32,768]{1,0:T(8,128)(2,1)S(1)}, bf16[32,768]{1,0:T(8,128)(2,1)S(1)}, u32[]{:S(2)}, u32[]{:S(2)}) %collective-permute-start.13) | collective-permute-done | bytes 49184 | tf_op jit(solution)/shard_map/ppermute | solution.py:22
  35.1 0.6 %finish.1 = bf16[2,16,768]{2,1,0:T(8,128)(2,1)} custom-call(f32[32,768]{1,0:T(8,128)S(1)} %get-tuple-element.59.refs_0_, bf16[32,768]{1,0:T(8,128)(2,1)S(1)} %collective-permute-done.12.refs_1_, bf16[32,768]{1,0:T(8,128)(2,1)S(1)} %collective-permute-done.13.refs_2_, bf16[32,768]{1,0:T(8,128)(2,1)S(1)} %collective-permute-done.14.refs_3_), custom_call_target="tpu_custom_call" | custom-call | tf_op jit(solution)/shard_map/finish/pallas_call | solution.py:337
  (7 shorter events, 0.0 us)
Async XLA Ops:
  0.0 1.8 %collective-permute-start = (bf16[32,3072]{1,0:T(8,128)(2,1)}, bf16[32,3072]{1,0:T(8,128)(2,1)S(1)}, u32[]{:S(2)}, u32[]{:S(2)}) collective-permute-start(bf16[32,3072]{1,0:T(8,128)(2,1)} %bitcast.10), channel_id=1, source_target_pairs={{0,4},{4,0},{8,12},{12,8},{16,20},{20,16},{24,28},{28,24},{1,5},{5... | collective-permute-start | bytes 589832 | tf_op jit(solution)/shard_map/ppermute | solution.py:22
  0.5 1.4 %collective-permute-start.1 = (s32[2,2,16]{2,1,0:T(2,128)}, s32[2,2,16]{2,1,0:T(2,128)S(1)}, u32[]{:S(2)}, u32[]{:S(2)}) collective-permute-start(s32[2,2,16]{2,1,0:T(2,128)} %bitcast.14), channel_id=1, source_target_pairs={{0,4},{4,0},{8,12},{12,8},{16,20},{20,16},{24,28},{28,24},{1,5},{5... | collective-permute-start | bytes 776 | tf_op jit(solution)/shard_map/ppermute | solution.py:22
  2.4 9.5 %collective-permute-start.2 = (bf16[32,3072]{1,0:T(8,128)(2,1)S(1)}, bf16[32,3072]{1,0:T(8,128)(2,1)S(1)}, u32[]{:S(2)}, u32[]{:S(2)}) collective-permute-start(bf16[32,3072]{1,0:T(8,128)(2,1)S(1)} %get-tuple-element.48), channel_id=1, source_target_pairs={{0,24},{4,28},{8,16},{12,20},{16,8},{20,12},{24,0},{28,4},{1,25},{... | collective-permute-start | bytes 589832 | tf_op jit(solution)/shard_map/ppermute | solution.py:22
  6.2 9.9 %collective-permute-start.6 = (bf16[32,3072]{1,0:T(8,128)(2,1)S(1)}, bf16[32,3072]{1,0:T(8,128)(2,1)S(1)}, u32[]{:S(2)}, u32[]{:S(2)}) collective-permute-start(bf16[32,3072]{1,0:T(8,128)(2,1)S(1)} %get-tuple-element.53), channel_id=1, source_target_pairs={{0,8},{4,12},{8,0},{12,4},{16,24},{20,28},{24,16},{28,20},{1,9},{5... | collective-permute-start | bytes 589832 | tf_op jit(solution)/shard_map/ppermute | solution.py:22
  6.7 9.4 %collective-permute-start.7 = (bf16[32,3072]{1,0:T(8,128)(2,1)S(1)}, bf16[32,3072]{1,0:T(8,128)(2,1)S(1)}, u32[]{:S(2)}, u32[]{:S(2)}) collective-permute-start(bf16[32,3072]{1,0:T(8,128)(2,1)S(1)} %get-tuple-element.54), channel_id=1, source_target_pairs={{0,16},{4,20},{8,24},{12,28},{16,0},{20,4},{24,8},{28,12},{1,17},{... | collective-permute-start | bytes 589832 | tf_op jit(solution)/shard_map/ppermute | solution.py:22
  12.9 6.0 %collective-permute-start.3 = (bf16[16,3072]{1,0:T(8,128)(2,1)S(1)}, bf16[16,3072]{1,0:T(8,128)(2,1)S(1)}, u32[]{:S(2)}, u32[]{:S(2)}) collective-permute-start(bf16[16,3072]{1,0:T(8,128)(2,1)S(1)} %get-tuple-element.50), channel_id=1, source_target_pairs={{0,4},{4,0},{8,12},{12,8},{16,20},{20,16},{24,28},{28,24},{1,5},{5... | collective-permute-start | bytes 294920 | tf_op jit(solution)/shard_map/ppermute | solution.py:22
  13.0 7.6 %collective-permute-start.4 = (bf16[16,3072]{1,0:T(8,128)(2,1)S(1)}, bf16[16,3072]{1,0:T(8,128)(2,1)S(1)}, u32[]{:S(2)}, u32[]{:S(2)}) collective-permute-start(bf16[16,3072]{1,0:T(8,128)(2,1)S(1)} %get-tuple-element.51), channel_id=1, source_target_pairs={{0,24},{4,28},{8,16},{12,20},{16,8},{20,12},{24,0},{28,4},{1,25},{... | collective-permute-start | bytes 294920 | tf_op jit(solution)/shard_map/ppermute | solution.py:22
  16.0 5.6 %collective-permute-start.5 = (bf16[16,3072]{1,0:T(8,128)(2,1)S(1)}, bf16[16,3072]{1,0:T(8,128)(2,1)S(1)}, u32[]{:S(2)}, u32[]{:S(2)}) collective-permute-start(bf16[16,3072]{1,0:T(8,128)(2,1)S(1)} %get-tuple-element.52), channel_id=1, source_target_pairs={{0,28},{4,24},{8,20},{12,16},{16,12},{20,8},{24,4},{28,0},{1,29},{... | collective-permute-start | bytes 294920 | tf_op jit(solution)/shard_map/ppermute | solution.py:22
  17.1 7.2 %collective-permute-start.8 = (bf16[16,3072]{1,0:T(8,128)(2,1)S(1)}, bf16[16,3072]{1,0:T(8,128)(2,1)S(1)}, u32[]{:S(2)}, u32[]{:S(2)}) collective-permute-start(bf16[16,3072]{1,0:T(8,128)(2,1)S(1)} %get-tuple-element.55), channel_id=1, source_target_pairs={{0,8},{4,12},{8,0},{12,4},{16,24},{20,28},{24,16},{28,20},{1,9},{5... | collective-permute-start | bytes 294920 | tf_op jit(solution)/shard_map/ppermute | solution.py:22
  18.8 6.7 %collective-permute-start.9 = (bf16[16,3072]{1,0:T(8,128)(2,1)S(1)}, bf16[16,3072]{1,0:T(8,128)(2,1)S(1)}, u32[]{:S(2)}, u32[]{:S(2)}) collective-permute-start(bf16[16,3072]{1,0:T(8,128)(2,1)S(1)} %get-tuple-element.56), channel_id=1, source_target_pairs={{0,12},{4,8},{8,4},{12,0},{16,28},{20,24},{24,20},{28,16},{1,13},{... | collective-permute-start | bytes 294920 | tf_op jit(solution)/shard_map/ppermute | solution.py:22
  18.9 6.6 %collective-permute-start.10 = (bf16[16,3072]{1,0:T(8,128)(2,1)S(1)}, bf16[16,3072]{1,0:T(8,128)(2,1)S(1)}, u32[]{:S(2)}, u32[]{:S(2)}) collective-permute-start(bf16[16,3072]{1,0:T(8,128)(2,1)S(1)} %get-tuple-element.57), channel_id=1, source_target_pairs={{0,16},{4,20},{8,24},{12,28},{16,0},{20,4},{24,8},{28,12},{1,17},{... | collective-permute-start | bytes 294920 | tf_op jit(solution)/shard_map/ppermute | solution.py:22
  20.6 5.4 %collective-permute-start.11 = (bf16[16,3072]{1,0:T(8,128)(2,1)S(1)}, bf16[16,3072]{1,0:T(8,128)(2,1)S(1)}, u32[]{:S(2)}, u32[]{:S(2)}) collective-permute-start(bf16[16,3072]{1,0:T(8,128)(2,1)S(1)} %get-tuple-element.58), channel_id=1, source_target_pairs={{0,20},{4,16},{8,28},{12,24},{16,4},{20,0},{24,12},{28,8},{1,21},{... | collective-permute-start | bytes 294920 | tf_op jit(solution)/shard_map/ppermute | solution.py:22
  26.3 6.0 %collective-permute-start.12 = (bf16[32,768]{1,0:T(8,128)(2,1)S(1)}, bf16[32,768]{1,0:T(8,128)(2,1)S(1)}, u32[]{:S(2)}, u32[]{:S(2)}) collective-permute-start(bf16[32,768]{1,0:T(8,128)(2,1)S(1)} %get-tuple-element.60), channel_id=1, source_target_pairs={{0,3},{1,2},{2,1},{3,0},{4,7},{5,6},{6,5},{7,4},{8,11},{9,10},{10,... | collective-permute-start | bytes 147464 | tf_op jit(solution)/shard_map/ppermute | solution.py:22
  30.1 5.0 %collective-permute-start.13 = (bf16[32,768]{1,0:T(8,128)(2,1)S(1)}, bf16[32,768]{1,0:T(8,128)(2,1)S(1)}, u32[]{:S(2)}, u32[]{:S(2)}) collective-permute-start(bf16[32,768]{1,0:T(8,128)(2,1)S(1)} %get-tuple-element.61), channel_id=1, source_target_pairs={{0,2},{1,3},{2,0},{3,1},{4,6},{5,7},{6,4},{7,5},{8,10},{9,11},{10,... | collective-permute-start | bytes 147464 | tf_op jit(solution)/shard_map/ppermute | solution.py:22
  30.1 5.0 %collective-permute-start.14 = (bf16[32,768]{1,0:T(8,128)(2,1)S(1)}, bf16[32,768]{1,0:T(8,128)(2,1)S(1)}, u32[]{:S(2)}, u32[]{:S(2)}) collective-permute-start(bf16[32,768]{1,0:T(8,128)(2,1)S(1)} %get-tuple-element.62), channel_id=1, source_target_pairs={{0,1},{1,0},{2,3},{3,2},{4,5},{5,4},{6,7},{7,6},{8,9},{9,8},{10,11... | collective-permute-start | bytes 147464 | tf_op jit(solution)/shard_map/ppermute | solution.py:22

commit v4 on v3

--- a/solution.py
+++ b/solution.py
@@ -22,79 +22,140 @@
     return lax.ppermute(value, axis, [(place, place ^ distance) for place in range(count)])
 
 
+def visit(value, step, cross):
+    count = lax.axis_size("section")
+    pairs = [(place, place ^ (2 * step[place % 2]) ^ cross) for place in range(count)]
+    return lax.ppermute(value, "section", pairs)
+
+
 def shaped(rows, width, dtype):
     return jax.ShapeDtypeStruct((rows, width), dtype)
 
 
-def expert_at(section, distance, per_expert):
-    return lax.div(section ^ distance, jnp.int32(per_expert))
-
-
-def pack_kernel(chips, per_expert, experts, section_ref, tokens_ref, other_ref, named_ref, other_named_ref, gain_ref, *refs):
-    out_refs, normed_ref, slots_ref, named_rows_ref = refs[:chips], refs[chips], refs[chips + 1], refs[chips + 2]
-    micro, _, row_count = named_ref.shape
-    rows = tokens_ref.shape[0]
-    for place, ref in enumerate((tokens_ref, other_ref)):
-        values = ref[...].astype(jnp.float32)
-        inv_rms = lax.rsqrt(jnp.mean(values * values, axis=-1, keepdims=True) + epsilon)
-        normed_ref[place * rows : (place + 1) * rows, :] = (
-            values * inv_rms * gain_ref[...]
-        ).astype(jnp.bfloat16)
-    named = [
-        jnp.concatenate(
-            [ref[m, k : k + 1, :] for ref in (named_ref, other_named_ref) for m in range(micro)],
-            axis=1,
-        ).astype(jnp.float32)
-        for k in range(2)
-    ]
-    every = 2 * rows
-    capacity = row_count // 2
-    ids = lax.broadcasted_iota(jnp.int32, (experts, every), 0).astype(jnp.float32)
+def expert_at(section, distances, per_expert):
+    distance = jnp.where(section % 2 == 0, distances[0], distances[1])
+    return lax.div(section ^ distance, jnp.int32(per_expert)).astype(jnp.float32)
+
+
+def slots_of(named, experts, row_count):
+    rows = named[0].shape[1]
+    ids = lax.broadcasted_iota(jnp.int32, (experts, rows), 0).astype(jnp.float32)
     hit = (named[0] == ids) | (named[1] == ids)
-    above = lax.broadcasted_iota(jnp.int32, (every, every), 0)
-    column = lax.broadcasted_iota(jnp.int32, (every, every), 1)
+    above = lax.broadcasted_iota(jnp.int32, (rows, rows), 0)
+    column = lax.broadcasted_iota(jnp.int32, (rows, rows), 1)
     earlier = (above < column) & (above // row_count == column // row_count)
     rank = jnp.dot(
         hit.astype(jnp.bfloat16), earlier.astype(jnp.bfloat16), preferred_element_type=jnp.float32
     )
-    group = lax.broadcasted_iota(jnp.int32, (experts, every), 1) // row_count
-    slots = jnp.where(hit, (group * capacity).astype(jnp.float32) + rank, -1.0)
-    slots_ref[...] = slots
-    named_rows_ref[0:1, :] = named[0]
-    named_rows_ref[1:2, :] = named[1]
-    section = section_ref[0]
-    slot_ids = lax.broadcasted_iota(jnp.int32, (rows, every), 0).astype(jnp.float32)
+    group = lax.broadcasted_iota(jnp.int32, (experts, rows), 1) // row_count
+    return jnp.where(hit, (group * (row_count // 2)).astype(jnp.float32) + rank, -1.0)
+
+
+def picked(section, slots, normed, steps, per_expert):
+    experts, rows = slots.shape
+    ids = lax.broadcasted_iota(jnp.int32, (experts, rows), 0).astype(jnp.float32)
+    slot_ids = lax.broadcasted_iota(jnp.int32, (rows // 2, rows), 0).astype(jnp.float32)
     picks = []
-    for k in range(chips):
-        expert = expert_at(section, 2 * k, per_expert).astype(jnp.float32)
+    for step in steps:
+        expert = expert_at(section, (2 * step[0], 2 * step[1]), per_expert)
         slot = jnp.sum(jnp.where(ids == expert, slots, 0.0), axis=0, keepdims=True)
         picks.append(jnp.where(slot == slot_ids, 1.0, 0.0))
     pick = jnp.concatenate(picks, axis=0).astype(jnp.bfloat16)
-    packed = jnp.dot(pick, normed_ref[...], preferred_element_type=jnp.float32)
-    for k, out_ref in enumerate(out_refs):
-        out_ref[...] = packed[k * rows : (k + 1) * rows, :].astype(jnp.bfloat16)
-
-
-def pack(section, tokens, other, named, other_named, gain, chips, per_expert, experts):
+    return jnp.dot(pick, normed, preferred_element_type=jnp.float32).astype(jnp.bfloat16)
+
+
+def normed_of(values, gain):
+    values = values.astype(jnp.float32)
+    inv_rms = lax.rsqrt(jnp.mean(values * values, axis=-1, keepdims=True) + epsilon)
+    return (values * inv_rms * gain).astype(jnp.bfloat16)
+
+
+def named_of(ref):
+    micro = ref.shape[0]
+    return [
+        jnp.concatenate([ref[m, k : k + 1, :] for m in range(micro)], axis=1).astype(jnp.float32)
+        for k in range(2)
+    ]
+
+
+def own_kernel(steps, per_expert, section_ref, tokens_ref, named_ref, gain_ref, *refs):
+    half_refs, refs = refs[: len(steps)], refs[len(steps) :]
+    own_ref, gain_out_ref, normed_ref, slots_ref, names_ref, held_ref, sems = refs
+    copies = [
+        pltpu.make_async_copy(source, target, sems.at[k])
+        for k, (source, target) in enumerate(
+            [(named_ref, held_ref), (gain_ref, gain_out_ref), (tokens_ref, own_ref)]
+        )
+    ]
+    for copy in copies:
+        copy.start()
+    copies[0].wait()
+    named = named_of(held_ref)
+    slots = slots_of(named, slots_ref.shape[0], named_ref.shape[2])
+    slots_ref[...] = slots
+    names_ref[0:1, :] = named[0]
+    names_ref[1:2, :] = named[1]
+    copies[1].wait()
+    copies[2].wait()
+    normed = normed_of(own_ref[...], gain_out_ref[...])
+    normed_ref[...] = normed
+    packed = picked(section_ref[0], slots, normed, steps, per_expert)
+    each = packed.shape[0] // len(steps)
+    for place, half_ref in enumerate(half_refs):
+        half_ref[...] = packed[place * each : (place + 1) * each, :]
+
+
+def own_part(section, tokens, named, gain, steps, per_expert, experts):
     rows, width = tokens.shape
-    return pl.pallas_call(
-        functools.partial(pack_kernel, chips, per_expert, experts),
-        out_shape=[shaped(rows, width, jnp.bfloat16)] * chips
-        + [
-            shaped(2 * rows, width, jnp.bfloat16),
-            shaped(experts, 2 * rows, jnp.float32),
-            shaped(2, 2 * rows, jnp.float32),
-        ],
-        in_specs=[SMEM] + [VMEM] * 5,
-        out_specs=[VMEM] * (chips + 3),
-        compiler_params=PARAMS,
-        name="pack",
-    )(section, tokens, other, named, other_named, gain)
+    arrays = [pltpu.with_memory_space_constraint(a, pltpu.HBM) for a in (tokens, named, gain)]
+    shapes = [shaped(rows // 2, width, jnp.bfloat16)] * len(steps) + [
+        shaped(rows, width, jnp.bfloat16),
+        shaped(1, width, jnp.float32),
+        shaped(rows, width, jnp.bfloat16),
+        shaped(experts, rows, jnp.float32),
+        shaped(2, rows, jnp.float32),
+    ]
+    return pl.pallas_call(
+        functools.partial(own_kernel, steps, per_expert),
+        out_shape=shapes,
+        in_specs=[SMEM] + [HBM] * 3,
+        out_specs=[VMEM] * len(shapes),
+        scratch_shapes=[pltpu.VMEM(named.shape, jnp.int32), pltpu.SemaphoreType.DMA((3,))],
+        compiler_params=PARAMS,
+        name="own_part",
+    )(section, *arrays)
+
+
+def other_kernel(steps, per_expert, section_ref, other_ref, named_ref, gain_ref, *refs):
+    count = len(steps)
+    half_refs, out_refs, normed_ref, slots_ref = refs[:count], refs[count:-2], refs[-2], refs[-1]
+    slots = slots_of(named_of(named_ref), slots_ref.shape[0], named_ref.shape[2])
+    slots_ref[...] = slots
+    normed = normed_of(other_ref[...], gain_ref[...])
+    normed_ref[...] = normed
+    packed = picked(section_ref[0], slots, normed, steps, per_expert)
+    each = packed.shape[0] // count
+    for place, (half_ref, out_ref) in enumerate(zip(half_refs, out_refs)):
+        out_ref[:each, :] = half_ref[...]
+        out_ref[each:, :] = packed[place * each : (place + 1) * each, :]
+
+
+def other_part(section, other, named, gain, halves, steps, per_expert, experts):
+    rows, width = other.shape
+    shapes = [shaped(rows, width, jnp.bfloat16)] * (len(steps) + 1)
+    shapes.append(shaped(experts, rows, jnp.float32))
+    return pl.pallas_call(
+        functools.partial(other_kernel, steps, per_expert),
+        out_shape=shapes,
+        in_specs=[SMEM] + [VMEM] * (3 + len(halves)),
+        out_specs=[VMEM] * len(shapes),
+        compiler_params=PARAMS,
+        name="other_part",
+    )(section, other, named, gain, *halves)
 
 
 def mix_kernel(sets, per_expert, section_ref, normed_ref, slots_ref, named_ref, router_ref, *outs):
     experts, every = slots_ref.shape
-    rows = every // 2
     logits = lax.dot_general(
         normed_ref[...], router_ref[...], NT, preferred_element_type=jnp.float32
     )
@@ -120,13 +181,13 @@
         lanes = lax.broadcasted_iota(jnp.int32, (count, width), 1).astype(jnp.float32)
         spread = jnp.zeros((count, width), jnp.float32)
         for at, distance in enumerate(distances):
-            expert = expert_at(section, distance, per_expert).astype(jnp.float32)
+            expert = expert_at(section, distance, per_expert)
             slot = jnp.sum(jnp.where(tall == expert, slots_ref[...], 0.0), axis=0, keepdims=True)
             weight = jnp.where(first == expert, weight_a, 0.0) + jnp.where(
                 second == expert, weight_b, 0.0
             )
             spread = spread + jnp.where(
-                upright(slot)[:count] + at * each == lanes, weight[:count], 0.0
+                upright(slot) + at * each == lanes, weight, 0.0
             )
         high = spread.astype(jnp.bfloat16)
         high_ref[...] = high
@@ -134,8 +195,7 @@
 
 
 def mix(section, normed, slots, named, router, early, near, per_expert):
-    every = normed.shape[0]
-    rows = every // 2
+    rows = normed.shape[0]
     shapes = [
         shaped(rows, len(distances) * rows // 2, jnp.bfloat16)
         for distances in (early, near)
@@ -151,34 +211,11 @@
     )(section, normed, slots, named, router)
 
 
-def fetch_kernel(count, *refs):
-    sources, targets, sems = refs[:count], refs[-1 - count : -1], refs[-1]
-    copies = [
-        pltpu.make_async_copy(source, target, sems.at[k])
-        for k, (source, target) in enumerate(zip(sources, targets))
-    ]
-    for copy in copies:
-        copy.start()
-    for copy in copies:
-        copy.wait()
-
-
-def fetch(arrays, after=()):
-    count = len(arrays)
-    return pl.pallas_call(
-        functools.partial(fetch_kernel, count),
-        out_shape=[jax.ShapeDtypeStruct(a.shape, a.dtype) for a in arrays],
-        in_specs=[HBM] * count + [VMEM] * len(after),
-        out_specs=[VMEM] * count,
-        scratch_shapes=[pltpu.SemaphoreType.DMA((count,))],
-        compiler_params=PARAMS,
-        name="fetch",
-    )(*[pltpu.with_memory_space_constraint(a, pltpu.HBM) for a in arrays], *after)
-
-
-def load_kernel(count, in_ref, *refs):
-    sources, targets = refs[:count], refs[count + 2 : 2 * count + 2]
-    turned_ref, held_ref, sems = refs[count + 1], refs[-2], refs[-1]
+def load_kernel(count, steps, per_expert, section_ref, in_ref, *refs):
+    sources, refs = refs[:count], refs[count:]
+    normed_refs, slots_refs, refs = refs[:2], refs[2:4], refs[4:]
+    turned_ref, targets, out_refs = refs[0], refs[1 : 1 + count], refs[1 + count : -2]
+    held_ref, sems = refs[-2:]
     pieces, rows, _ = held_ref.shape
     copies = [
         pltpu.make_async_copy(in_ref.at[pl.ds(k * rows, rows)], held_ref.at[k], sems.at[k])
@@ -190,6 +227,13 @@
     ]
     for copy in copies + others:
         copy.start()
+    for part, (normed_ref, slots_ref) in enumerate(zip(normed_refs, slots_refs)):
+        packed = picked(section_ref[0], slots_ref[...], normed_ref[...], steps, per_expert)
+        each = packed.shape[0] // len(steps)
+        for place, out_ref in enumerate(out_refs):
+            out_ref[part * each : (part + 1) * each, :] = packed[
+                place * each : (place + 1) * each, :
+            ]
     for k in range(pieces):
         copies[k].wait()
         turned_ref[:, k * rows : (k + 1) * rows] = held_ref[k].T
@@ -197,24 +241,26 @@
         copy.wait()
 
 
-def load_weights(stacked_in, others, after):
+def load_weights(section, stacked_in, others, normed, slots, steps, per_expert):
     count = len(others)
     rows, width = stacked_in.shape
     pieces = max(1, rows // LANES)
-    arrays = [stacked_in, *others]
-    return pl.pallas_call(
-        functools.partial(load_kernel, count),
-        out_shape=[shaped(width, rows, stacked_in.dtype)]
-        + [jax.ShapeDtypeStruct(a.shape, a.dtype) for a in others],
-        in_specs=[HBM] * (count + 1) + [VMEM],
-        out_specs=[VMEM] * (count + 1),
+    arrays = [pltpu.with_memory_space_constraint(a, pltpu.HBM) for a in (stacked_in, *others)]
+    shapes = [shaped(width, rows, stacked_in.dtype)]
+    shapes += [jax.ShapeDtypeStruct(a.shape, a.dtype) for a in others]
+    shapes += [shaped(normed[0].shape[0], width, jnp.bfloat16)] * len(steps)
+    return pl.pallas_call(
+        functools.partial(load_kernel, count, steps, per_expert),
+        out_shape=shapes,
+        in_specs=[SMEM] + [HBM] * (count + 1) + [VMEM] * 4,
+        out_specs=[VMEM] * len(shapes),
         scratch_shapes=[
             pltpu.VMEM((pieces, rows // pieces, width), stacked_in.dtype),
             pltpu.SemaphoreType.DMA((pieces + count,)),
         ],
         compiler_params=PARAMS,
         name="load_weights",
-    )(*[pltpu.with_memory_space_constraint(a, pltpu.HBM) for a in arrays], after)
+    )(section, *arrays, *normed, *slots)
 
 
 def expert_kernel(count, after, in_ref, down_ref, *refs):
@@ -359,38 +405,47 @@
     named = choices.transpose(0, 2, 1)
     gain = norm_gain.reshape(1, width)
 
+    far = chips - 1
+    first_steps = ((0, 0), (far, far))
+    steps = []
+    for k in range(1, far, 2):
+        steps += [(k, k + 1), (k + 1, k)]
+
     other = trade(own, "section", 1)
     other_named = trade(named, "section", 1)
-    own, named, gain = fetch((own, named, gain))
-    *messages, normed, slots, names = pack(
-        section, own, other, named, other_named, gain, chips, per_expert, experts
-    )
-    order = list(range(1, chips))
-    arrived = {k: trade(messages[k], "section", 2 * k) for k in reversed(order)}
-    turned_in, router_rows, down = load_weights(
-        expert_in[0].reshape(2 * hidden, width), (router.T, expert_out[0]), slots
-    )
-    far, near = order[-1], order[:-1]
-    early = (0, 1, 2 * far, 2 * far + 1)
-    late = tuple(distance for k in near for distance in (2 * k, 2 * k + 1))
+    *halves, own, gain, normed, slots, names = own_part(
+        section, own, named, gain, first_steps, per_expert, experts
+    )
+    message, away, other_normed, other_slots = other_part(
+        section, other, other_named, gain, halves, first_steps, per_expert, experts
+    )
+    away = visit(away, (far, far), 0)
+    turned_in, router_rows, down, *messages = load_weights(
+        section,
+        expert_in[0].reshape(2 * hidden, width),
+        (router.T, expert_out[0]),
+        (normed, other_normed),
+        (slots, other_slots),
+        tuple(steps),
+        per_expert,
+    )
+    arrived = [visit(value, step, 0) for value, step in zip(messages, steps)]
+
+    def origins(step):
+        a, b = step
+        return ((2 * a, 2 * b), (2 * b + 1, 2 * a + 1))
+
+    early = origins((0, 0)) + origins((far, far))
+    late = tuple(pair for step in steps for pair in origins(step))
     high_a, low_a, high_b, low_b = mix(
         section, normed, slots, names, router_rows, early, late, per_expert
     )
-
-    def come_back(blocks, distances):
-        return [
-            trade(block, "section", distance) if distance else block
-            for block, distance in zip(blocks, distances)
-        ]
-
-    early_blocks = run_expert([messages[0], arrived[far]], turned_in, down, 2)
-    late_blocks = run_expert(
-        [arrived[k] for k in near], turned_in, down, 2, (early_blocks[0],)
-    )
-    begun = begin(high_a, low_a, come_back(early_blocks, early))
-    split = close(
-        high_b, low_b, begun, come_back(late_blocks, late), own, member, inner_count
-    )
+    here, beside, *away = run_expert([message, away], turned_in, down, 2)
+    results = run_expert(arrived, turned_in, down, 2, (here,))
+    away = [visit(value, (far, far), cross) for cross, value in enumerate(away)]
+    begun = begin(high_a, low_a, [here, trade(beside, "section", 1), *away])
+    results = [visit(value, steps[j // 2], j % 2) for j, value in enumerate(results)]
+    split = close(high_b, low_b, begun, results, own, member, inner_count)
     pieces = {k: trade(split[k], "inner", k) for k in reversed(range(1, inner_count))}
     pieces[0] = split[0]
     return finish([pieces[k] for k in [0] + list(reversed(range(1, inner_count)))], micro, row_count)

time: 35.9 us -> 35.2 us (0.981)
  waiting for transfers between devices: 12 us -> 10.6 us
  starting transfers between devices: 16.1 us -> 16.7 us
    ppermute x0 -> x9, starting transfers between devices: none -> 11.7 us  [visit(): return lax.ppermute(value, 'section', pairs)]
    ppermute x15 -> x6, starting transfers between devices: 16.1 us -> 5.06 us  [trade(): lax.ppermute(value, axis, [(place, place ^ distance) for place in range(c...]
    ppermute x15 -> x6, waiting for transfers between devices: 12 us -> 4.43 us  [trade(): lax.ppermute(value, axis, [(place, place ^ distance) for place in range(c...]
    ppermute x0 -> x9, waiting for transfers between devices: none -> 6.13 us  [visit(): return lax.ppermute(value, 'section', pairs)]
  transfers between devices with their start and end apart: 15 -> 15, of which waited for: 8 -> 7; matrix products, arithmetic and copies ran while one was open for 0% -> 0% of each run, Pallas kernels for 17% -> 18%
where the time goes in v4:
time: 35.2 us; the launch traced here: 35.1 us
  starting transfers between devices  16.7 us (47%)
  waiting for transfers between devices  10.6 us (30%)
  Pallas kernels  7.68 us (22%)
    ppermute x9, starting transfers between devices, visit(): return lax.ppermute(value, 'section', pairs)  11.7 us
    ppermute x9, waiting for transfers between devices, visit(): return lax.ppermute(value, 'section', pairs)  6.13 us
    ppermute x6, starting transfers between devices, trade(): lax.ppermute(value, axis, [(place, place ^ distance) for place in range(c...  5.06 us
    ppermute x6, waiting for transfers between devices, trade(): lax.ppermute(value, axis, [(place, place ^ distance) for place in range(c...  4.43 us
    pallas_call x1, Pallas kernels, load_weights(): pl.pallas_call(functools.partial(load_kernel, count, steps, per_expert),...  2.46 us
    pallas_call x2, Pallas kernels, run_expert(): pl.pallas_call(functools.partial(expert_kernel, count, len(after)), out_s...  2.05 us
    pallas_call x1, Pallas kernels, own_part(): pl.pallas_call(functools.partial(own_kernel, steps, per_expert), out_shap...  1.31 us
  transfers between devices with their start and end apart: 15, of which 7 were waited for; matrix products, arithmetic and copies ran while one was open for 0% of the time, Pallas kernels for 18%

profile of v4, /device:TPU:0, one launch (start us, length us, event | category | flops | bytes accessed | tf_op | source)
XLA Modules:
  0.0 35.1 jit_solution(1512839253288113972)
XLA Ops:
  0.0 0.5 %collective-permute-start = (bf16[32,3072]{1,0:T(8,128)(2,1)}, bf16[32,3072]{1,0:T(8,128)(2,1)S(1)}, u32[]{:S(2)}, u32[]{:S(2)}) collective-permute-start(bf16[32,3072]{1,0:T(8,128)(2,1)} %bitcast.10), channel_id=1, source_target_pairs={{0,4},{4,0},{8,12},{12,8},{16,20},{20,16},{24,28},{28,24},{1,5},{5... | collective-permute-start | bytes 589832 | tf_op jit(solution)/shard_map/ppermute | solution.py:22
  0.5 0.1 collective-permute-start.1
  0.5 1.3 %own_part.1 = (bf16[16,3072]{1,0:T(8,128)(2,1)S(1)}, bf16[16,3072]{1,0:T(8,128)(2,1)S(1)}, bf16[32,3072]{1,0:T(8,128)(2,1)S(1)}, f32[1,3072]{1,0:T(1,128)S(1)}, ...) custom-call(s32[1]{0:T(128)} %bitcast.1.section_ref, bf16[32,3072]{1,0:T(8,128)(2,1)} %bitcast.11, ...), custom_call_target="tpu_custom_call" | custom-call | tf_op jit(solution)/shard_map/own_part/pallas_call | solution.py:118
  1.9 0.4 %other_part.1 = (bf16[32,3072]{1,0:T(8,128)(2,1)S(1)}, bf16[32,3072]{1,0:T(8,128)(2,1)S(1)}, bf16[32,3072]{1,0:T(8,128)(2,1)S(1)}, f32[8,32]{1,0:T(8,128)S(1)}) custom-call(s32[1]{0:T(128)} %bitcast.1.section_ref, bf16[32,3072]{1,0:T(8,128)(2,1)S(1)} %collective-permute-done.other_ref, s32[2,2,16]{2,1,0:T(2,128)S(1)} %collective-permute-done.1.named_ref, ...), custom_call_target="tpu_custom_call" | custom-call | tf_op jit(solution)/shard_map/other_part/pallas_call | solution.py:147
  2.2 4.0 %collective-permute-start.2 = (bf16[32,3072]{1,0:T(8,128)(2,1)S(1)}, bf16[32,3072]{1,0:T(8,128)(2,1)S(1)}, u32[]{:S(2)}, u32[]{:S(2)}) collective-permute-start(bf16[32,3072]{1,0:T(8,128)(2,1)S(1)} %get-tuple-element.54), channel_id=1, source_target_pairs={{0,24},{4,28},{8,16},{12,20},{16,8},{20,12},{24,0},{28,4},{1,25},{... | collective-permute-start | bytes 589832 | tf_op jit(solution)/shard_map/ppermute | solution.py:28
  6.2 2.5 %load_weights.1 = (bf16[3072,512]{1,0:T(8,128)(2,1)S(1)}, bf16[8,3072]{1,0:T(8,128)(2,1)S(1)}, bf16[256,3072]{1,0:T(8,128)(2,1)S(1)}, bf16[32,3072]{1,0:T(8,128)(2,1)S(1)}, bf16[32,3072]{1,0:T(8,128)(2,1)S(1)}) custom-call(s32[1]{0:T(128)} %bitcast.1.section_ref, bf16[512,3072]{1,0:T(8,128)(2,1)} %bitcast.8, bf16[8,3072]{1,0:T(8,128)(2,1)} %bitcast.12, ...), custom_call_target="tpu_custom_call" | custom-call | tf_op jit(solution)/shard_map/load_weights/pallas_call | solution.py:252
  8.7 0.6 %collective-permute-start.6 = (bf16[32,3072]{1,0:T(8,128)(2,1)S(1)}, bf16[32,3072]{1,0:T(8,128)(2,1)S(1)}, u32[]{:S(2)}, u32[]{:S(2)}) collective-permute-start(bf16[32,3072]{1,0:T(8,128)(2,1)S(1)} %get-tuple-element.59), channel_id=1, source_target_pairs={{0,8},{4,20},{8,0},{12,28},{16,24},{20,4},{24,16},{28,12},{1,9},{5... | collective-permute-start | bytes 589832 | tf_op jit(solution)/shard_map/ppermute | solution.py:28
  9.3 0.0 collective-permute-start.7
  9.3 2.2 %collective-permute-done.2.refs_1_ = bf16[32,3072]{1,0:T(8,128)(2,1)S(1)} collective-permute-done((bf16[32,3072]{1,0:T(8,128)(2,1)S(1)}, bf16[32,3072]{1,0:T(8,128)(2,1)S(1)}, u32[]{:S(2)}, u32[]{:S(2)}) %collective-permute-start.2) | collective-permute-done | bytes 196640 | tf_op jit(solution)/shard_map/ppermute | solution.py:28
  11.5 1.0 %expert.2 = (bf16[16,3072]{1,0:T(8,128)(2,1)S(1)}, bf16[16,3072]{1,0:T(8,128)(2,1)S(1)}, bf16[16,3072]{1,0:T(8,128)(2,1)S(1)}, bf16[16,3072]{1,0:T(8,128)(2,1)S(1)}) custom-call(bf16[3072,512]{1,0:T(8,128)(2,1)S(1)} %get-tuple-element.51.in_ref, bf16[256,3072]{1,0:T(8,128)(2,1)S(1)} %get-tuple-element.52.down_ref, ...), custom_call_target="tpu_custom_call" | custom-call | tf_op jit(solution)/shard_map/expert/pallas_call | solution.py:283
  12.5 0.1 collective-permute-start.3
  12.6 3.4 %collective-permute-start.4 = (bf16[16,3072]{1,0:T(8,128)(2,1)S(1)}, bf16[16,3072]{1,0:T(8,128)(2,1)S(1)}, u32[]{:S(2)}, u32[]{:S(2)}) collective-permute-start(bf16[16,3072]{1,0:T(8,128)(2,1)S(1)} %get-tuple-element.57), channel_id=1, source_target_pairs={{0,24},{4,28},{8,16},{12,20},{16,8},{20,12},{24,0},{28,4},{1,25},{... | collective-permute-start | bytes 294920 | tf_op jit(solution)/shard_map/ppermute | solution.py:28
  16.1 0.1 collective-permute-start.5
  16.1 1.0 %expert.3 = (bf16[16,3072]{1,0:T(8,128)(2,1)S(1)}, bf16[16,3072]{1,0:T(8,128)(2,1)S(1)}, bf16[16,3072]{1,0:T(8,128)(2,1)S(1)}, bf16[16,3072]{1,0:T(8,128)(2,1)S(1)}) custom-call(bf16[3072,512]{1,0:T(8,128)(2,1)S(1)} %get-tuple-element.51.in_ref, bf16[256,3072]{1,0:T(8,128)(2,1)S(1)} %get-tuple-element.52.down_ref, ...), custom_call_target="tpu_custom_call" | custom-call | tf_op jit(solution)/shard_map/expert/pallas_call | solution.py:283
  17.2 1.2 %collective-permute-start.8 = (bf16[16,3072]{1,0:T(8,128)(2,1)S(1)}, bf16[16,3072]{1,0:T(8,128)(2,1)S(1)}, u32[]{:S(2)}, u32[]{:S(2)}) collective-permute-start(bf16[16,3072]{1,0:T(8,128)(2,1)S(1)} %get-tuple-element.61), channel_id=1, source_target_pairs={{0,8},{4,20},{8,0},{12,28},{16,24},{20,4},{24,16},{28,12},{1,9},{5... | collective-permute-start | bytes 294920 | tf_op jit(solution)/shard_map/ppermute | solution.py:28
  18.4 1.7 %collective-permute-start.9 = (bf16[16,3072]{1,0:T(8,128)(2,1)S(1)}, bf16[16,3072]{1,0:T(8,128)(2,1)S(1)}, u32[]{:S(2)}, u32[]{:S(2)}) collective-permute-start(bf16[16,3072]{1,0:T(8,128)(2,1)S(1)} %get-tuple-element.62), channel_id=1, source_target_pairs={{0,12},{4,16},{8,4},{12,24},{16,28},{20,0},{24,20},{28,8},{1,13},{... | collective-permute-start | bytes 294920 | tf_op jit(solution)/shard_map/ppermute | solution.py:28
  20.1 0.4 %collective-permute-start.10 = (bf16[16,3072]{1,0:T(8,128)(2,1)S(1)}, bf16[16,3072]{1,0:T(8,128)(2,1)S(1)}, u32[]{:S(2)}, u32[]{:S(2)}) collective-permute-start(bf16[16,3072]{1,0:T(8,128)(2,1)S(1)} %get-tuple-element.63), channel_id=1, source_target_pairs={{0,16},{4,12},{8,24},{12,4},{16,0},{20,28},{24,8},{28,20},{1,17},{... | collective-permute-start | bytes 294920 | tf_op jit(solution)/shard_map/ppermute | solution.py:28
  20.5 0.3 collective-permute-start.11
  20.7 0.3 mix.1
  21.1 0.8 %collective-permute-done.5.refs_3_ = bf16[16,3072]{1,0:T(8,128)(2,1)S(1)} collective-permute-done((bf16[16,3072]{1,0:T(8,128)(2,1)S(1)}, bf16[16,3072]{1,0:T(8,128)(2,1)S(1)}, u32[]{:S(2)}, u32[]{:S(2)}) %collective-permute-start.5) | collective-permute-done | bytes 98336 | tf_op jit(solution)/shard_map/ppermute | solution.py:28
  21.8 0.2 begin.1.begun_ref
  22.1 0.7 %collective-permute-done.8.refs_0_ = bf16[16,3072]{1,0:T(8,128)(2,1)S(1)} collective-permute-done((bf16[16,3072]{1,0:T(8,128)(2,1)S(1)}, bf16[16,3072]{1,0:T(8,128)(2,1)S(1)}, u32[]{:S(2)}, u32[]{:S(2)}) %collective-permute-start.8) | collective-permute-done | bytes 98336 | tf_op jit(solution)/shard_map/ppermute | solution.py:28
  22.8 2.1 %collective-permute-done.9.refs_1_ = bf16[16,3072]{1,0:T(8,128)(2,1)S(1)} collective-permute-done((bf16[16,3072]{1,0:T(8,128)(2,1)S(1)}, bf16[16,3072]{1,0:T(8,128)(2,1)S(1)}, u32[]{:S(2)}, u32[]{:S(2)}) %collective-permute-start.9) | collective-permute-done | bytes 98336 | tf_op jit(solution)/shard_map/ppermute | solution.py:28
  24.9 0.4 collective-permute-done.10.refs_2_
  25.2 0.0 collective-permute-done.11.refs_3_
  25.2 0.3 close.1
  25.5 3.7 %collective-permute-start.12 = (bf16[32,768]{1,0:T(8,128)(2,1)S(1)}, bf16[32,768]{1,0:T(8,128)(2,1)S(1)}, u32[]{:S(2)}, u32[]{:S(2)}) collective-permute-start(bf16[32,768]{1,0:T(8,128)(2,1)S(1)} %get-tuple-element.66), channel_id=1, source_target_pairs={{0,3},{1,2},{2,1},{3,0},{4,7},{5,6},{6,5},{7,4},{8,11},{9,10},{10,... | collective-permute-start | bytes 147464 | tf_op jit(solution)/shard_map/ppermute | solution.py:22
  29.2 0.8 %collective-permute-start.14 = (bf16[32,768]{1,0:T(8,128)(2,1)S(1)}, bf16[32,768]{1,0:T(8,128)(2,1)S(1)}, u32[]{:S(2)}, u32[]{:S(2)}) collective-permute-start(bf16[32,768]{1,0:T(8,128)(2,1)S(1)} %get-tuple-element.68), channel_id=1, source_target_pairs={{0,1},{1,0},{2,3},{3,2},{4,5},{5,4},{6,7},{7,6},{8,9},{9,8},{10,11... | collective-permute-start | bytes 147464 | tf_op jit(solution)/shard_map/ppermute | solution.py:22
  30.0 2.0 %collective-permute-done.12.refs_1_ = bf16[32,768]{1,0:T(8,128)(2,1)S(1)} collective-permute-done((bf16[32,768]{1,0:T(8,128)(2,1)S(1)}, bf16[32,768]{1,0:T(8,128)(2,1)S(1)}, u32[]{:S(2)}, u32[]{:S(2)}) %collective-permute-start.12) | collective-permute-done | bytes 49184 | tf_op jit(solution)/shard_map/ppermute | solution.py:22
  32.0 2.4 %collective-permute-done.13.refs_2_ = bf16[32,768]{1,0:T(8,128)(2,1)S(1)} collective-permute-done((bf16[32,768]{1,0:T(8,128)(2,1)S(1)}, bf16[32,768]{1,0:T(8,128)(2,1)S(1)}, u32[]{:S(2)}, u32[]{:S(2)}) %collective-permute-start.13) | collective-permute-done | bytes 49184 | tf_op jit(solution)/shard_map/ppermute | solution.py:22
  34.4 0.0 collective-permute-done.14.refs_3_
  34.4 0.6 %finish.1 = bf16[2,16,768]{2,1,0:T(8,128)(2,1)} custom-call(f32[32,768]{1,0:T(8,128)S(1)} %get-tuple-element.65.refs_0_, bf16[32,768]{1,0:T(8,128)(2,1)S(1)} %collective-permute-done.12.refs_1_, bf16[32,768]{1,0:T(8,128)(2,1)S(1)} %collective-permute-done.13.refs_2_, bf16[32,768]{1,0:T(8,128)(2,1)S(1)} %collective-permute-done.14.refs_3_), custom_call_target="tpu_custom_call" | custom-call | tf_op jit(solution)/shard_map/finish/pallas_call | solution.py:383
  (7 shorter events, 0.0 us)
Async XLA Ops:
  0.0 1.8 %collective-permute-start = (bf16[32,3072]{1,0:T(8,128)(2,1)}, bf16[32,3072]{1,0:T(8,128)(2,1)S(1)}, u32[]{:S(2)}, u32[]{:S(2)}) collective-permute-start(bf16[32,3072]{1,0:T(8,128)(2,1)} %bitcast.10), channel_id=1, source_target_pairs={{0,4},{4,0},{8,12},{12,8},{16,20},{20,16},{24,28},{28,24},{1,5},{5... | collective-permute-start | bytes 589832 | tf_op jit(solution)/shard_map/ppermute | solution.py:22
  0.5 1.4 %collective-permute-start.1 = (s32[2,2,16]{2,1,0:T(2,128)}, s32[2,2,16]{2,1,0:T(2,128)S(1)}, u32[]{:S(2)}, u32[]{:S(2)}) collective-permute-start(s32[2,2,16]{2,1,0:T(2,128)} %bitcast.14), channel_id=1, source_target_pairs={{0,4},{4,0},{8,12},{12,8},{16,20},{20,16},{24,28},{28,24},{1,5},{5... | collective-permute-start | bytes 776 | tf_op jit(solution)/shard_map/ppermute | solution.py:22
  2.2 9.3 %collective-permute-start.2 = (bf16[32,3072]{1,0:T(8,128)(2,1)S(1)}, bf16[32,3072]{1,0:T(8,128)(2,1)S(1)}, u32[]{:S(2)}, u32[]{:S(2)}) collective-permute-start(bf16[32,3072]{1,0:T(8,128)(2,1)S(1)} %get-tuple-element.54), channel_id=1, source_target_pairs={{0,24},{4,28},{8,16},{12,20},{16,8},{20,12},{24,0},{28,4},{1,25},{... | collective-permute-start | bytes 589832 | tf_op jit(solution)/shard_map/ppermute | solution.py:28
  8.7 7.5 %collective-permute-start.6 = (bf16[32,3072]{1,0:T(8,128)(2,1)S(1)}, bf16[32,3072]{1,0:T(8,128)(2,1)S(1)}, u32[]{:S(2)}, u32[]{:S(2)}) collective-permute-start(bf16[32,3072]{1,0:T(8,128)(2,1)S(1)} %get-tuple-element.59), channel_id=1, source_target_pairs={{0,8},{4,20},{8,0},{12,28},{16,24},{20,4},{24,16},{28,12},{1,9},{5... | collective-permute-start | bytes 589832 | tf_op jit(solution)/shard_map/ppermute | solution.py:28
  9.3 6.9 %collective-permute-start.7 = (bf16[32,3072]{1,0:T(8,128)(2,1)S(1)}, bf16[32,3072]{1,0:T(8,128)(2,1)S(1)}, u32[]{:S(2)}, u32[]{:S(2)}) collective-permute-start(bf16[32,3072]{1,0:T(8,128)(2,1)S(1)} %get-tuple-element.60), channel_id=1, source_target_pairs={{0,16},{4,12},{8,24},{12,4},{16,0},{20,28},{24,8},{28,20},{1,17},{... | collective-permute-start | bytes 589832 | tf_op jit(solution)/shard_map/ppermute | solution.py:28
  12.5 7.6 %collective-permute-start.3 = (bf16[16,3072]{1,0:T(8,128)(2,1)S(1)}, bf16[16,3072]{1,0:T(8,128)(2,1)S(1)}, u32[]{:S(2)}, u32[]{:S(2)}) collective-permute-start(bf16[16,3072]{1,0:T(8,128)(2,1)S(1)} %get-tuple-element.56), channel_id=1, source_target_pairs={{0,4},{4,0},{8,12},{12,8},{16,20},{20,16},{24,28},{28,24},{1,5},{5... | collective-permute-start | bytes 294920 | tf_op jit(solution)/shard_map/ppermute | solution.py:22
  12.6 7.9 %collective-permute-start.4 = (bf16[16,3072]{1,0:T(8,128)(2,1)S(1)}, bf16[16,3072]{1,0:T(8,128)(2,1)S(1)}, u32[]{:S(2)}, u32[]{:S(2)}) collective-permute-start(bf16[16,3072]{1,0:T(8,128)(2,1)S(1)} %get-tuple-element.57), channel_id=1, source_target_pairs={{0,24},{4,28},{8,16},{12,20},{16,8},{20,12},{24,0},{28,4},{1,25},{... | collective-permute-start | bytes 294920 | tf_op jit(solution)/shard_map/ppermute | solution.py:28
  16.1 5.7 %collective-permute-start.5 = (bf16[16,3072]{1,0:T(8,128)(2,1)S(1)}, bf16[16,3072]{1,0:T(8,128)(2,1)S(1)}, u32[]{:S(2)}, u32[]{:S(2)}) collective-permute-start(bf16[16,3072]{1,0:T(8,128)(2,1)S(1)} %get-tuple-element.58), channel_id=1, source_target_pairs={{0,28},{4,24},{8,20},{12,16},{16,12},{20,8},{24,4},{28,0},{1,29},{... | collective-permute-start | bytes 294920 | tf_op jit(solution)/shard_map/ppermute | solution.py:28
  17.2 5.6 %collective-permute-start.8 = (bf16[16,3072]{1,0:T(8,128)(2,1)S(1)}, bf16[16,3072]{1,0:T(8,128)(2,1)S(1)}, u32[]{:S(2)}, u32[]{:S(2)}) collective-permute-start(bf16[16,3072]{1,0:T(8,128)(2,1)S(1)} %get-tuple-element.61), channel_id=1, source_target_pairs={{0,8},{4,20},{8,0},{12,28},{16,24},{20,4},{24,16},{28,12},{1,9},{5... | collective-permute-start | bytes 294920 | tf_op jit(solution)/shard_map/ppermute | solution.py:28
  18.4 6.5 %collective-permute-start.9 = (bf16[16,3072]{1,0:T(8,128)(2,1)S(1)}, bf16[16,3072]{1,0:T(8,128)(2,1)S(1)}, u32[]{:S(2)}, u32[]{:S(2)}) collective-permute-start(bf16[16,3072]{1,0:T(8,128)(2,1)S(1)} %get-tuple-element.62), channel_id=1, source_target_pairs={{0,12},{4,16},{8,4},{12,24},{16,28},{20,0},{24,20},{28,8},{1,13},{... | collective-permute-start | bytes 294920 | tf_op jit(solution)/shard_map/ppermute | solution.py:28
  20.1 5.1 %collective-permute-start.10 = (bf16[16,3072]{1,0:T(8,128)(2,1)S(1)}, bf16[16,3072]{1,0:T(8,128)(2,1)S(1)}, u32[]{:S(2)}, u32[]{:S(2)}) collective-permute-start(bf16[16,3072]{1,0:T(8,128)(2,1)S(1)} %get-tuple-element.63), channel_id=1, source_target_pairs={{0,16},{4,12},{8,24},{12,4},{16,0},{20,28},{24,8},{28,20},{1,17},{... | collective-permute-start | bytes 294920 | tf_op jit(solution)/shard_map/ppermute | solution.py:28
  20.5 4.8 %collective-permute-start.11 = (bf16[16,3072]{1,0:T(8,128)(2,1)S(1)}, bf16[16,3072]{1,0:T(8,128)(2,1)S(1)}, u32[]{:S(2)}, u32[]{:S(2)}) collective-permute-start(bf16[16,3072]{1,0:T(8,128)(2,1)S(1)} %get-tuple-element.64), channel_id=1, source_target_pairs={{0,20},{4,8},{8,28},{12,0},{16,4},{20,24},{24,12},{28,16},{1,21},{... | collective-permute-start | bytes 294920 | tf_op jit(solution)/shard_map/ppermute | solution.py:28
  25.5 6.5 %collective-permute-start.12 = (bf16[32,768]{1,0:T(8,128)(2,1)S(1)}, bf16[32,768]{1,0:T(8,128)(2,1)S(1)}, u32[]{:S(2)}, u32[]{:S(2)}) collective-permute-start(bf16[32,768]{1,0:T(8,128)(2,1)S(1)} %get-tuple-element.66), channel_id=1, source_target_pairs={{0,3},{1,2},{2,1},{3,0},{4,7},{5,6},{6,5},{7,4},{8,11},{9,10},{10,... | collective-permute-start | bytes 147464 | tf_op jit(solution)/shard_map/ppermute | solution.py:22
  29.2 5.2 %collective-permute-start.13 = (bf16[32,768]{1,0:T(8,128)(2,1)S(1)}, bf16[32,768]{1,0:T(8,128)(2,1)S(1)}, u32[]{:S(2)}, u32[]{:S(2)}) collective-permute-start(bf16[32,768]{1,0:T(8,128)(2,1)S(1)} %get-tuple-element.67), channel_id=1, source_target_pairs={{0,2},{1,3},{2,0},{3,1},{4,6},{5,7},{6,4},{7,5},{8,10},{9,11},{10,... | collective-permute-start | bytes 147464 | tf_op jit(solution)/shard_map/ppermute | solution.py:22
  29.2 5.2 %collective-permute-start.14 = (bf16[32,768]{1,0:T(8,128)(2,1)S(1)}, bf16[32,768]{1,0:T(8,128)(2,1)S(1)}, u32[]{:S(2)}, u32[]{:S(2)}) collective-permute-start(bf16[32,768]{1,0:T(8,128)(2,1)S(1)} %get-tuple-element.68), channel_id=1, source_target_pairs={{0,1},{1,0},{2,3},{3,2},{4,5},{5,4},{6,7},{7,6},{8,9},{9,8},{10,11... | collective-permute-start | bytes 147464 | tf_op jit(solution)/shard_map/ppermute | solution.py:22

commit v5 on v4

--- a/solution.py
+++ b/solution.py
@@ -9,6 +9,7 @@
 
 epsilon = 1e-05
 LANES = 128
+TOKEN_COPIES = 4
 NT = (((1,), (1,)), ((), ()))
 VMEM = pl.BlockSpec(memory_space=pltpu.VMEM)
 ANY = pl.BlockSpec(memory_space=pl.ANY)
@@ -20,6 +21,12 @@
 def trade(value, axis, distance):
     count = lax.axis_size(axis)
     return lax.ppermute(value, axis, [(place, place ^ distance) for place in range(count)])
+
+
+def turn(value, distance):
+    count = lax.axis_size("inner")
+    pairs = [(place, (place + distance) % count) for place in range(count)]
+    return lax.ppermute(value, "inner", pairs)
 
 
 def visit(value, step, cross):
@@ -81,11 +88,14 @@
 def own_kernel(steps, per_expert, section_ref, tokens_ref, named_ref, gain_ref, *refs):
     half_refs, refs = refs[: len(steps)], refs[len(steps) :]
     own_ref, gain_out_ref, normed_ref, slots_ref, names_ref, held_ref, sems = refs
+    width = tokens_ref.shape[1]
+    chunk = width // TOKEN_COPIES
+    spans = [pl.ds(k * chunk, chunk) for k in range(TOKEN_COPIES)]
+    pairs = [(tokens_ref.at[:, span], own_ref.at[:, span]) for span in spans]
+    pairs = [(named_ref, held_ref), *pairs, (gain_ref, gain_out_ref)]
     copies = [
         pltpu.make_async_copy(source, target, sems.at[k])
-        for k, (source, target) in enumerate(
-            [(named_ref, held_ref), (gain_ref, gain_out_ref), (tokens_ref, own_ref)]
-        )
+        for k, (source, target) in enumerate(pairs)
     ]
     for copy in copies:
         copy.start()
@@ -95,8 +105,8 @@
     slots_ref[...] = slots
     names_ref[0:1, :] = named[0]
     names_ref[1:2, :] = named[1]
-    copies[1].wait()
-    copies[2].wait()
+    for copy in copies[1:]:
+        copy.wait()
     normed = normed_of(own_ref[...], gain_out_ref[...])
     normed_ref[...] = normed
     packed = picked(section_ref[0], slots, normed, steps, per_expert)
@@ -120,7 +130,7 @@
         out_shape=shapes,
         in_specs=[SMEM] + [HBM] * 3,
         out_specs=[VMEM] * len(shapes),
-        scratch_shapes=[pltpu.VMEM(named.shape, jnp.int32), pltpu.SemaphoreType.DMA((3,))],
+        scratch_shapes=[pltpu.VMEM(named.shape, jnp.int32), pltpu.SemaphoreType.DMA((TOKEN_COPIES + 2,))],
         compiler_params=PARAMS,
         name="own_part",
     )(section, *arrays)
@@ -329,7 +339,7 @@
         return
     part = outs[0].shape[1]
     for k, out_ref in enumerate(outs):
-        columns = pl.ds(pl.multiple_of((member_ref[0] ^ k) * part, LANES), part)
+        columns = pl.ds(pl.multiple_of(lax.rem(member_ref[0] + k, len(outs)) * part, LANES), part)
         value = total_ref[:, columns]
         if k == 0:
             value = value + tokens_ref[:, columns].astype(jnp.float32)
@@ -364,7 +374,8 @@
     total = outs[0] + tokens.astype(jnp.float32)
     outs = [lax.dynamic_slice_in_dim(total, member * part, part, 1)]
     for k in range(1, inner_count):
-        outs.append(lax.dynamic_slice_in_dim(rounded, (member ^ k) * part, part, 1))
+        place = lax.rem(member + k, inner_count)
+        outs.append(lax.dynamic_slice_in_dim(rounded, place * part, part, 1))
     return outs
 
 
@@ -435,7 +446,7 @@
         a, b = step
         return ((2 * a, 2 * b), (2 * b + 1, 2 * a + 1))
 
-    early = origins((0, 0)) + origins((far, far))
+    early = origins((far, far)) + origins((0, 0))
     late = tuple(pair for step in steps for pair in origins(step))
     high_a, low_a, high_b, low_b = mix(
         section, normed, slots, names, router_rows, early, late, per_expert
@@ -443,12 +454,12 @@
     here, beside, *away = run_expert([message, away], turned_in, down, 2)
     results = run_expert(arrived, turned_in, down, 2, (here,))
     away = [visit(value, (far, far), cross) for cross, value in enumerate(away)]
-    begun = begin(high_a, low_a, [here, trade(beside, "section", 1), *away])
+    begun = begin(high_a, low_a, [*away, here, trade(beside, "section", 1)])
     results = [visit(value, steps[j // 2], j % 2) for j, value in enumerate(results)]
     split = close(high_b, low_b, begun, results, own, member, inner_count)
-    pieces = {k: trade(split[k], "inner", k) for k in reversed(range(1, inner_count))}
+    pieces = {k: turn(split[k], k) for k in range(1, inner_count)}
     pieces[0] = split[0]
-    return finish([pieces[k] for k in [0] + list(reversed(range(1, inner_count)))], micro, row_count)
+    return finish([pieces[k] for k in range(inner_count)], micro, row_count)
 
 
 def solution(mesh):

time: 35.2 us -> 35 us (level)
  waiting for transfers between devices: 10.6 us -> 8.86 us
  starting transfers between devices: 16.7 us -> 18.2 us
    ppermute x0 -> x3, starting transfers between devices: none -> 5.54 us  [turn(): return lax.ppermute(value, 'inner', pairs)]
    ppermute x6 -> x3, waiting for transfers between devices: 4.43 us -> 0.04 us  [trade(): lax.ppermute(value, axis, [(place, place ^ distance) for place in range(c...]
    ppermute x6 -> x3, starting transfers between devices: 5.06 us -> 0.7 us  [trade(): lax.ppermute(value, axis, [(place, place ^ distance) for place in range(c...]
    ppermute x0 -> x3, waiting for transfers between devices: none -> 2.89 us  [turn(): return lax.ppermute(value, 'inner', pairs)]
  transfers between devices with their start and end apart: 15 -> 15, of which waited for: 7 -> 8; matrix products, arithmetic and copies ran while one was open for 0% -> 0% of each run, Pallas kernels for 18% -> 18%
where the time goes in v5:
time: 35 us; the launch traced here: 34.8 us
  starting transfers between devices  18.2 us (52%)
  waiting for transfers between devices  8.86 us (25%)
  Pallas kernels  7.65 us (22%)
    ppermute x9, starting transfers between devices, visit(): return lax.ppermute(value, 'section', pairs)  12 us
    ppermute x9, waiting for transfers between devices, visit(): return lax.ppermute(value, 'section', pairs)  5.93 us
    ppermute x3, starting transfers between devices, turn(): return lax.ppermute(value, 'inner', pairs)  5.54 us
    ppermute x3, waiting for transfers between devices, turn(): return lax.ppermute(value, 'inner', pairs)  2.89 us
    pallas_call x1, Pallas kernels, load_weights(): pl.pallas_call(functools.partial(load_kernel, count, steps, per_expert),...  2.46 us
    pallas_call x2, Pallas kernels, run_expert(): pl.pallas_call(functools.partial(expert_kernel, count, len(after)), out_s...  2.06 us
    pallas_call x1, Pallas kernels, own_part(): pl.pallas_call(functools.partial(own_kernel, steps, per_expert), out_shap...  1.26 us
    ppermute x3, starting transfers between devices, trade(): lax.ppermute(value, axis, [(place, place ^ distance) for place in range(c...  0.7 us
  transfers between devices with their start and end apart: 15, of which 8 were waited for; matrix products, arithmetic and copies ran while one was open for 0% of the time, Pallas kernels for 18%

profile of v5, /device:TPU:0, one launch (start us, length us, event | category | flops | bytes accessed | tf_op | source)
XLA Modules:
  0.0 34.8 jit_solution(3855164333516364812)
XLA Ops:
  0.0 0.5 %collective-permute-start = (bf16[32,3072]{1,0:T(8,128)(2,1)}, bf16[32,3072]{1,0:T(8,128)(2,1)S(1)}, u32[]{:S(2)}, u32[]{:S(2)}) collective-permute-start(bf16[32,3072]{1,0:T(8,128)(2,1)} %bitcast.10), channel_id=1, source_target_pairs={{0,4},{4,0},{8,12},{12,8},{16,20},{20,16},{24,28},{28,24},{1,5},{5... | collective-permute-start | bytes 589832 | tf_op jit(solution)/shard_map/ppermute | solution.py:23
  0.5 0.1 collective-permute-start.1
  0.5 1.3 %own_part.1 = (bf16[16,3072]{1,0:T(8,128)(2,1)S(1)}, bf16[16,3072]{1,0:T(8,128)(2,1)S(1)}, bf16[32,3072]{1,0:T(8,128)(2,1)S(1)}, f32[1,3072]{1,0:T(1,128)S(1)}, ...) custom-call(s32[1]{0:T(128)} %bitcast.1.section_ref, bf16[32,3072]{1,0:T(8,128)(2,1)} %bitcast.11, ...), custom_call_target="tpu_custom_call" | custom-call | tf_op jit(solution)/shard_map/own_part/pallas_call | solution.py:128
  1.8 0.0 collective-permute-done.1.named_ref
  1.8 0.4 %other_part.1 = (bf16[32,3072]{1,0:T(8,128)(2,1)S(1)}, bf16[32,3072]{1,0:T(8,128)(2,1)S(1)}, bf16[32,3072]{1,0:T(8,128)(2,1)S(1)}, f32[8,32]{1,0:T(8,128)S(1)}) custom-call(s32[1]{0:T(128)} %bitcast.1.section_ref, bf16[32,3072]{1,0:T(8,128)(2,1)S(1)} %collective-permute-done.other_ref, s32[2,2,16]{2,1,0:T(2,128)S(1)} %collective-permute-done.1.named_ref, ...), custom_call_target="tpu_custom_call" | custom-call | tf_op jit(solution)/shard_map/other_part/pallas_call | solution.py:157
  2.2 3.9 %collective-permute-start.2 = (bf16[32,3072]{1,0:T(8,128)(2,1)S(1)}, bf16[32,3072]{1,0:T(8,128)(2,1)S(1)}, u32[]{:S(2)}, u32[]{:S(2)}) collective-permute-start(bf16[32,3072]{1,0:T(8,128)(2,1)S(1)} %get-tuple-element.54), channel_id=1, source_target_pairs={{0,24},{4,28},{8,16},{12,20},{16,8},{20,12},{24,0},{28,4},{1,25},{... | collective-permute-start | bytes 589832 | tf_op jit(solution)/shard_map/ppermute | solution.py:35
  6.1 2.5 %load_weights.1 = (bf16[3072,512]{1,0:T(8,128)(2,1)S(1)}, bf16[8,3072]{1,0:T(8,128)(2,1)S(1)}, bf16[256,3072]{1,0:T(8,128)(2,1)S(1)}, bf16[32,3072]{1,0:T(8,128)(2,1)S(1)}, bf16[32,3072]{1,0:T(8,128)(2,1)S(1)}) custom-call(s32[1]{0:T(128)} %bitcast.1.section_ref, bf16[512,3072]{1,0:T(8,128)(2,1)} %bitcast.8, bf16[8,3072]{1,0:T(8,128)(2,1)} %bitcast.12, ...), custom_call_target="tpu_custom_call" | custom-call | tf_op jit(solution)/shard_map/load_weights/pallas_call | solution.py:262
  8.6 0.6 %collective-permute-start.6 = (bf16[32,3072]{1,0:T(8,128)(2,1)S(1)}, bf16[32,3072]{1,0:T(8,128)(2,1)S(1)}, u32[]{:S(2)}, u32[]{:S(2)}) collective-permute-start(bf16[32,3072]{1,0:T(8,128)(2,1)S(1)} %get-tuple-element.59), channel_id=1, source_target_pairs={{0,8},{4,20},{8,0},{12,28},{16,24},{20,4},{24,16},{28,12},{1,9},{5... | collective-permute-start | bytes 589832 | tf_op jit(solution)/shard_map/ppermute | solution.py:35
  9.2 0.0 collective-permute-start.7
  9.3 2.2 %collective-permute-done.2.refs_1_ = bf16[32,3072]{1,0:T(8,128)(2,1)S(1)} collective-permute-done((bf16[32,3072]{1,0:T(8,128)(2,1)S(1)}, bf16[32,3072]{1,0:T(8,128)(2,1)S(1)}, u32[]{:S(2)}, u32[]{:S(2)}) %collective-permute-start.2) | collective-permute-done | bytes 196640 | tf_op jit(solution)/shard_map/ppermute | solution.py:35
  11.4 1.0 %expert.2 = (bf16[16,3072]{1,0:T(8,128)(2,1)S(1)}, bf16[16,3072]{1,0:T(8,128)(2,1)S(1)}, bf16[16,3072]{1,0:T(8,128)(2,1)S(1)}, bf16[16,3072]{1,0:T(8,128)(2,1)S(1)}) custom-call(bf16[3072,512]{1,0:T(8,128)(2,1)S(1)} %get-tuple-element.51.in_ref, bf16[256,3072]{1,0:T(8,128)(2,1)S(1)} %get-tuple-element.52.down_ref, ...), custom_call_target="tpu_custom_call" | custom-call | tf_op jit(solution)/shard_map/expert/pallas_call | solution.py:293
  12.5 3.4 %collective-permute-start.3 = (bf16[16,3072]{1,0:T(8,128)(2,1)S(1)}, bf16[16,3072]{1,0:T(8,128)(2,1)S(1)}, u32[]{:S(2)}, u32[]{:S(2)}) collective-permute-start(bf16[16,3072]{1,0:T(8,128)(2,1)S(1)} %get-tuple-element.55), channel_id=1, source_target_pairs={{0,24},{4,28},{8,16},{12,20},{16,8},{20,12},{24,0},{28,4},{1,25},{... | collective-permute-start | bytes 294920 | tf_op jit(solution)/shard_map/ppermute | solution.py:35
  15.9 0.2 collective-permute-start.5
  16.1 1.0 %expert.3 = (bf16[16,3072]{1,0:T(8,128)(2,1)S(1)}, bf16[16,3072]{1,0:T(8,128)(2,1)S(1)}, bf16[16,3072]{1,0:T(8,128)(2,1)S(1)}, bf16[16,3072]{1,0:T(8,128)(2,1)S(1)}) custom-call(bf16[3072,512]{1,0:T(8,128)(2,1)S(1)} %get-tuple-element.51.in_ref, bf16[256,3072]{1,0:T(8,128)(2,1)S(1)} %get-tuple-element.52.down_ref, ...), custom_call_target="tpu_custom_call" | custom-call | tf_op jit(solution)/shard_map/expert/pallas_call | solution.py:293
  17.2 1.5 %collective-permute-start.8 = (bf16[16,3072]{1,0:T(8,128)(2,1)S(1)}, bf16[16,3072]{1,0:T(8,128)(2,1)S(1)}, u32[]{:S(2)}, u32[]{:S(2)}) collective-permute-start(bf16[16,3072]{1,0:T(8,128)(2,1)S(1)} %get-tuple-element.61), channel_id=1, source_target_pairs={{0,8},{4,20},{8,0},{12,28},{16,24},{20,4},{24,16},{28,12},{1,9},{5... | collective-permute-start | bytes 294920 | tf_op jit(solution)/shard_map/ppermute | solution.py:35
  18.7 1.3 %collective-permute-start.9 = (bf16[16,3072]{1,0:T(8,128)(2,1)S(1)}, bf16[16,3072]{1,0:T(8,128)(2,1)S(1)}, u32[]{:S(2)}, u32[]{:S(2)}) collective-permute-start(bf16[16,3072]{1,0:T(8,128)(2,1)S(1)} %get-tuple-element.62), channel_id=1, source_target_pairs={{0,12},{4,16},{8,4},{12,24},{16,28},{20,0},{24,20},{28,8},{1,13},{... | collective-permute-start | bytes 294920 | tf_op jit(solution)/shard_map/ppermute | solution.py:35
  20.0 0.7 %collective-permute-start.10 = (bf16[16,3072]{1,0:T(8,128)(2,1)S(1)}, bf16[16,3072]{1,0:T(8,128)(2,1)S(1)}, u32[]{:S(2)}, u32[]{:S(2)}) collective-permute-start(bf16[16,3072]{1,0:T(8,128)(2,1)S(1)} %get-tuple-element.63), channel_id=1, source_target_pairs={{0,16},{4,12},{8,24},{12,4},{16,0},{20,28},{24,8},{28,20},{1,17},{... | collective-permute-start | bytes 294920 | tf_op jit(solution)/shard_map/ppermute | solution.py:35
  20.7 0.3 collective-permute-done.4.refs_1_
  20.9 0.4 %collective-permute-start.11 = (bf16[16,3072]{1,0:T(8,128)(2,1)S(1)}, bf16[16,3072]{1,0:T(8,128)(2,1)S(1)}, u32[]{:S(2)}, u32[]{:S(2)}) collective-permute-start(bf16[16,3072]{1,0:T(8,128)(2,1)S(1)} %get-tuple-element.64), channel_id=1, source_target_pairs={{0,20},{4,8},{8,28},{12,0},{16,4},{20,24},{24,12},{28,16},{1,21},{... | collective-permute-start | bytes 294920 | tf_op jit(solution)/shard_map/ppermute | solution.py:35
  21.4 0.3 mix.1
  21.7 0.2 begin.1.begun_ref
  22.0 1.1 %collective-permute-done.9.refs_1_ = bf16[16,3072]{1,0:T(8,128)(2,1)S(1)} collective-permute-done((bf16[16,3072]{1,0:T(8,128)(2,1)S(1)}, bf16[16,3072]{1,0:T(8,128)(2,1)S(1)}, u32[]{:S(2)}, u32[]{:S(2)}) %collective-permute-start.9) | collective-permute-done | bytes 98336 | tf_op jit(solution)/shard_map/ppermute | solution.py:35
  23.1 1.5 %collective-permute-done.10.refs_2_ = bf16[16,3072]{1,0:T(8,128)(2,1)S(1)} collective-permute-done((bf16[16,3072]{1,0:T(8,128)(2,1)S(1)}, bf16[16,3072]{1,0:T(8,128)(2,1)S(1)}, u32[]{:S(2)}, u32[]{:S(2)}) %collective-permute-start.10) | collective-permute-done | bytes 98336 | tf_op jit(solution)/shard_map/ppermute | solution.py:35
  24.6 0.9 %collective-permute-done.11.refs_3_ = bf16[16,3072]{1,0:T(8,128)(2,1)S(1)} collective-permute-done((bf16[16,3072]{1,0:T(8,128)(2,1)S(1)}, bf16[16,3072]{1,0:T(8,128)(2,1)S(1)}, u32[]{:S(2)}, u32[]{:S(2)}) %collective-permute-start.11) | collective-permute-done | bytes 98336 | tf_op jit(solution)/shard_map/ppermute | solution.py:35
  25.5 0.3 close.1
  25.8 1.6 %collective-permute-start.12 = (bf16[32,768]{1,0:T(8,128)(2,1)S(1)}, bf16[32,768]{1,0:T(8,128)(2,1)S(1)}, u32[]{:S(2)}, u32[]{:S(2)}) collective-permute-start(bf16[32,768]{1,0:T(8,128)(2,1)S(1)} %get-tuple-element.66), channel_id=1, source_target_pairs={{0,1},{1,2},{2,3},{3,0},{4,5},{5,6},{6,7},{7,4},{8,9},{9,10},{10,1... | collective-permute-start | bytes 147464 | tf_op jit(solution)/shard_map/ppermute | solution.py:29
  27.4 2.6 %collective-permute-start.13 = (bf16[32,768]{1,0:T(8,128)(2,1)S(1)}, bf16[32,768]{1,0:T(8,128)(2,1)S(1)}, u32[]{:S(2)}, u32[]{:S(2)}) collective-permute-start(bf16[32,768]{1,0:T(8,128)(2,1)S(1)} %get-tuple-element.67), channel_id=1, source_target_pairs={{0,2},{1,3},{2,0},{3,1},{4,6},{5,7},{6,4},{7,5},{8,10},{9,11},{10,... | collective-permute-start | bytes 147464 | tf_op jit(solution)/shard_map/ppermute | solution.py:29
  30.0 1.3 %collective-permute-start.14 = (bf16[32,768]{1,0:T(8,128)(2,1)S(1)}, bf16[32,768]{1,0:T(8,128)(2,1)S(1)}, u32[]{:S(2)}, u32[]{:S(2)}) collective-permute-start(bf16[32,768]{1,0:T(8,128)(2,1)S(1)} %get-tuple-element.68), channel_id=1, source_target_pairs={{0,3},{1,0},{2,1},{3,2},{4,7},{5,4},{6,5},{7,6},{8,11},{9,8},{10,9... | collective-permute-start | bytes 147464 | tf_op jit(solution)/shard_map/ppermute | solution.py:29
  31.3 0.4 %collective-permute-done.12.refs_1_ = bf16[32,768]{1,0:T(8,128)(2,1)S(1)} collective-permute-done((bf16[32,768]{1,0:T(8,128)(2,1)S(1)}, bf16[32,768]{1,0:T(8,128)(2,1)S(1)}, u32[]{:S(2)}, u32[]{:S(2)}) %collective-permute-start.12) | collective-permute-done | bytes 49184 | tf_op jit(solution)/shard_map/ppermute | solution.py:29
  31.7 2.1 %collective-permute-done.13.refs_2_ = bf16[32,768]{1,0:T(8,128)(2,1)S(1)} collective-permute-done((bf16[32,768]{1,0:T(8,128)(2,1)S(1)}, bf16[32,768]{1,0:T(8,128)(2,1)S(1)}, u32[]{:S(2)}, u32[]{:S(2)}) %collective-permute-start.13) | collective-permute-done | bytes 49184 | tf_op jit(solution)/shard_map/ppermute | solution.py:29
  33.8 0.4 %collective-permute-done.14.refs_3_ = bf16[32,768]{1,0:T(8,128)(2,1)S(1)} collective-permute-done((bf16[32,768]{1,0:T(8,128)(2,1)S(1)}, bf16[32,768]{1,0:T(8,128)(2,1)S(1)}, u32[]{:S(2)}, u32[]{:S(2)}) %collective-permute-start.14) | collective-permute-done | bytes 49184 | tf_op jit(solution)/shard_map/ppermute | solution.py:29
  34.2 0.6 %finish.1 = bf16[2,16,768]{2,1,0:T(8,128)(2,1)} custom-call(f32[32,768]{1,0:T(8,128)S(1)} %get-tuple-element.65.refs_0_, bf16[32,768]{1,0:T(8,128)(2,1)S(1)} %collective-permute-done.12.refs_1_, bf16[32,768]{1,0:T(8,128)(2,1)S(1)} %collective-permute-done.13.refs_2_, bf16[32,768]{1,0:T(8,128)(2,1)S(1)} %collective-permute-done.14.refs_3_), custom_call_target="tpu_custom_call" | custom-call | tf_op jit(solution)/shard_map/finish/pallas_call | solution.py:394
  (7 shorter events, 0.0 us)
Async XLA Ops:
  0.0 1.8 %collective-permute-start = (bf16[32,3072]{1,0:T(8,128)(2,1)}, bf16[32,3072]{1,0:T(8,128)(2,1)S(1)}, u32[]{:S(2)}, u32[]{:S(2)}) collective-permute-start(bf16[32,3072]{1,0:T(8,128)(2,1)} %bitcast.10), channel_id=1, source_target_pairs={{0,4},{4,0},{8,12},{12,8},{16,20},{20,16},{24,28},{28,24},{1,5},{5... | collective-permute-start | bytes 589832 | tf_op jit(solution)/shard_map/ppermute | solution.py:23
  0.5 1.4 %collective-permute-start.1 = (s32[2,2,16]{2,1,0:T(2,128)}, s32[2,2,16]{2,1,0:T(2,128)S(1)}, u32[]{:S(2)}, u32[]{:S(2)}) collective-permute-start(s32[2,2,16]{2,1,0:T(2,128)} %bitcast.14), channel_id=1, source_target_pairs={{0,4},{4,0},{8,12},{12,8},{16,20},{20,16},{24,28},{28,24},{1,5},{5... | collective-permute-start | bytes 776 | tf_op jit(solution)/shard_map/ppermute | solution.py:23
  2.2 9.2 %collective-permute-start.2 = (bf16[32,3072]{1,0:T(8,128)(2,1)S(1)}, bf16[32,3072]{1,0:T(8,128)(2,1)S(1)}, u32[]{:S(2)}, u32[]{:S(2)}) collective-permute-start(bf16[32,3072]{1,0:T(8,128)(2,1)S(1)} %get-tuple-element.54), channel_id=1, source_target_pairs={{0,24},{4,28},{8,16},{12,20},{16,8},{20,12},{24,0},{28,4},{1,25},{... | collective-permute-start | bytes 589832 | tf_op jit(solution)/shard_map/ppermute | solution.py:35
  8.6 7.5 %collective-permute-start.6 = (bf16[32,3072]{1,0:T(8,128)(2,1)S(1)}, bf16[32,3072]{1,0:T(8,128)(2,1)S(1)}, u32[]{:S(2)}, u32[]{:S(2)}) collective-permute-start(bf16[32,3072]{1,0:T(8,128)(2,1)S(1)} %get-tuple-element.59), channel_id=1, source_target_pairs={{0,8},{4,20},{8,0},{12,28},{16,24},{20,4},{24,16},{28,12},{1,9},{5... | collective-permute-start | bytes 589832 | tf_op jit(solution)/shard_map/ppermute | solution.py:35
  9.2 6.9 %collective-permute-start.7 = (bf16[32,3072]{1,0:T(8,128)(2,1)S(1)}, bf16[32,3072]{1,0:T(8,128)(2,1)S(1)}, u32[]{:S(2)}, u32[]{:S(2)}) collective-permute-start(bf16[32,3072]{1,0:T(8,128)(2,1)S(1)} %get-tuple-element.60), channel_id=1, source_target_pairs={{0,16},{4,12},{8,24},{12,4},{16,0},{20,28},{24,8},{28,20},{1,17},{... | collective-permute-start | bytes 589832 | tf_op jit(solution)/shard_map/ppermute | solution.py:35
  12.5 7.5 %collective-permute-start.3 = (bf16[16,3072]{1,0:T(8,128)(2,1)S(1)}, bf16[16,3072]{1,0:T(8,128)(2,1)S(1)}, u32[]{:S(2)}, u32[]{:S(2)}) collective-permute-start(bf16[16,3072]{1,0:T(8,128)(2,1)S(1)} %get-tuple-element.55), channel_id=1, source_target_pairs={{0,24},{4,28},{8,16},{12,20},{16,8},{20,12},{24,0},{28,4},{1,25},{... | collective-permute-start | bytes 294920 | tf_op jit(solution)/shard_map/ppermute | solution.py:35
  15.9 5.0 %collective-permute-start.4 = (bf16[16,3072]{1,0:T(8,128)(2,1)S(1)}, bf16[16,3072]{1,0:T(8,128)(2,1)S(1)}, u32[]{:S(2)}, u32[]{:S(2)}) collective-permute-start(bf16[16,3072]{1,0:T(8,128)(2,1)S(1)} %get-tuple-element.56), channel_id=1, source_target_pairs={{0,28},{4,24},{8,20},{12,16},{16,12},{20,8},{24,4},{28,0},{1,29},{... | collective-permute-start | bytes 294920 | tf_op jit(solution)/shard_map/ppermute | solution.py:35
  15.9 5.8 %collective-permute-start.5 = (bf16[16,3072]{1,0:T(8,128)(2,1)S(1)}, bf16[16,3072]{1,0:T(8,128)(2,1)S(1)}, u32[]{:S(2)}, u32[]{:S(2)}) collective-permute-start(bf16[16,3072]{1,0:T(8,128)(2,1)S(1)} %get-tuple-element.58), channel_id=1, source_target_pairs={{0,4},{4,0},{8,12},{12,8},{16,20},{20,16},{24,28},{28,24},{1,5},{5... | collective-permute-start | bytes 294920 | tf_op jit(solution)/shard_map/ppermute | solution.py:23
  17.2 4.8 %collective-permute-start.8 = (bf16[16,3072]{1,0:T(8,128)(2,1)S(1)}, bf16[16,3072]{1,0:T(8,128)(2,1)S(1)}, u32[]{:S(2)}, u32[]{:S(2)}) collective-permute-start(bf16[16,3072]{1,0:T(8,128)(2,1)S(1)} %get-tuple-element.61), channel_id=1, source_target_pairs={{0,8},{4,20},{8,0},{12,28},{16,24},{20,4},{24,16},{28,12},{1,9},{5... | collective-permute-start | bytes 294920 | tf_op jit(solution)/shard_map/ppermute | solution.py:35
  18.7 4.4 %collective-permute-start.9 = (bf16[16,3072]{1,0:T(8,128)(2,1)S(1)}, bf16[16,3072]{1,0:T(8,128)(2,1)S(1)}, u32[]{:S(2)}, u32[]{:S(2)}) collective-permute-start(bf16[16,3072]{1,0:T(8,128)(2,1)S(1)} %get-tuple-element.62), channel_id=1, source_target_pairs={{0,12},{4,16},{8,4},{12,24},{16,28},{20,0},{24,20},{28,8},{1,13},{... | collective-permute-start | bytes 294920 | tf_op jit(solution)/shard_map/ppermute | solution.py:35
  20.0 4.6 %collective-permute-start.10 = (bf16[16,3072]{1,0:T(8,128)(2,1)S(1)}, bf16[16,3072]{1,0:T(8,128)(2,1)S(1)}, u32[]{:S(2)}, u32[]{:S(2)}) collective-permute-start(bf16[16,3072]{1,0:T(8,128)(2,1)S(1)} %get-tuple-element.63), channel_id=1, source_target_pairs={{0,16},{4,12},{8,24},{12,4},{16,0},{20,28},{24,8},{28,20},{1,17},{... | collective-permute-start | bytes 294920 | tf_op jit(solution)/shard_map/ppermute | solution.py:35
  20.9 4.5 %collective-permute-start.11 = (bf16[16,3072]{1,0:T(8,128)(2,1)S(1)}, bf16[16,3072]{1,0:T(8,128)(2,1)S(1)}, u32[]{:S(2)}, u32[]{:S(2)}) collective-permute-start(bf16[16,3072]{1,0:T(8,128)(2,1)S(1)} %get-tuple-element.64), channel_id=1, source_target_pairs={{0,20},{4,8},{8,28},{12,0},{16,4},{20,24},{24,12},{28,16},{1,21},{... | collective-permute-start | bytes 294920 | tf_op jit(solution)/shard_map/ppermute | solution.py:35
  25.8 5.9 %collective-permute-start.12 = (bf16[32,768]{1,0:T(8,128)(2,1)S(1)}, bf16[32,768]{1,0:T(8,128)(2,1)S(1)}, u32[]{:S(2)}, u32[]{:S(2)}) collective-permute-start(bf16[32,768]{1,0:T(8,128)(2,1)S(1)} %get-tuple-element.66), channel_id=1, source_target_pairs={{0,1},{1,2},{2,3},{3,0},{4,5},{5,6},{6,7},{7,4},{8,9},{9,10},{10,1... | collective-permute-start | bytes 147464 | tf_op jit(solution)/shard_map/ppermute | solution.py:29
  27.4 6.4 %collective-permute-start.13 = (bf16[32,768]{1,0:T(8,128)(2,1)S(1)}, bf16[32,768]{1,0:T(8,128)(2,1)S(1)}, u32[]{:S(2)}, u32[]{:S(2)}) collective-permute-start(bf16[32,768]{1,0:T(8,128)(2,1)S(1)} %get-tuple-element.67), channel_id=1, source_target_pairs={{0,2},{1,3},{2,0},{3,1},{4,6},{5,7},{6,4},{7,5},{8,10},{9,11},{10,... | collective-permute-start | bytes 147464 | tf_op jit(solution)/shard_map/ppermute | solution.py:29
  30.0 4.2 %collective-permute-start.14 = (bf16[32,768]{1,0:T(8,128)(2,1)S(1)}, bf16[32,768]{1,0:T(8,128)(2,1)S(1)}, u32[]{:S(2)}, u32[]{:S(2)}) collective-permute-start(bf16[32,768]{1,0:T(8,128)(2,1)S(1)} %get-tuple-element.68), channel_id=1, source_target_pairs={{0,3},{1,0},{2,1},{3,2},{4,7},{5,4},{6,5},{7,6},{8,11},{9,8},{10,9... | collective-permute-start | bytes 147464 | tf_op jit(solution)/shard_map/ppermute | solution.py:29

commit v6 on v5

--- a/solution.py
+++ b/solution.py
@@ -9,6 +9,7 @@
 
 epsilon = 1e-05
 LANES = 128
+INNER_ORDER = ((1, 2, 3, 0), (2, 3, 0, 1), (3, 0, 1, 2))
 TOKEN_COPIES = 4
 NT = (((1,), (1,)), ((), ()))
 VMEM = pl.BlockSpec(memory_space=pltpu.VMEM)
@@ -23,10 +24,20 @@
     return lax.ppermute(value, axis, [(place, place ^ distance) for place in range(count)])
 
 
-def turn(value, distance):
-    count = lax.axis_size("inner")
-    pairs = [(place, (place + distance) % count) for place in range(count)]
-    return lax.ppermute(value, "inner", pairs)
+def inner_targets(count):
+    if count == len(INNER_ORDER[0]):
+        return INNER_ORDER
+    return tuple(
+        tuple((place + k) % count for place in range(count)) for k in range(1, count)
+    )
+
+
+def target_of(member, targets):
+    return sum(jnp.where(member == place, target, 0) for place, target in enumerate(targets))
+
+
+def turn(value, targets):
+    return lax.ppermute(value, "inner", list(enumerate(targets)))
 
 
 def visit(value, step, cross):
@@ -329,7 +340,7 @@
     )(high, low, *blocks)
 
 
-def close_kernel(count, member_ref, tokens_ref, high_ref, low_ref, begun_ref, *refs):
+def close_kernel(count, targets, member_ref, tokens_ref, high_ref, low_ref, begun_ref, *refs):
     blocks, outs, every_ref, total_ref = refs[:count], refs[count:-2], refs[-2], refs[-1]
     every = gathered(blocks, every_ref)
     total = begun_ref[...] + jnp.dot(low_ref[...], every, preferred_element_type=jnp.float32)
@@ -339,7 +350,8 @@
         return
     part = outs[0].shape[1]
     for k, out_ref in enumerate(outs):
-        columns = pl.ds(pl.multiple_of(lax.rem(member_ref[0] + k, len(outs)) * part, LANES), part)
+        place = target_of(member_ref[0], targets[k - 1]) if k else member_ref[0]
+        columns = pl.ds(pl.multiple_of(place * part, LANES), part)
         value = total_ref[:, columns]
         if k == 0:
             value = value + tokens_ref[:, columns].astype(jnp.float32)
@@ -352,12 +364,13 @@
     rows, width = begun.shape
     part = width // inner_count
     whole = part % LANES != 0
+    targets = inner_targets(inner_count)
     kinds = [jnp.float32] + [jnp.bfloat16] * (inner_count - 1)
     shapes = [shaped(rows, part, kind) for kind in kinds]
     if whole:
         shapes = [shaped(rows, width, jnp.float32)]
     outs = pl.pallas_call(
-        functools.partial(close_kernel, count),
+        functools.partial(close_kernel, count, targets),
         out_shape=shapes,
         in_specs=[SMEM] + [VMEM] * (4 + count),
         out_specs=[VMEM] * len(shapes),
@@ -374,7 +387,7 @@
     total = outs[0] + tokens.astype(jnp.float32)
     outs = [lax.dynamic_slice_in_dim(total, member * part, part, 1)]
     for k in range(1, inner_count):
-        place = lax.rem(member + k, inner_count)
+        place = target_of(member, targets[k - 1])
         outs.append(lax.dynamic_slice_in_dim(rounded, place * part, part, 1))
     return outs
 
@@ -451,15 +464,17 @@
     high_a, low_a, high_b, low_b = mix(
         section, normed, slots, names, router_rows, early, late, per_expert
     )
-    here, beside, *away = run_expert([message, away], turned_in, down, 2)
-    results = run_expert(arrived, turned_in, down, 2, (here,))
+    here, beside = run_expert([message], turned_in, down, 2)
+    beside = trade(beside, "section", 1)
+    away = run_expert([away], turned_in, down, 2, (here,))
+    results = run_expert(arrived, turned_in, down, 2, (away[0],))
     away = [visit(value, (far, far), cross) for cross, value in enumerate(away)]
-    begun = begin(high_a, low_a, [*away, here, trade(beside, "section", 1)])
+    begun = begin(high_a, low_a, [*away, here, beside])
     results = [visit(value, steps[j // 2], j % 2) for j, value in enumerate(results)]
     split = close(high_b, low_b, begun, results, own, member, inner_count)
-    pieces = {k: turn(split[k], k) for k in range(1, inner_count)}
-    pieces[0] = split[0]
-    return finish([pieces[k] for k in range(inner_count)], micro, row_count)
+    targets = inner_targets(inner_count)
+    pieces = [split[0]] + [turn(value, order) for value, order in zip(split[1:], targets)]
+    return finish(pieces, micro, row_count)
 
 
 def solution(mesh):

time: 35 us -> 34.5 us (0.986)
  waiting for transfers between devices: 8.86 us -> 7.85 us
  Pallas kernels: 7.65 us -> 8.6 us
  starting transfers between devices: 18.2 us -> 17.8 us
    ppermute x9, waiting for transfers between devices: 5.93 us -> 4.86 us  [visit(): return lax.ppermute(value, 'section', pairs)]
    pallas_call x2 -> x3, Pallas kernels: 2.06 us -> 3.01 us  [run_expert(): pl.pallas_call(functools.partial(expert_kernel, count, len(after)), out_s...]
  transfers between devices with their start and end apart: 15 -> 15, of which waited for: 8 -> 8; matrix products, arithmetic and copies ran while one was open for 0% -> 0% of each run, Pallas kernels for 18% -> 21%
where the time goes in v6:
time: 34.5 us; the launch traced here: 34.3 us
  starting transfers between devices  17.8 us (52%)
  Pallas kernels  8.6 us (25%)
  waiting for transfers between devices  7.85 us (23%)
    ppermute x9, starting transfers between devices, visit(): return lax.ppermute(value, 'section', pairs)  11.7 us
    ppermute x3, starting transfers between devices, turn(): return lax.ppermute(value, 'inner', list(enumerate(targets)))  5.57 us
    ppermute x9, waiting for transfers between devices, visit(): return lax.ppermute(value, 'section', pairs)  4.86 us
    pallas_call x3, Pallas kernels, run_expert(): pl.pallas_call(functools.partial(expert_kernel, count, len(after)), out_s...  3.01 us
    ppermute x3, waiting for transfers between devices, turn(): return lax.ppermute(value, 'inner', list(enumerate(targets)))  2.95 us
    pallas_call x1, Pallas kernels, load_weights(): pl.pallas_call(functools.partial(load_kernel, count, steps, per_expert),...  2.46 us
    pallas_call x1, Pallas kernels, own_part(): pl.pallas_call(functools.partial(own_kernel, steps, per_expert), out_shap...  1.26 us
  transfers between devices with their start and end apart: 15, of which 8 were waited for; matrix products, arithmetic and copies ran while one was open for 0% of the time, Pallas kernels for 21%

profile of v6, /device:TPU:0, one launch (start us, length us, event | category | flops | bytes accessed | tf_op | source)
XLA Modules:
  0.0 34.3 jit_solution(12448757717627408057)
XLA Ops:
  0.0 0.5 %collective-permute-start = (bf16[32,3072]{1,0:T(8,128)(2,1)}, bf16[32,3072]{1,0:T(8,128)(2,1)S(1)}, u32[]{:S(2)}, u32[]{:S(2)}) collective-permute-start(bf16[32,3072]{1,0:T(8,128)(2,1)} %bitcast.10), channel_id=1, source_target_pairs={{0,4},{4,0},{8,12},{12,8},{16,20},{20,16},{24,28},{28,24},{1,5},{5... | collective-permute-start | bytes 589832 | tf_op jit(solution)/shard_map/ppermute | solution.py:24
  0.5 0.1 collective-permute-start.1
  0.5 1.3 %own_part.1 = (bf16[16,3072]{1,0:T(8,128)(2,1)S(1)}, bf16[16,3072]{1,0:T(8,128)(2,1)S(1)}, bf16[32,3072]{1,0:T(8,128)(2,1)S(1)}, f32[1,3072]{1,0:T(1,128)S(1)}, ...) custom-call(s32[1]{0:T(128)} %bitcast.1.section_ref, bf16[32,3072]{1,0:T(8,128)(2,1)} %bitcast.11, ...), custom_call_target="tpu_custom_call" | custom-call | tf_op jit(solution)/shard_map/own_part/pallas_call | solution.py:139
  1.8 0.4 %other_part.1 = (bf16[32,3072]{1,0:T(8,128)(2,1)S(1)}, bf16[32,3072]{1,0:T(8,128)(2,1)S(1)}, bf16[32,3072]{1,0:T(8,128)(2,1)S(1)}, f32[8,32]{1,0:T(8,128)S(1)}) custom-call(s32[1]{0:T(128)} %bitcast.1.section_ref, bf16[32,3072]{1,0:T(8,128)(2,1)S(1)} %collective-permute-done.other_ref, s32[2,2,16]{2,1,0:T(2,128)S(1)} %collective-permute-done.1.named_ref, ...), custom_call_target="tpu_custom_call" | custom-call | tf_op jit(solution)/shard_map/other_part/pallas_call | solution.py:168
  2.2 3.9 %collective-permute-start.2 = (bf16[32,3072]{1,0:T(8,128)(2,1)S(1)}, bf16[32,3072]{1,0:T(8,128)(2,1)S(1)}, u32[]{:S(2)}, u32[]{:S(2)}) collective-permute-start(bf16[32,3072]{1,0:T(8,128)(2,1)S(1)} %get-tuple-element.53), channel_id=1, source_target_pairs={{0,24},{4,28},{8,16},{12,20},{16,8},{20,12},{24,0},{28,4},{1,25},{... | collective-permute-start | bytes 589832 | tf_op jit(solution)/shard_map/ppermute | solution.py:46
  6.1 2.5 %load_weights.1 = (bf16[3072,512]{1,0:T(8,128)(2,1)S(1)}, bf16[8,3072]{1,0:T(8,128)(2,1)S(1)}, bf16[256,3072]{1,0:T(8,128)(2,1)S(1)}, bf16[32,3072]{1,0:T(8,128)(2,1)S(1)}, bf16[32,3072]{1,0:T(8,128)(2,1)S(1)}) custom-call(s32[1]{0:T(128)} %bitcast.1.section_ref, bf16[512,3072]{1,0:T(8,128)(2,1)} %bitcast.8, bf16[8,3072]{1,0:T(8,128)(2,1)} %bitcast.12, ...), custom_call_target="tpu_custom_call" | custom-call | tf_op jit(solution)/shard_map/load_weights/pallas_call | solution.py:273
  8.6 0.6 %collective-permute-start.6 = (bf16[32,3072]{1,0:T(8,128)(2,1)S(1)}, bf16[32,3072]{1,0:T(8,128)(2,1)S(1)}, u32[]{:S(2)}, u32[]{:S(2)}) collective-permute-start(bf16[32,3072]{1,0:T(8,128)(2,1)S(1)} %get-tuple-element.59), channel_id=1, source_target_pairs={{0,8},{4,20},{8,0},{12,28},{16,24},{20,4},{24,16},{28,12},{1,9},{5... | collective-permute-start | bytes 589832 | tf_op jit(solution)/shard_map/ppermute | solution.py:46
  9.3 1.0 %expert.3 = (bf16[16,3072]{1,0:T(8,128)(2,1)S(1)}, bf16[16,3072]{1,0:T(8,128)(2,1)S(1)}) custom-call(bf16[3072,512]{1,0:T(8,128)(2,1)S(1)} %get-tuple-element.51.in_ref, bf16[256,3072]{1,0:T(8,128)(2,1)S(1)} %get-tuple-element.52.down_ref, bf16[32,3072]{1,0:T(8,128)(2,1)S(1)} %get-tuple-element.54.refs_0_), custom_call_target="tpu_custom_call" | custom-call | tf_op jit(solution)/shard_map/expert/pallas_call | solution.py:304
  10.2 0.1 collective-permute-start.5
  10.3 1.1 %collective-permute-done.2.refs_0_ = bf16[32,3072]{1,0:T(8,128)(2,1)S(1)} collective-permute-done((bf16[32,3072]{1,0:T(8,128)(2,1)S(1)}, bf16[32,3072]{1,0:T(8,128)(2,1)S(1)}, u32[]{:S(2)}, u32[]{:S(2)}) %collective-permute-start.2) | collective-permute-done | bytes 196640 | tf_op jit(solution)/shard_map/ppermute | solution.py:46
  11.4 1.0 %expert.4 = (bf16[16,3072]{1,0:T(8,128)(2,1)S(1)}, bf16[16,3072]{1,0:T(8,128)(2,1)S(1)}) custom-call(bf16[3072,512]{1,0:T(8,128)(2,1)S(1)} %get-tuple-element.51.in_ref, bf16[256,3072]{1,0:T(8,128)(2,1)S(1)} %get-tuple-element.52.down_ref, bf16[32,3072]{1,0:T(8,128)(2,1)S(1)} %collective-permute-done.2.refs_0_, ...), custom_call_target="tpu_custom_call" | custom-call | tf_op jit(solution)/shard_map/expert/pallas_call | solution.py:304
  12.4 1.9 %collective-permute-start.4 = (bf16[16,3072]{1,0:T(8,128)(2,1)S(1)}, bf16[16,3072]{1,0:T(8,128)(2,1)S(1)}, u32[]{:S(2)}, u32[]{:S(2)}) collective-permute-start(bf16[16,3072]{1,0:T(8,128)(2,1)S(1)} %get-tuple-element.57), channel_id=1, source_target_pairs={{0,28},{4,24},{8,20},{12,16},{16,12},{20,8},{24,4},{28,0},{1,29},{... | collective-permute-start | bytes 294920 | tf_op jit(solution)/shard_map/ppermute | solution.py:46
  14.4 1.6 %collective-permute-start.3 = (bf16[16,3072]{1,0:T(8,128)(2,1)S(1)}, bf16[16,3072]{1,0:T(8,128)(2,1)S(1)}, u32[]{:S(2)}, u32[]{:S(2)}) collective-permute-start(bf16[16,3072]{1,0:T(8,128)(2,1)S(1)} %get-tuple-element.56.refs_2_), channel_id=1, source_target_pairs={{0,24},{4,28},{8,16},{12,20},{16,8},{20,12},{24,0},{28,4},{1,25},{... | collective-permute-start | bytes 294920 | tf_op jit(solution)/shard_map/ppermute | solution.py:46
  15.9 1.0 %expert.5 = (bf16[16,3072]{1,0:T(8,128)(2,1)S(1)}, bf16[16,3072]{1,0:T(8,128)(2,1)S(1)}, bf16[16,3072]{1,0:T(8,128)(2,1)S(1)}, bf16[16,3072]{1,0:T(8,128)(2,1)S(1)}) custom-call(bf16[3072,512]{1,0:T(8,128)(2,1)S(1)} %get-tuple-element.51.in_ref, bf16[256,3072]{1,0:T(8,128)(2,1)S(1)} %get-tuple-element.52.down_ref, ...), custom_call_target="tpu_custom_call" | custom-call | tf_op jit(solution)/shard_map/expert/pallas_call | solution.py:304
  17.0 1.4 %collective-permute-start.8 = (bf16[16,3072]{1,0:T(8,128)(2,1)S(1)}, bf16[16,3072]{1,0:T(8,128)(2,1)S(1)}, u32[]{:S(2)}, u32[]{:S(2)}) collective-permute-start(bf16[16,3072]{1,0:T(8,128)(2,1)S(1)} %get-tuple-element.61), channel_id=1, source_target_pairs={{0,8},{4,20},{8,0},{12,28},{16,24},{20,4},{24,16},{28,12},{1,9},{5... | collective-permute-start | bytes 294920 | tf_op jit(solution)/shard_map/ppermute | solution.py:46
  18.4 1.2 %collective-permute-start.9 = (bf16[16,3072]{1,0:T(8,128)(2,1)S(1)}, bf16[16,3072]{1,0:T(8,128)(2,1)S(1)}, u32[]{:S(2)}, u32[]{:S(2)}) collective-permute-start(bf16[16,3072]{1,0:T(8,128)(2,1)S(1)} %get-tuple-element.62), channel_id=1, source_target_pairs={{0,12},{4,16},{8,4},{12,24},{16,28},{20,0},{24,20},{28,8},{1,13},{... | collective-permute-start | bytes 294920 | tf_op jit(solution)/shard_map/ppermute | solution.py:46
  19.6 0.3 %collective-permute-start.10 = (bf16[16,3072]{1,0:T(8,128)(2,1)S(1)}, bf16[16,3072]{1,0:T(8,128)(2,1)S(1)}, u32[]{:S(2)}, u32[]{:S(2)}) collective-permute-start(bf16[16,3072]{1,0:T(8,128)(2,1)S(1)} %get-tuple-element.63), channel_id=1, source_target_pairs={{0,16},{4,12},{8,24},{12,4},{16,0},{20,28},{24,8},{28,20},{1,17},{... | collective-permute-start | bytes 294920 | tf_op jit(solution)/shard_map/ppermute | solution.py:46
  20.0 0.6 %collective-permute-start.11 = (bf16[16,3072]{1,0:T(8,128)(2,1)S(1)}, bf16[16,3072]{1,0:T(8,128)(2,1)S(1)}, u32[]{:S(2)}, u32[]{:S(2)}) collective-permute-start(bf16[16,3072]{1,0:T(8,128)(2,1)S(1)} %get-tuple-element.64), channel_id=1, source_target_pairs={{0,20},{4,8},{8,28},{12,0},{16,4},{20,24},{24,12},{28,16},{1,21},{... | collective-permute-start | bytes 294920 | tf_op jit(solution)/shard_map/ppermute | solution.py:46
  20.6 0.3 mix.1
  20.9 0.2 begin.1.begun_ref
  21.1 0.6 %collective-permute-done.8.refs_0_ = bf16[16,3072]{1,0:T(8,128)(2,1)S(1)} collective-permute-done((bf16[16,3072]{1,0:T(8,128)(2,1)S(1)}, bf16[16,3072]{1,0:T(8,128)(2,1)S(1)}, u32[]{:S(2)}, u32[]{:S(2)}) %collective-permute-start.8) | collective-permute-done | bytes 98336 | tf_op jit(solution)/shard_map/ppermute | solution.py:46
  21.7 1.3 %collective-permute-done.9.refs_1_ = bf16[16,3072]{1,0:T(8,128)(2,1)S(1)} collective-permute-done((bf16[16,3072]{1,0:T(8,128)(2,1)S(1)}, bf16[16,3072]{1,0:T(8,128)(2,1)S(1)}, u32[]{:S(2)}, u32[]{:S(2)}) %collective-permute-start.9) | collective-permute-done | bytes 98336 | tf_op jit(solution)/shard_map/ppermute | solution.py:46
  23.0 1.2 %collective-permute-done.10.refs_2_ = bf16[16,3072]{1,0:T(8,128)(2,1)S(1)} collective-permute-done((bf16[16,3072]{1,0:T(8,128)(2,1)S(1)}, bf16[16,3072]{1,0:T(8,128)(2,1)S(1)}, u32[]{:S(2)}, u32[]{:S(2)}) %collective-permute-start.10) | collective-permute-done | bytes 98336 | tf_op jit(solution)/shard_map/ppermute | solution.py:46
  24.2 0.6 %collective-permute-done.11.refs_3_ = bf16[16,3072]{1,0:T(8,128)(2,1)S(1)} collective-permute-done((bf16[16,3072]{1,0:T(8,128)(2,1)S(1)}, bf16[16,3072]{1,0:T(8,128)(2,1)S(1)}, u32[]{:S(2)}, u32[]{:S(2)}) %collective-permute-start.11) | collective-permute-done | bytes 98336 | tf_op jit(solution)/shard_map/ppermute | solution.py:46
  24.9 0.3 close.1
  25.2 1.6 %collective-permute-start.12 = (bf16[32,768]{1,0:T(8,128)(2,1)S(1)}, bf16[32,768]{1,0:T(8,128)(2,1)S(1)}, u32[]{:S(2)}, u32[]{:S(2)}) collective-permute-start(bf16[32,768]{1,0:T(8,128)(2,1)S(1)} %get-tuple-element.66), channel_id=1, source_target_pairs={{0,1},{1,2},{2,3},{3,0},{4,5},{5,6},{6,7},{7,4},{8,9},{9,10},{10,1... | collective-permute-start | bytes 147464 | tf_op jit(solution)/shard_map/ppermute | solution.py:40
  26.8 2.6 %collective-permute-start.13 = (bf16[32,768]{1,0:T(8,128)(2,1)S(1)}, bf16[32,768]{1,0:T(8,128)(2,1)S(1)}, u32[]{:S(2)}, u32[]{:S(2)}) collective-permute-start(bf16[32,768]{1,0:T(8,128)(2,1)S(1)} %get-tuple-element.67), channel_id=1, source_target_pairs={{0,2},{1,3},{2,0},{3,1},{4,6},{5,7},{6,4},{7,5},{8,10},{9,11},{10,... | collective-permute-start | bytes 147464 | tf_op jit(solution)/shard_map/ppermute | solution.py:40
  29.4 1.3 %collective-permute-start.14 = (bf16[32,768]{1,0:T(8,128)(2,1)S(1)}, bf16[32,768]{1,0:T(8,128)(2,1)S(1)}, u32[]{:S(2)}, u32[]{:S(2)}) collective-permute-start(bf16[32,768]{1,0:T(8,128)(2,1)S(1)} %get-tuple-element.68), channel_id=1, source_target_pairs={{0,3},{1,0},{2,1},{3,2},{4,7},{5,4},{6,5},{7,6},{8,11},{9,8},{10,9... | collective-permute-start | bytes 147464 | tf_op jit(solution)/shard_map/ppermute | solution.py:40
  30.7 0.4 %collective-permute-done.12.refs_1_ = bf16[32,768]{1,0:T(8,128)(2,1)S(1)} collective-permute-done((bf16[32,768]{1,0:T(8,128)(2,1)S(1)}, bf16[32,768]{1,0:T(8,128)(2,1)S(1)}, u32[]{:S(2)}, u32[]{:S(2)}) %collective-permute-start.12) | collective-permute-done | bytes 49184 | tf_op jit(solution)/shard_map/ppermute | solution.py:40
  31.1 2.2 %collective-permute-done.13.refs_2_ = bf16[32,768]{1,0:T(8,128)(2,1)S(1)} collective-permute-done((bf16[32,768]{1,0:T(8,128)(2,1)S(1)}, bf16[32,768]{1,0:T(8,128)(2,1)S(1)}, u32[]{:S(2)}, u32[]{:S(2)}) %collective-permute-start.13) | collective-permute-done | bytes 49184 | tf_op jit(solution)/shard_map/ppermute | solution.py:40
  33.4 0.3 collective-permute-done.14.refs_3_
  33.7 0.6 %finish.1 = bf16[2,16,768]{2,1,0:T(8,128)(2,1)} custom-call(f32[32,768]{1,0:T(8,128)S(1)} %get-tuple-element.65.refs_0_, bf16[32,768]{1,0:T(8,128)(2,1)S(1)} %collective-permute-done.12.refs_1_, bf16[32,768]{1,0:T(8,128)(2,1)S(1)} %collective-permute-done.13.refs_2_, bf16[32,768]{1,0:T(8,128)(2,1)S(1)} %collective-permute-done.14.refs_3_), custom_call_target="tpu_custom_call" | custom-call | tf_op jit(solution)/shard_map/finish/pallas_call | solution.py:407
  (8 shorter events, 0.1 us)
Async XLA Ops:
  0.0 1.8 %collective-permute-start = (bf16[32,3072]{1,0:T(8,128)(2,1)}, bf16[32,3072]{1,0:T(8,128)(2,1)S(1)}, u32[]{:S(2)}, u32[]{:S(2)}) collective-permute-start(bf16[32,3072]{1,0:T(8,128)(2,1)} %bitcast.10), channel_id=1, source_target_pairs={{0,4},{4,0},{8,12},{12,8},{16,20},{20,16},{24,28},{28,24},{1,5},{5... | collective-permute-start | bytes 589832 | tf_op jit(solution)/shard_map/ppermute | solution.py:24
  0.5 1.4 %collective-permute-start.1 = (s32[2,2,16]{2,1,0:T(2,128)}, s32[2,2,16]{2,1,0:T(2,128)S(1)}, u32[]{:S(2)}, u32[]{:S(2)}) collective-permute-start(s32[2,2,16]{2,1,0:T(2,128)} %bitcast.14), channel_id=1, source_target_pairs={{0,4},{4,0},{8,12},{12,8},{16,20},{20,16},{24,28},{28,24},{1,5},{5... | collective-permute-start | bytes 776 | tf_op jit(solution)/shard_map/ppermute | solution.py:24
  2.2 9.2 %collective-permute-start.2 = (bf16[32,3072]{1,0:T(8,128)(2,1)S(1)}, bf16[32,3072]{1,0:T(8,128)(2,1)S(1)}, u32[]{:S(2)}, u32[]{:S(2)}) collective-permute-start(bf16[32,3072]{1,0:T(8,128)(2,1)S(1)} %get-tuple-element.53), channel_id=1, source_target_pairs={{0,24},{4,28},{8,16},{12,20},{16,8},{20,12},{24,0},{28,4},{1,25},{... | collective-permute-start | bytes 589832 | tf_op jit(solution)/shard_map/ppermute | solution.py:46
  8.6 7.3 %collective-permute-start.6 = (bf16[32,3072]{1,0:T(8,128)(2,1)S(1)}, bf16[32,3072]{1,0:T(8,128)(2,1)S(1)}, u32[]{:S(2)}, u32[]{:S(2)}) collective-permute-start(bf16[32,3072]{1,0:T(8,128)(2,1)S(1)} %get-tuple-element.59), channel_id=1, source_target_pairs={{0,8},{4,20},{8,0},{12,28},{16,24},{20,4},{24,16},{28,12},{1,9},{5... | collective-permute-start | bytes 589832 | tf_op jit(solution)/shard_map/ppermute | solution.py:46
  9.2 6.7 %collective-permute-start.7 = (bf16[32,3072]{1,0:T(8,128)(2,1)S(1)}, bf16[32,3072]{1,0:T(8,128)(2,1)S(1)}, u32[]{:S(2)}, u32[]{:S(2)}) collective-permute-start(bf16[32,3072]{1,0:T(8,128)(2,1)S(1)} %get-tuple-element.60), channel_id=1, source_target_pairs={{0,16},{4,12},{8,24},{12,4},{16,0},{20,28},{24,8},{28,20},{1,17},{... | collective-permute-start | bytes 589832 | tf_op jit(solution)/shard_map/ppermute | solution.py:46
  10.2 9.4 %collective-permute-start.5 = (bf16[16,3072]{1,0:T(8,128)(2,1)S(1)}, bf16[16,3072]{1,0:T(8,128)(2,1)S(1)}, u32[]{:S(2)}, u32[]{:S(2)}) collective-permute-start(bf16[16,3072]{1,0:T(8,128)(2,1)S(1)} %get-tuple-element.58), channel_id=1, source_target_pairs={{0,4},{4,0},{8,12},{12,8},{16,20},{20,16},{24,28},{28,24},{1,5},{5... | collective-permute-start | bytes 294920 | tf_op jit(solution)/shard_map/ppermute | solution.py:24
  12.4 7.5 %collective-permute-start.4 = (bf16[16,3072]{1,0:T(8,128)(2,1)S(1)}, bf16[16,3072]{1,0:T(8,128)(2,1)S(1)}, u32[]{:S(2)}, u32[]{:S(2)}) collective-permute-start(bf16[16,3072]{1,0:T(8,128)(2,1)S(1)} %get-tuple-element.57), channel_id=1, source_target_pairs={{0,28},{4,24},{8,20},{12,16},{16,12},{20,8},{24,4},{28,0},{1,29},{... | collective-permute-start | bytes 294920 | tf_op jit(solution)/shard_map/ppermute | solution.py:46
  14.4 6.5 %collective-permute-start.3 = (bf16[16,3072]{1,0:T(8,128)(2,1)S(1)}, bf16[16,3072]{1,0:T(8,128)(2,1)S(1)}, u32[]{:S(2)}, u32[]{:S(2)}) collective-permute-start(bf16[16,3072]{1,0:T(8,128)(2,1)S(1)} %get-tuple-element.56.refs_2_), channel_id=1, source_target_pairs={{0,24},{4,28},{8,16},{12,20},{16,8},{20,12},{24,0},{28,4},{1,25},{... | collective-permute-start | bytes 294920 | tf_op jit(solution)/shard_map/ppermute | solution.py:46
  17.0 4.7 %collective-permute-start.8 = (bf16[16,3072]{1,0:T(8,128)(2,1)S(1)}, bf16[16,3072]{1,0:T(8,128)(2,1)S(1)}, u32[]{:S(2)}, u32[]{:S(2)}) collective-permute-start(bf16[16,3072]{1,0:T(8,128)(2,1)S(1)} %get-tuple-element.61), channel_id=1, source_target_pairs={{0,8},{4,20},{8,0},{12,28},{16,24},{20,4},{24,16},{28,12},{1,9},{5... | collective-permute-start | bytes 294920 | tf_op jit(solution)/shard_map/ppermute | solution.py:46
  18.4 4.7 %collective-permute-start.9 = (bf16[16,3072]{1,0:T(8,128)(2,1)S(1)}, bf16[16,3072]{1,0:T(8,128)(2,1)S(1)}, u32[]{:S(2)}, u32[]{:S(2)}) collective-permute-start(bf16[16,3072]{1,0:T(8,128)(2,1)S(1)} %get-tuple-element.62), channel_id=1, source_target_pairs={{0,12},{4,16},{8,4},{12,24},{16,28},{20,0},{24,20},{28,8},{1,13},{... | collective-permute-start | bytes 294920 | tf_op jit(solution)/shard_map/ppermute | solution.py:46
  19.6 4.6 %collective-permute-start.10 = (bf16[16,3072]{1,0:T(8,128)(2,1)S(1)}, bf16[16,3072]{1,0:T(8,128)(2,1)S(1)}, u32[]{:S(2)}, u32[]{:S(2)}) collective-permute-start(bf16[16,3072]{1,0:T(8,128)(2,1)S(1)} %get-tuple-element.63), channel_id=1, source_target_pairs={{0,16},{4,12},{8,24},{12,4},{16,0},{20,28},{24,8},{28,20},{1,17},{... | collective-permute-start | bytes 294920 | tf_op jit(solution)/shard_map/ppermute | solution.py:46
  20.0 4.9 %collective-permute-start.11 = (bf16[16,3072]{1,0:T(8,128)(2,1)S(1)}, bf16[16,3072]{1,0:T(8,128)(2,1)S(1)}, u32[]{:S(2)}, u32[]{:S(2)}) collective-permute-start(bf16[16,3072]{1,0:T(8,128)(2,1)S(1)} %get-tuple-element.64), channel_id=1, source_target_pairs={{0,20},{4,8},{8,28},{12,0},{16,4},{20,24},{24,12},{28,16},{1,21},{... | collective-permute-start | bytes 294920 | tf_op jit(solution)/shard_map/ppermute | solution.py:46
  25.2 5.9 %collective-permute-start.12 = (bf16[32,768]{1,0:T(8,128)(2,1)S(1)}, bf16[32,768]{1,0:T(8,128)(2,1)S(1)}, u32[]{:S(2)}, u32[]{:S(2)}) collective-permute-start(bf16[32,768]{1,0:T(8,128)(2,1)S(1)} %get-tuple-element.66), channel_id=1, source_target_pairs={{0,1},{1,2},{2,3},{3,0},{4,5},{5,6},{6,7},{7,4},{8,9},{9,10},{10,1... | collective-permute-start | bytes 147464 | tf_op jit(solution)/shard_map/ppermute | solution.py:40
  26.8 6.6 %collective-permute-start.13 = (bf16[32,768]{1,0:T(8,128)(2,1)S(1)}, bf16[32,768]{1,0:T(8,128)(2,1)S(1)}, u32[]{:S(2)}, u32[]{:S(2)}) collective-permute-start(bf16[32,768]{1,0:T(8,128)(2,1)S(1)} %get-tuple-element.67), channel_id=1, source_target_pairs={{0,2},{1,3},{2,0},{3,1},{4,6},{5,7},{6,4},{7,5},{8,10},{9,11},{10,... | collective-permute-start | bytes 147464 | tf_op jit(solution)/shard_map/ppermute | solution.py:40
  29.4 4.3 %collective-permute-start.14 = (bf16[32,768]{1,0:T(8,128)(2,1)S(1)}, bf16[32,768]{1,0:T(8,128)(2,1)S(1)}, u32[]{:S(2)}, u32[]{:S(2)}) collective-permute-start(bf16[32,768]{1,0:T(8,128)(2,1)S(1)} %get-tuple-element.68), channel_id=1, source_target_pairs={{0,3},{1,0},{2,1},{3,2},{4,7},{5,4},{6,5},{7,6},{8,11},{9,8},{10,9... | collective-permute-start | bytes 147464 | tf_op jit(solution)/shard_map/ppermute | solution.py:40

commit v7 on v5

--- a/solution.py
+++ b/solution.py
@@ -9,6 +9,8 @@
 
 epsilon = 1e-05
 LANES = 128
+FIRST = (0,)
+INNER_STEPS = ((1, 2), (2, 1), (3, 3))
 TOKEN_COPIES = 4
 NT = (((1,), (1,)), ((), ()))
 VMEM = pl.BlockSpec(memory_space=pltpu.VMEM)
@@ -23,10 +25,24 @@
     return lax.ppermute(value, axis, [(place, place ^ distance) for place in range(count)])
 
 
-def turn(value, distance):
-    count = lax.axis_size("inner")
-    pairs = [(place, (place + distance) % count) for place in range(count)]
-    return lax.ppermute(value, "inner", pairs)
+def inner_steps(count):
+    if count == len(INNER_STEPS) + 1:
+        return INNER_STEPS
+    return tuple((k, k) for k in range(1, count))
+
+
+def place_after(member, section, step, count):
+    return lax.rem(member + jnp.where(section % 2 == 0, step[0], step[1]), count)
+
+
+def turn(value, step):
+    sections, count = lax.axis_size("section"), lax.axis_size("inner")
+    pairs = [
+        (section * count + place, section * count + (place + step[section % 2]) % count)
+        for section in range(sections)
+        for place in range(count)
+    ]
+    return lax.ppermute(value, ("section", "inner"), pairs)
 
 
 def visit(value, step, cross):
@@ -185,8 +201,8 @@
     section = section_ref[0]
     tall = lax.broadcasted_iota(jnp.int32, (experts, every), 0).astype(jnp.float32)
     for place, distances in enumerate(sets):
-        high_ref, low_ref = outs[2 * place : 2 * place + 2]
-        count, width = high_ref.shape
+        out_ref = outs[place]
+        count, width = out_ref.shape[0], out_ref.shape[1] // 2
         each = width // len(distances)
         lanes = lax.broadcasted_iota(jnp.int32, (count, width), 1).astype(jnp.float32)
         spread = jnp.zeros((count, width), jnp.float32)
@@ -200,16 +216,14 @@
                 upright(slot) + at * each == lanes, weight, 0.0
             )
         high = spread.astype(jnp.bfloat16)
-        high_ref[...] = high
-        low_ref[...] = (spread - high.astype(jnp.float32)).astype(jnp.bfloat16)
+        low = (spread - high.astype(jnp.float32)).astype(jnp.bfloat16)
+        out_ref[...] = jnp.concatenate([high, low], axis=1)
 
 
 def mix(section, normed, slots, named, router, early, near, per_expert):
     rows = normed.shape[0]
     shapes = [
-        shaped(rows, len(distances) * rows // 2, jnp.bfloat16)
-        for distances in (early, near)
-        for _ in range(2)
+        shaped(rows, len(distances) * rows, jnp.bfloat16) for distances in (early, near)
     ]
     return pl.pallas_call(
         functools.partial(mix_kernel, (early, near), per_expert),
@@ -308,73 +322,78 @@
     return every_ref[...]
 
 
-def begin_kernel(count, high_ref, low_ref, *refs):
+def weighed(weights_ref, blocks, every_ref):
+    gathered((*blocks, *blocks), every_ref)
+    return jnp.dot(weights_ref[...], every_ref[...], preferred_element_type=jnp.float32)
+
+
+def begin_kernel(count, weights_ref, *refs):
     blocks, out_ref, every_ref = refs[:count], refs[count], refs[-1]
-    every = gathered(blocks, every_ref)
-    total = jnp.dot(low_ref[...], every, preferred_element_type=jnp.float32)
-    out_ref[...] = total + jnp.dot(high_ref[...], every, preferred_element_type=jnp.float32)
-
-
-def begin(high, low, blocks):
+    out_ref[...] = weighed(weights_ref, blocks, every_ref)
+
+
+def begin(weights, blocks):
     count = len(blocks)
     each, width = blocks[0].shape
     return pl.pallas_call(
         functools.partial(begin_kernel, count),
-        out_shape=shaped(high.shape[0], width, jnp.float32),
-        in_specs=[VMEM] * (2 + count),
+        out_shape=shaped(weights.shape[0], width, jnp.float32),
+        in_specs=[VMEM] * (1 + count),
         out_specs=VMEM,
-        scratch_shapes=[pltpu.VMEM((count * each, width), jnp.bfloat16)],
+        scratch_shapes=[pltpu.VMEM((2 * count * each, width), jnp.bfloat16)],
         compiler_params=PARAMS,
         name="begin",
-    )(high, low, *blocks)
-
-
-def close_kernel(count, member_ref, tokens_ref, high_ref, low_ref, begun_ref, *refs):
+    )(weights, *blocks)
+
+
+def close_kernel(count, steps, member_ref, section_ref, tokens_ref, weights_ref, begun_ref, *refs):
     blocks, outs, every_ref, total_ref = refs[:count], refs[count:-2], refs[-2], refs[-1]
-    every = gathered(blocks, every_ref)
-    total = begun_ref[...] + jnp.dot(low_ref[...], every, preferred_element_type=jnp.float32)
-    total_ref[...] = total + jnp.dot(high_ref[...], every, preferred_element_type=jnp.float32)
+    total_ref[...] = begun_ref[...] + weighed(weights_ref, blocks, every_ref)
     if len(outs) == 1:
         outs[0][...] = total_ref[...]
         return
     part = outs[0].shape[1]
     for k, out_ref in enumerate(outs):
-        columns = pl.ds(pl.multiple_of(lax.rem(member_ref[0] + k, len(outs)) * part, LANES), part)
+        place = member_ref[0]
+        if k:
+            place = place_after(place, section_ref[0], steps[k - 1], len(outs))
+        columns = pl.ds(pl.multiple_of(place * part, LANES), part)
         value = total_ref[:, columns]
         if k == 0:
             value = value + tokens_ref[:, columns].astype(jnp.float32)
         out_ref[...] = value.astype(out_ref.dtype)
 
 
-def close(high, low, begun, blocks, tokens, member, inner_count):
+def close(weights, begun, blocks, tokens, member, section, inner_count):
     count = len(blocks)
     each = blocks[0].shape[0]
     rows, width = begun.shape
     part = width // inner_count
     whole = part % LANES != 0
+    steps = inner_steps(inner_count)
     kinds = [jnp.float32] + [jnp.bfloat16] * (inner_count - 1)
     shapes = [shaped(rows, part, kind) for kind in kinds]
     if whole:
         shapes = [shaped(rows, width, jnp.float32)]
     outs = pl.pallas_call(
-        functools.partial(close_kernel, count),
+        functools.partial(close_kernel, count, steps),
         out_shape=shapes,
-        in_specs=[SMEM] + [VMEM] * (4 + count),
+        in_specs=[SMEM] * 2 + [VMEM] * (3 + count),
         out_specs=[VMEM] * len(shapes),
         scratch_shapes=[
-            pltpu.VMEM((count * each, width), jnp.bfloat16),
+            pltpu.VMEM((2 * count * each, width), jnp.bfloat16),
             pltpu.VMEM((rows, width), jnp.float32),
         ],
         compiler_params=PARAMS,
         name="close",
-    )(member.reshape(1), tokens, high, low, begun, *blocks)
+    )(member.reshape(1), section, tokens, weights, begun, *blocks)
     if not whole:
         return outs
     rounded = outs[0].astype(jnp.bfloat16)
     total = outs[0] + tokens.astype(jnp.float32)
     outs = [lax.dynamic_slice_in_dim(total, member * part, part, 1)]
     for k in range(1, inner_count):
-        place = lax.rem(member + k, inner_count)
+        place = place_after(member, section[0], steps[k - 1], inner_count)
         outs.append(lax.dynamic_slice_in_dim(rounded, place * part, part, 1))
     return outs
 
@@ -417,49 +436,62 @@
     gain = norm_gain.reshape(1, width)
 
     far = chips - 1
-    first_steps = ((0, 0), (far, far))
-    steps = []
+    steps = [(far, far)]
     for k in range(1, far, 2):
         steps += [(k, k + 1), (k + 1, k)]
+    first = [steps[k] for k in FIRST]
+    second = [step for step in steps if step not in first]
+    first_steps = ((0, 0), *first)
 
     other = trade(own, "section", 1)
     other_named = trade(named, "section", 1)
     *halves, own, gain, normed, slots, names = own_part(
         section, own, named, gain, first_steps, per_expert, experts
     )
-    message, away, other_normed, other_slots = other_part(
+    message, *messages, other_normed, other_slots = other_part(
         section, other, other_named, gain, halves, first_steps, per_expert, experts
     )
-    away = visit(away, (far, far), 0)
+    first_blocks = [visit(value, step, 0) for value, step in zip(messages, first)]
     turned_in, router_rows, down, *messages = load_weights(
         section,
         expert_in[0].reshape(2 * hidden, width),
         (router.T, expert_out[0]),
         (normed, other_normed),
         (slots, other_slots),
-        tuple(steps),
+        tuple(second),
         per_expert,
     )
-    arrived = [visit(value, step, 0) for value, step in zip(messages, steps)]
+    second_blocks = [visit(value, step, 0) for value, step in zip(messages, second)]
 
     def origins(step):
         a, b = step
         return ((2 * a, 2 * b), (2 * b + 1, 2 * a + 1))
 
-    early = origins((far, far)) + origins((0, 0))
-    late = tuple(pair for step in steps for pair in origins(step))
-    high_a, low_a, high_b, low_b = mix(
+    def send_back(results, steps):
+        return [visit(value, steps[j // 2], j % 2) for j, value in enumerate(results)]
+
+    early = tuple(pair for step in (*first, (0, 0)) for pair in origins(step))
+    late = tuple(pair for step in second for pair in origins(step))
+    early_weights, late_weights = mix(
         section, normed, slots, names, router_rows, early, late, per_expert
     )
-    here, beside, *away = run_expert([message, away], turned_in, down, 2)
-    results = run_expert(arrived, turned_in, down, 2, (here,))
-    away = [visit(value, (far, far), cross) for cross, value in enumerate(away)]
-    begun = begin(high_a, low_a, [*away, here, trade(beside, "section", 1)])
-    results = [visit(value, steps[j // 2], j % 2) for j, value in enumerate(results)]
-    split = close(high_b, low_b, begun, results, own, member, inner_count)
-    pieces = {k: turn(split[k], k) for k in range(1, inner_count)}
-    pieces[0] = split[0]
-    return finish([pieces[k] for k in range(inner_count)], micro, row_count)
+    here, beside = run_expert([message], turned_in, down, 2)
+    beside = trade(beside, "section", 1)
+    first_results = run_expert(first_blocks, turned_in, down, 2, (here,))
+    second_results = run_expert(second_blocks, turned_in, down, 2, (first_results[0],))
+    begun = begin(early_weights, [*send_back(first_results, first), here, beside])
+    split = close(
+        late_weights,
+        begun,
+        send_back(second_results, second),
+        own,
+        member,
+        section,
+        inner_count,
+    )
+    pieces = [split[0]]
+    pieces += [turn(value, step) for value, step in zip(split[1:], inner_steps(inner_count))]
+    return finish(pieces, micro, row_count)
 
 
 def solution(mesh):

time: 35 us -> 34.4 us (0.983)
  waiting for transfers between devices: 8.86 us -> 7.73 us
  Pallas kernels: 7.65 us -> 8.63 us
  starting transfers between devices: 18.2 us -> 17.8 us
    ppermute x9, waiting for transfers between devices: 5.93 us -> 4.83 us  [visit(): return lax.ppermute(value, 'section', pairs)]
    pallas_call x2 -> x3, Pallas kernels: 2.06 us -> 3 us  [run_expert(): pl.pallas_call(functools.partial(expert_kernel, count, len(after)), out_s...]
  transfers between devices with their start and end apart: 15 -> 15, of which waited for: 8 -> 8; matrix products, arithmetic and copies ran while one was open for 0% -> 0% of each run, Pallas kernels for 18% -> 21%
where the time goes in v7:
time: 34.4 us; the launch traced here: 34.2 us
  starting transfers between devices  17.8 us (52%)
  Pallas kernels  8.63 us (25%)
  waiting for transfers between devices  7.73 us (22%)
    ppermute x9, starting transfers between devices, visit(): return lax.ppermute(value, 'section', pairs)  11.7 us
    ppermute x3, starting transfers between devices, turn(): return lax.ppermute(value, ('section', 'inner'), pairs)  5.57 us
    ppermute x9, waiting for transfers between devices, visit(): return lax.ppermute(value, 'section', pairs)  4.83 us
    pallas_call x3, Pallas kernels, run_expert(): pl.pallas_call(functools.partial(expert_kernel, count, len(after)), out_s...  3 us
    ppermute x3, waiting for transfers between devices, turn(): return lax.ppermute(value, ('section', 'inner'), pairs)  2.86 us
    pallas_call x1, Pallas kernels, load_weights(): pl.pallas_call(functools.partial(load_kernel, count, steps, per_expert),...  2.46 us
    pallas_call x1, Pallas kernels, own_part(): pl.pallas_call(functools.partial(own_kernel, steps, per_expert), out_shap...  1.26 us
  transfers between devices with their start and end apart: 15, of which 8 were waited for; matrix products, arithmetic and copies ran while one was open for 0% of the time, Pallas kernels for 21%

profile of v7, /device:TPU:0, one launch (start us, length us, event | category | flops | bytes accessed | tf_op | source)
XLA Modules:
  0.0 34.2 jit_solution(16705793373238474808)
XLA Ops:
  0.0 0.5 %collective-permute-start = (bf16[32,3072]{1,0:T(8,128)(2,1)}, bf16[32,3072]{1,0:T(8,128)(2,1)S(1)}, u32[]{:S(2)}, u32[]{:S(2)}) collective-permute-start(bf16[32,3072]{1,0:T(8,128)(2,1)} %bitcast.10), channel_id=1, source_target_pairs={{0,4},{4,0},{8,12},{12,8},{16,20},{20,16},{24,28},{28,24},{1,5},{5... | collective-permute-start | bytes 589832 | tf_op jit(solution)/shard_map/ppermute | solution.py:25
  0.5 0.1 collective-permute-start.1
  0.5 1.3 %own_part.1 = (bf16[16,3072]{1,0:T(8,128)(2,1)S(1)}, bf16[16,3072]{1,0:T(8,128)(2,1)S(1)}, bf16[32,3072]{1,0:T(8,128)(2,1)S(1)}, f32[1,3072]{1,0:T(1,128)S(1)}, ...) custom-call(s32[1]{0:T(128)} %bitcast.1.section_ref, bf16[32,3072]{1,0:T(8,128)(2,1)} %bitcast.11, ...), custom_call_target="tpu_custom_call" | custom-call | tf_op jit(solution)/shard_map/own_part/pallas_call | solution.py:144
  1.8 0.4 %other_part.1 = (bf16[32,3072]{1,0:T(8,128)(2,1)S(1)}, bf16[32,3072]{1,0:T(8,128)(2,1)S(1)}, bf16[32,3072]{1,0:T(8,128)(2,1)S(1)}, f32[8,32]{1,0:T(8,128)S(1)}) custom-call(s32[1]{0:T(128)} %bitcast.1.section_ref, bf16[32,3072]{1,0:T(8,128)(2,1)S(1)} %collective-permute-done.other_ref, s32[2,2,16]{2,1,0:T(2,128)S(1)} %collective-permute-done.1.named_ref, ...), custom_call_target="tpu_custom_call" | custom-call | tf_op jit(solution)/shard_map/other_part/pallas_call | solution.py:173
  2.2 3.9 %collective-permute-start.2 = (bf16[32,3072]{1,0:T(8,128)(2,1)S(1)}, bf16[32,3072]{1,0:T(8,128)(2,1)S(1)}, u32[]{:S(2)}, u32[]{:S(2)}) collective-permute-start(bf16[32,3072]{1,0:T(8,128)(2,1)S(1)} %get-tuple-element.49), channel_id=1, source_target_pairs={{0,24},{4,28},{8,16},{12,20},{16,8},{20,12},{24,0},{28,4},{1,25},{... | collective-permute-start | bytes 589832 | tf_op jit(solution)/shard_map/ppermute | solution.py:51
  6.2 2.5 %load_weights.1 = (bf16[3072,512]{1,0:T(8,128)(2,1)S(1)}, bf16[8,3072]{1,0:T(8,128)(2,1)S(1)}, bf16[256,3072]{1,0:T(8,128)(2,1)S(1)}, bf16[32,3072]{1,0:T(8,128)(2,1)S(1)}, bf16[32,3072]{1,0:T(8,128)(2,1)S(1)}) custom-call(s32[1]{0:T(128)} %bitcast.1.section_ref, bf16[512,3072]{1,0:T(8,128)(2,1)} %bitcast.8, bf16[8,3072]{1,0:T(8,128)(2,1)} %bitcast.12, ...), custom_call_target="tpu_custom_call" | custom-call | tf_op jit(solution)/shard_map/load_weights/pallas_call | solution.py:276
  8.6 0.6 %collective-permute-start.6 = (bf16[32,3072]{1,0:T(8,128)(2,1)S(1)}, bf16[32,3072]{1,0:T(8,128)(2,1)S(1)}, u32[]{:S(2)}, u32[]{:S(2)}) collective-permute-start(bf16[32,3072]{1,0:T(8,128)(2,1)S(1)} %get-tuple-element.55), channel_id=1, source_target_pairs={{0,8},{4,20},{8,0},{12,28},{16,24},{20,4},{24,16},{28,12},{1,9},{5... | collective-permute-start | bytes 589832 | tf_op jit(solution)/shard_map/ppermute | solution.py:51
  9.2 0.1 collective-permute-start.7
  9.3 1.0 %expert.3 = (bf16[16,3072]{1,0:T(8,128)(2,1)S(1)}, bf16[16,3072]{1,0:T(8,128)(2,1)S(1)}) custom-call(bf16[3072,512]{1,0:T(8,128)(2,1)S(1)} %get-tuple-element.47.in_ref, bf16[256,3072]{1,0:T(8,128)(2,1)S(1)} %get-tuple-element.48.down_ref, bf16[32,3072]{1,0:T(8,128)(2,1)S(1)} %get-tuple-element.50.refs_0_), custom_call_target="tpu_custom_call" | custom-call | tf_op jit(solution)/shard_map/expert/pallas_call | solution.py:307
  10.3 1.1 %collective-permute-done.2.refs_0_ = bf16[32,3072]{1,0:T(8,128)(2,1)S(1)} collective-permute-done((bf16[32,3072]{1,0:T(8,128)(2,1)S(1)}, bf16[32,3072]{1,0:T(8,128)(2,1)S(1)}, u32[]{:S(2)}, u32[]{:S(2)}) %collective-permute-start.2) | collective-permute-done | bytes 196640 | tf_op jit(solution)/shard_map/ppermute | solution.py:51
  11.4 1.0 %expert.4 = (bf16[16,3072]{1,0:T(8,128)(2,1)S(1)}, bf16[16,3072]{1,0:T(8,128)(2,1)S(1)}) custom-call(bf16[3072,512]{1,0:T(8,128)(2,1)S(1)} %get-tuple-element.47.in_ref, bf16[256,3072]{1,0:T(8,128)(2,1)S(1)} %get-tuple-element.48.down_ref, bf16[32,3072]{1,0:T(8,128)(2,1)S(1)} %collective-permute-done.2.refs_0_, ...), custom_call_target="tpu_custom_call" | custom-call | tf_op jit(solution)/shard_map/expert/pallas_call | solution.py:307
  12.4 1.9 %collective-permute-start.4 = (bf16[16,3072]{1,0:T(8,128)(2,1)S(1)}, bf16[16,3072]{1,0:T(8,128)(2,1)S(1)}, u32[]{:S(2)}, u32[]{:S(2)}) collective-permute-start(bf16[16,3072]{1,0:T(8,128)(2,1)S(1)} %get-tuple-element.53), channel_id=1, source_target_pairs={{0,28},{4,24},{8,20},{12,16},{16,12},{20,8},{24,4},{28,0},{1,29},{... | collective-permute-start | bytes 294920 | tf_op jit(solution)/shard_map/ppermute | solution.py:51
  14.4 1.6 %collective-permute-start.3 = (bf16[16,3072]{1,0:T(8,128)(2,1)S(1)}, bf16[16,3072]{1,0:T(8,128)(2,1)S(1)}, u32[]{:S(2)}, u32[]{:S(2)}) collective-permute-start(bf16[16,3072]{1,0:T(8,128)(2,1)S(1)} %get-tuple-element.52.refs_2_), channel_id=1, source_target_pairs={{0,24},{4,28},{8,16},{12,20},{16,8},{20,12},{24,0},{28,4},{1,25},{... | collective-permute-start | bytes 294920 | tf_op jit(solution)/shard_map/ppermute | solution.py:51
  16.0 1.0 %expert.5 = (bf16[16,3072]{1,0:T(8,128)(2,1)S(1)}, bf16[16,3072]{1,0:T(8,128)(2,1)S(1)}, bf16[16,3072]{1,0:T(8,128)(2,1)S(1)}, bf16[16,3072]{1,0:T(8,128)(2,1)S(1)}) custom-call(bf16[3072,512]{1,0:T(8,128)(2,1)S(1)} %get-tuple-element.47.in_ref, bf16[256,3072]{1,0:T(8,128)(2,1)S(1)} %get-tuple-element.48.down_ref, ...), custom_call_target="tpu_custom_call" | custom-call | tf_op jit(solution)/shard_map/expert/pallas_call | solution.py:307
  17.0 1.4 %collective-permute-start.8 = (bf16[16,3072]{1,0:T(8,128)(2,1)S(1)}, bf16[16,3072]{1,0:T(8,128)(2,1)S(1)}, u32[]{:S(2)}, u32[]{:S(2)}) collective-permute-start(bf16[16,3072]{1,0:T(8,128)(2,1)S(1)} %get-tuple-element.57), channel_id=1, source_target_pairs={{0,8},{4,20},{8,0},{12,28},{16,24},{20,4},{24,16},{28,12},{1,9},{5... | collective-permute-start | bytes 294920 | tf_op jit(solution)/shard_map/ppermute | solution.py:51
  18.4 1.3 %collective-permute-start.9 = (bf16[16,3072]{1,0:T(8,128)(2,1)S(1)}, bf16[16,3072]{1,0:T(8,128)(2,1)S(1)}, u32[]{:S(2)}, u32[]{:S(2)}) collective-permute-start(bf16[16,3072]{1,0:T(8,128)(2,1)S(1)} %get-tuple-element.58), channel_id=1, source_target_pairs={{0,12},{4,16},{8,4},{12,24},{16,28},{20,0},{24,20},{28,8},{1,13},{... | collective-permute-start | bytes 294920 | tf_op jit(solution)/shard_map/ppermute | solution.py:51
  19.6 0.3 %collective-permute-start.10 = (bf16[16,3072]{1,0:T(8,128)(2,1)S(1)}, bf16[16,3072]{1,0:T(8,128)(2,1)S(1)}, u32[]{:S(2)}, u32[]{:S(2)}) collective-permute-start(bf16[16,3072]{1,0:T(8,128)(2,1)S(1)} %get-tuple-element.59), channel_id=1, source_target_pairs={{0,16},{4,12},{8,24},{12,4},{16,0},{20,28},{24,8},{28,20},{1,17},{... | collective-permute-start | bytes 294920 | tf_op jit(solution)/shard_map/ppermute | solution.py:51
  20.0 0.6 %collective-permute-start.11 = (bf16[16,3072]{1,0:T(8,128)(2,1)S(1)}, bf16[16,3072]{1,0:T(8,128)(2,1)S(1)}, u32[]{:S(2)}, u32[]{:S(2)}) collective-permute-start(bf16[16,3072]{1,0:T(8,128)(2,1)S(1)} %get-tuple-element.60), channel_id=1, source_target_pairs={{0,20},{4,8},{8,28},{12,0},{16,4},{20,24},{24,12},{28,16},{1,21},{... | collective-permute-start | bytes 294920 | tf_op jit(solution)/shard_map/ppermute | solution.py:51
  20.6 0.4 %mix.1 = (bf16[32,128]{1,0:T(8,128)(2,1)S(1)}, bf16[32,128]{1,0:T(8,128)(2,1)S(1)}) custom-call(s32[1]{0:T(128)} %bitcast.1.section_ref, bf16[32,3072]{1,0:T(8,128)(2,1)S(1)} %get-tuple-element.36.refs_2_.normed_ref, f32[8,32]{1,0:T(8,128)S(1)} %get-tuple-element.37.refs_4_.slots_ref, f32[2,32]{1,0:T(2,128)S(1)} %get-tuple-element.38.named_ref, ...), custom_call_target="tpu_custom_call" | custom-call | tf_op jit(solution)/shard_map/mix/pallas_call | solution.py:228
  20.9 0.2 begin.1.begun_ref
  21.2 0.5 %collective-permute-done.8.refs_0_ = bf16[16,3072]{1,0:T(8,128)(2,1)S(1)} collective-permute-done((bf16[16,3072]{1,0:T(8,128)(2,1)S(1)}, bf16[16,3072]{1,0:T(8,128)(2,1)S(1)}, u32[]{:S(2)}, u32[]{:S(2)}) %collective-permute-start.8) | collective-permute-done | bytes 98336 | tf_op jit(solution)/shard_map/ppermute | solution.py:51
  21.7 1.3 %collective-permute-done.9.refs_1_ = bf16[16,3072]{1,0:T(8,128)(2,1)S(1)} collective-permute-done((bf16[16,3072]{1,0:T(8,128)(2,1)S(1)}, bf16[16,3072]{1,0:T(8,128)(2,1)S(1)}, u32[]{:S(2)}, u32[]{:S(2)}) %collective-permute-start.9) | collective-permute-done | bytes 98336 | tf_op jit(solution)/shard_map/ppermute | solution.py:51
  23.0 1.2 %collective-permute-done.10.refs_2_ = bf16[16,3072]{1,0:T(8,128)(2,1)S(1)} collective-permute-done((bf16[16,3072]{1,0:T(8,128)(2,1)S(1)}, bf16[16,3072]{1,0:T(8,128)(2,1)S(1)}, u32[]{:S(2)}, u32[]{:S(2)}) %collective-permute-start.10) | collective-permute-done | bytes 98336 | tf_op jit(solution)/shard_map/ppermute | solution.py:51
  24.2 0.6 %collective-permute-done.11.refs_3_ = bf16[16,3072]{1,0:T(8,128)(2,1)S(1)} collective-permute-done((bf16[16,3072]{1,0:T(8,128)(2,1)S(1)}, bf16[16,3072]{1,0:T(8,128)(2,1)S(1)}, u32[]{:S(2)}, u32[]{:S(2)}) %collective-permute-start.11) | collective-permute-done | bytes 98336 | tf_op jit(solution)/shard_map/ppermute | solution.py:51
  24.9 0.3 close.1
  25.1 1.6 %collective-permute-start.12 = (bf16[32,768]{1,0:T(8,128)(2,1)S(1)}, bf16[32,768]{1,0:T(8,128)(2,1)S(1)}, u32[]{:S(2)}, u32[]{:S(2)}) collective-permute-start(bf16[32,768]{1,0:T(8,128)(2,1)S(1)} %get-tuple-element.62), channel_id=1, source_target_pairs={{0,1},{1,2},{2,3},{3,0},{4,6},{5,7},{6,4},{7,5},{8,9},{9,10},{10,1... | collective-permute-start | bytes 147464 | tf_op jit(solution)/shard_map/ppermute | solution.py:45
  26.8 2.6 %collective-permute-start.13 = (bf16[32,768]{1,0:T(8,128)(2,1)S(1)}, bf16[32,768]{1,0:T(8,128)(2,1)S(1)}, u32[]{:S(2)}, u32[]{:S(2)}) collective-permute-start(bf16[32,768]{1,0:T(8,128)(2,1)S(1)} %get-tuple-element.63), channel_id=1, source_target_pairs={{0,2},{1,3},{2,0},{3,1},{4,5},{5,6},{6,7},{7,4},{8,10},{9,11},{10,... | collective-permute-start | bytes 147464 | tf_op jit(solution)/shard_map/ppermute | solution.py:45
  29.4 1.4 %collective-permute-start.14 = (bf16[32,768]{1,0:T(8,128)(2,1)S(1)}, bf16[32,768]{1,0:T(8,128)(2,1)S(1)}, u32[]{:S(2)}, u32[]{:S(2)}) collective-permute-start(bf16[32,768]{1,0:T(8,128)(2,1)S(1)} %get-tuple-element.64), channel_id=1, source_target_pairs={{0,3},{1,0},{2,1},{3,2},{4,7},{5,4},{6,5},{7,6},{8,11},{9,8},{10,9... | collective-permute-start | bytes 147464 | tf_op jit(solution)/shard_map/ppermute | solution.py:45
  30.7 0.4 %collective-permute-done.12.refs_1_ = bf16[32,768]{1,0:T(8,128)(2,1)S(1)} collective-permute-done((bf16[32,768]{1,0:T(8,128)(2,1)S(1)}, bf16[32,768]{1,0:T(8,128)(2,1)S(1)}, u32[]{:S(2)}, u32[]{:S(2)}) %collective-permute-start.12) | collective-permute-done | bytes 49184 | tf_op jit(solution)/shard_map/ppermute | solution.py:45
  31.1 1.2 %collective-permute-done.13.refs_2_ = bf16[32,768]{1,0:T(8,128)(2,1)S(1)} collective-permute-done((bf16[32,768]{1,0:T(8,128)(2,1)S(1)}, bf16[32,768]{1,0:T(8,128)(2,1)S(1)}, u32[]{:S(2)}, u32[]{:S(2)}) %collective-permute-start.13) | collective-permute-done | bytes 49184 | tf_op jit(solution)/shard_map/ppermute | solution.py:45
  32.3 1.3 %collective-permute-done.14.refs_3_ = bf16[32,768]{1,0:T(8,128)(2,1)S(1)} collective-permute-done((bf16[32,768]{1,0:T(8,128)(2,1)S(1)}, bf16[32,768]{1,0:T(8,128)(2,1)S(1)}, u32[]{:S(2)}, u32[]{:S(2)}) %collective-permute-start.14) | collective-permute-done | bytes 49184 | tf_op jit(solution)/shard_map/ppermute | solution.py:45
  33.6 0.6 %finish.1 = bf16[2,16,768]{2,1,0:T(8,128)(2,1)} custom-call(f32[32,768]{1,0:T(8,128)S(1)} %get-tuple-element.61.refs_0_, bf16[32,768]{1,0:T(8,128)(2,1)S(1)} %collective-permute-done.12.refs_1_, bf16[32,768]{1,0:T(8,128)(2,1)S(1)} %collective-permute-done.13.refs_2_, bf16[32,768]{1,0:T(8,128)(2,1)S(1)} %collective-permute-done.14.refs_3_), custom_call_target="tpu_custom_call" | custom-call | tf_op jit(solution)/shard_map/finish/pallas_call | solution.py:413
  (8 shorter events, 0.1 us)
Async XLA Ops:
  0.0 1.8 %collective-permute-start = (bf16[32,3072]{1,0:T(8,128)(2,1)}, bf16[32,3072]{1,0:T(8,128)(2,1)S(1)}, u32[]{:S(2)}, u32[]{:S(2)}) collective-permute-start(bf16[32,3072]{1,0:T(8,128)(2,1)} %bitcast.10), channel_id=1, source_target_pairs={{0,4},{4,0},{8,12},{12,8},{16,20},{20,16},{24,28},{28,24},{1,5},{5... | collective-permute-start | bytes 589832 | tf_op jit(solution)/shard_map/ppermute | solution.py:25
  0.5 1.4 %collective-permute-start.1 = (s32[2,2,16]{2,1,0:T(2,128)}, s32[2,2,16]{2,1,0:T(2,128)S(1)}, u32[]{:S(2)}, u32[]{:S(2)}) collective-permute-start(s32[2,2,16]{2,1,0:T(2,128)} %bitcast.14), channel_id=1, source_target_pairs={{0,4},{4,0},{8,12},{12,8},{16,20},{20,16},{24,28},{28,24},{1,5},{5... | collective-permute-start | bytes 776 | tf_op jit(solution)/shard_map/ppermute | solution.py:25
  2.2 9.2 %collective-permute-start.2 = (bf16[32,3072]{1,0:T(8,128)(2,1)S(1)}, bf16[32,3072]{1,0:T(8,128)(2,1)S(1)}, u32[]{:S(2)}, u32[]{:S(2)}) collective-permute-start(bf16[32,3072]{1,0:T(8,128)(2,1)S(1)} %get-tuple-element.49), channel_id=1, source_target_pairs={{0,24},{4,28},{8,16},{12,20},{16,8},{20,12},{24,0},{28,4},{1,25},{... | collective-permute-start | bytes 589832 | tf_op jit(solution)/shard_map/ppermute | solution.py:51
  8.6 7.3 %collective-permute-start.6 = (bf16[32,3072]{1,0:T(8,128)(2,1)S(1)}, bf16[32,3072]{1,0:T(8,128)(2,1)S(1)}, u32[]{:S(2)}, u32[]{:S(2)}) collective-permute-start(bf16[32,3072]{1,0:T(8,128)(2,1)S(1)} %get-tuple-element.55), channel_id=1, source_target_pairs={{0,8},{4,20},{8,0},{12,28},{16,24},{20,4},{24,16},{28,12},{1,9},{5... | collective-permute-start | bytes 589832 | tf_op jit(solution)/shard_map/ppermute | solution.py:51
  9.2 6.7 %collective-permute-start.7 = (bf16[32,3072]{1,0:T(8,128)(2,1)S(1)}, bf16[32,3072]{1,0:T(8,128)(2,1)S(1)}, u32[]{:S(2)}, u32[]{:S(2)}) collective-permute-start(bf16[32,3072]{1,0:T(8,128)(2,1)S(1)} %get-tuple-element.56), channel_id=1, source_target_pairs={{0,16},{4,12},{8,24},{12,4},{16,0},{20,28},{24,8},{28,20},{1,17},{... | collective-permute-start | bytes 589832 | tf_op jit(solution)/shard_map/ppermute | solution.py:51
  10.3 9.4 %collective-permute-start.5 = (bf16[16,3072]{1,0:T(8,128)(2,1)S(1)}, bf16[16,3072]{1,0:T(8,128)(2,1)S(1)}, u32[]{:S(2)}, u32[]{:S(2)}) collective-permute-start(bf16[16,3072]{1,0:T(8,128)(2,1)S(1)} %get-tuple-element.54), channel_id=1, source_target_pairs={{0,4},{4,0},{8,12},{12,8},{16,20},{20,16},{24,28},{28,24},{1,5},{5... | collective-permute-start | bytes 294920 | tf_op jit(solution)/shard_map/ppermute | solution.py:25
  12.4 7.5 %collective-permute-start.4 = (bf16[16,3072]{1,0:T(8,128)(2,1)S(1)}, bf16[16,3072]{1,0:T(8,128)(2,1)S(1)}, u32[]{:S(2)}, u32[]{:S(2)}) collective-permute-start(bf16[16,3072]{1,0:T(8,128)(2,1)S(1)} %get-tuple-element.53), channel_id=1, source_target_pairs={{0,28},{4,24},{8,20},{12,16},{16,12},{20,8},{24,4},{28,0},{1,29},{... | collective-permute-start | bytes 294920 | tf_op jit(solution)/shard_map/ppermute | solution.py:51
  14.4 6.6 %collective-permute-start.3 = (bf16[16,3072]{1,0:T(8,128)(2,1)S(1)}, bf16[16,3072]{1,0:T(8,128)(2,1)S(1)}, u32[]{:S(2)}, u32[]{:S(2)}) collective-permute-start(bf16[16,3072]{1,0:T(8,128)(2,1)S(1)} %get-tuple-element.52.refs_2_), channel_id=1, source_target_pairs={{0,24},{4,28},{8,16},{12,20},{16,8},{20,12},{24,0},{28,4},{1,25},{... | collective-permute-start | bytes 294920 | tf_op jit(solution)/shard_map/ppermute | solution.py:51
  17.0 4.7 %collective-permute-start.8 = (bf16[16,3072]{1,0:T(8,128)(2,1)S(1)}, bf16[16,3072]{1,0:T(8,128)(2,1)S(1)}, u32[]{:S(2)}, u32[]{:S(2)}) collective-permute-start(bf16[16,3072]{1,0:T(8,128)(2,1)S(1)} %get-tuple-element.57), channel_id=1, source_target_pairs={{0,8},{4,20},{8,0},{12,28},{16,24},{20,4},{24,16},{28,12},{1,9},{5... | collective-permute-start | bytes 294920 | tf_op jit(solution)/shard_map/ppermute | solution.py:51
  18.4 4.7 %collective-permute-start.9 = (bf16[16,3072]{1,0:T(8,128)(2,1)S(1)}, bf16[16,3072]{1,0:T(8,128)(2,1)S(1)}, u32[]{:S(2)}, u32[]{:S(2)}) collective-permute-start(bf16[16,3072]{1,0:T(8,128)(2,1)S(1)} %get-tuple-element.58), channel_id=1, source_target_pairs={{0,12},{4,16},{8,4},{12,24},{16,28},{20,0},{24,20},{28,8},{1,13},{... | collective-permute-start | bytes 294920 | tf_op jit(solution)/shard_map/ppermute | solution.py:51
  19.6 4.6 %collective-permute-start.10 = (bf16[16,3072]{1,0:T(8,128)(2,1)S(1)}, bf16[16,3072]{1,0:T(8,128)(2,1)S(1)}, u32[]{:S(2)}, u32[]{:S(2)}) collective-permute-start(bf16[16,3072]{1,0:T(8,128)(2,1)S(1)} %get-tuple-element.59), channel_id=1, source_target_pairs={{0,16},{4,12},{8,24},{12,4},{16,0},{20,28},{24,8},{28,20},{1,17},{... | collective-permute-start | bytes 294920 | tf_op jit(solution)/shard_map/ppermute | solution.py:51
  20.0 4.9 %collective-permute-start.11 = (bf16[16,3072]{1,0:T(8,128)(2,1)S(1)}, bf16[16,3072]{1,0:T(8,128)(2,1)S(1)}, u32[]{:S(2)}, u32[]{:S(2)}) collective-permute-start(bf16[16,3072]{1,0:T(8,128)(2,1)S(1)} %get-tuple-element.60), channel_id=1, source_target_pairs={{0,20},{4,8},{8,28},{12,0},{16,4},{20,24},{24,12},{28,16},{1,21},{... | collective-permute-start | bytes 294920 | tf_op jit(solution)/shard_map/ppermute | solution.py:51
  25.1 5.9 %collective-permute-start.12 = (bf16[32,768]{1,0:T(8,128)(2,1)S(1)}, bf16[32,768]{1,0:T(8,128)(2,1)S(1)}, u32[]{:S(2)}, u32[]{:S(2)}) collective-permute-start(bf16[32,768]{1,0:T(8,128)(2,1)S(1)} %get-tuple-element.62), channel_id=1, source_target_pairs={{0,1},{1,2},{2,3},{3,0},{4,6},{5,7},{6,4},{7,5},{8,9},{9,10},{10,1... | collective-permute-start | bytes 147464 | tf_op jit(solution)/shard_map/ppermute | solution.py:45
  26.8 5.5 %collective-permute-start.13 = (bf16[32,768]{1,0:T(8,128)(2,1)S(1)}, bf16[32,768]{1,0:T(8,128)(2,1)S(1)}, u32[]{:S(2)}, u32[]{:S(2)}) collective-permute-start(bf16[32,768]{1,0:T(8,128)(2,1)S(1)} %get-tuple-element.63), channel_id=1, source_target_pairs={{0,2},{1,3},{2,0},{3,1},{4,5},{5,6},{6,7},{7,4},{8,10},{9,11},{10,... | collective-permute-start | bytes 147464 | tf_op jit(solution)/shard_map/ppermute | solution.py:45
  29.4 4.2 %collective-permute-start.14 = (bf16[32,768]{1,0:T(8,128)(2,1)S(1)}, bf16[32,768]{1,0:T(8,128)(2,1)S(1)}, u32[]{:S(2)}, u32[]{:S(2)}) collective-permute-start(bf16[32,768]{1,0:T(8,128)(2,1)S(1)} %get-tuple-element.64), channel_id=1, source_target_pairs={{0,3},{1,0},{2,1},{3,2},{4,7},{5,4},{6,5},{7,6},{8,11},{9,8},{10,9... | collective-permute-start | bytes 147464 | tf_op jit(solution)/shard_map/ppermute | solution.py:45

commit v8 on v6

--- a/solution.py
+++ b/solution.py
@@ -215,15 +215,15 @@
         low_ref[...] = (spread - high.astype(jnp.float32)).astype(jnp.bfloat16)
 
 
-def mix(section, normed, slots, named, router, early, near, per_expert):
+def mix(section, normed, slots, named, router, sets, per_expert):
     rows = normed.shape[0]
     shapes = [
         shaped(rows, len(distances) * rows // 2, jnp.bfloat16)
-        for distances in (early, near)
+        for distances in sets
         for _ in range(2)
     ]
     return pl.pallas_call(
-        functools.partial(mix_kernel, (early, near), per_expert),
+        functools.partial(mix_kernel, sets, per_expert),
         out_shape=shapes,
         in_specs=[SMEM] + [VMEM] * 4,
         out_specs=[VMEM] * len(shapes),
@@ -319,6 +319,27 @@
     return every_ref[...]
 
 
+def add_kernel(count, high_ref, low_ref, begun_ref, *refs):
+    blocks, out_ref, every_ref = refs[:count], refs[count], refs[-1]
+    every = gathered(blocks, every_ref)
+    total = begun_ref[...] + jnp.dot(low_ref[...], every, preferred_element_type=jnp.float32)
+    out_ref[...] = total + jnp.dot(high_ref[...], every, preferred_element_type=jnp.float32)
+
+
+def add_to(high, low, begun, blocks):
+    count = len(blocks)
+    each, width = blocks[0].shape
+    return pl.pallas_call(
+        functools.partial(add_kernel, count),
+        out_shape=shaped(*begun.shape, jnp.float32),
+        in_specs=[VMEM] * (3 + count),
+        out_specs=VMEM,
+        scratch_shapes=[pltpu.VMEM((count * each, width), jnp.bfloat16)],
+        compiler_params=PARAMS,
+        name="add_to",
+    )(high, low, begun, *blocks)
+
+
 def begin_kernel(count, high_ref, low_ref, *refs):
     blocks, out_ref, every_ref = refs[:count], refs[count], refs[-1]
     every = gathered(blocks, every_ref)
@@ -461,8 +482,9 @@
 
     early = origins((far, far)) + origins((0, 0))
     late = tuple(pair for step in steps for pair in origins(step))
-    high_a, low_a, high_b, low_b = mix(
-        section, normed, slots, names, router_rows, early, late, per_expert
+    sets = (early, late[:2], late[2:])
+    high_a, low_a, high_m, low_m, high_b, low_b = mix(
+        section, normed, slots, names, router_rows, sets, per_expert
     )
     here, beside = run_expert([message], turned_in, down, 2)
     beside = trade(beside, "section", 1)
@@ -471,7 +493,8 @@
     away = [visit(value, (far, far), cross) for cross, value in enumerate(away)]
     begun = begin(high_a, low_a, [*away, here, beside])
     results = [visit(value, steps[j // 2], j % 2) for j, value in enumerate(results)]
-    split = close(high_b, low_b, begun, results, own, member, inner_count)
+    begun = add_to(high_m, low_m, begun, results[:2])
+    split = close(high_b, low_b, begun, results[2:], own, member, inner_count)
     targets = inner_targets(inner_count)
     pieces = [split[0]] + [turn(value, order) for value, order in zip(split[1:], targets)]
     return finish(pieces, micro, row_count)

time: 34.5 us -> 34.5 us (level)
  transfers between devices with their start and end apart: 15 -> 15, of which waited for: 8 -> 8; matrix products, arithmetic and copies ran while one was open for 0% -> 0% of each run, Pallas kernels for 21% -> 22%
where the time goes in v8:
time: 34.5 us; the launch traced here: 34.3 us
  starting transfers between devices  17.8 us (52%)
  Pallas kernels  8.82 us (26%)
  waiting for transfers between devices  7.6 us (22%)
    ppermute x9, starting transfers between devices, visit(): return lax.ppermute(value, 'section', pairs)  11.7 us
    ppermute x3, starting transfers between devices, turn(): return lax.ppermute(value, 'inner', list(enumerate(targets)))  5.57 us
    ppermute x9, waiting for transfers between devices, visit(): return lax.ppermute(value, 'section', pairs)  4.62 us
    pallas_call x3, Pallas kernels, run_expert(): pl.pallas_call(functools.partial(expert_kernel, count, len(after)), out_s...  3 us
    ppermute x3, waiting for transfers between devices, turn(): return lax.ppermute(value, 'inner', list(enumerate(targets)))  2.95 us
    pallas_call x1, Pallas kernels, load_weights(): pl.pallas_call(functools.partial(load_kernel, count, steps, per_expert),...  2.46 us
    pallas_call x1, Pallas kernels, own_part(): pl.pallas_call(functools.partial(own_kernel, steps, per_expert), out_shap...  1.26 us
  transfers between devices with their start and end apart: 15, of which 8 were waited for; matrix products, arithmetic and copies ran while one was open for 0% of the time, Pallas kernels for 22%

profile of v8, /device:TPU:0, one launch (start us, length us, event | category | flops | bytes accessed | tf_op | source)
XLA Modules:
  0.0 34.3 jit_solution(15609096565717926698)
XLA Ops:
  0.0 0.5 %collective-permute-start = (bf16[32,3072]{1,0:T(8,128)(2,1)}, bf16[32,3072]{1,0:T(8,128)(2,1)S(1)}, u32[]{:S(2)}, u32[]{:S(2)}) collective-permute-start(bf16[32,3072]{1,0:T(8,128)(2,1)} %bitcast.10), channel_id=1, source_target_pairs={{0,4},{4,0},{8,12},{12,8},{16,20},{20,16},{24,28},{28,24},{1,5},{5... | collective-permute-start | bytes 589832 | tf_op jit(solution)/shard_map/ppermute | solution.py:24
  0.5 0.1 collective-permute-start.1
  0.5 1.3 %own_part.1 = (bf16[16,3072]{1,0:T(8,128)(2,1)S(1)}, bf16[16,3072]{1,0:T(8,128)(2,1)S(1)}, bf16[32,3072]{1,0:T(8,128)(2,1)S(1)}, f32[1,3072]{1,0:T(1,128)S(1)}, ...) custom-call(s32[1]{0:T(128)} %bitcast.1.section_ref, bf16[32,3072]{1,0:T(8,128)(2,1)} %bitcast.11, ...), custom_call_target="tpu_custom_call" | custom-call | tf_op jit(solution)/shard_map/own_part/pallas_call | solution.py:139
  1.8 0.4 %other_part.1 = (bf16[32,3072]{1,0:T(8,128)(2,1)S(1)}, bf16[32,3072]{1,0:T(8,128)(2,1)S(1)}, bf16[32,3072]{1,0:T(8,128)(2,1)S(1)}, f32[8,32]{1,0:T(8,128)S(1)}) custom-call(s32[1]{0:T(128)} %bitcast.1.section_ref, bf16[32,3072]{1,0:T(8,128)(2,1)S(1)} %collective-permute-done.other_ref, s32[2,2,16]{2,1,0:T(2,128)S(1)} %collective-permute-done.1.named_ref, ...), custom_call_target="tpu_custom_call" | custom-call | tf_op jit(solution)/shard_map/other_part/pallas_call | solution.py:168
  2.2 3.9 %collective-permute-start.2 = (bf16[32,3072]{1,0:T(8,128)(2,1)S(1)}, bf16[32,3072]{1,0:T(8,128)(2,1)S(1)}, u32[]{:S(2)}, u32[]{:S(2)}) collective-permute-start(bf16[32,3072]{1,0:T(8,128)(2,1)S(1)} %get-tuple-element.57), channel_id=1, source_target_pairs={{0,24},{4,28},{8,16},{12,20},{16,8},{20,12},{24,0},{28,4},{1,25},{... | collective-permute-start | bytes 589832 | tf_op jit(solution)/shard_map/ppermute | solution.py:46
  6.2 2.5 %load_weights.1 = (bf16[3072,512]{1,0:T(8,128)(2,1)S(1)}, bf16[8,3072]{1,0:T(8,128)(2,1)S(1)}, bf16[256,3072]{1,0:T(8,128)(2,1)S(1)}, bf16[32,3072]{1,0:T(8,128)(2,1)S(1)}, bf16[32,3072]{1,0:T(8,128)(2,1)S(1)}) custom-call(s32[1]{0:T(128)} %bitcast.1.section_ref, bf16[512,3072]{1,0:T(8,128)(2,1)} %bitcast.8, bf16[8,3072]{1,0:T(8,128)(2,1)} %bitcast.12, ...), custom_call_target="tpu_custom_call" | custom-call | tf_op jit(solution)/shard_map/load_weights/pallas_call | solution.py:273
  8.6 0.6 %collective-permute-start.6 = (bf16[32,3072]{1,0:T(8,128)(2,1)S(1)}, bf16[32,3072]{1,0:T(8,128)(2,1)S(1)}, u32[]{:S(2)}, u32[]{:S(2)}) collective-permute-start(bf16[32,3072]{1,0:T(8,128)(2,1)S(1)} %get-tuple-element.63), channel_id=1, source_target_pairs={{0,8},{4,20},{8,0},{12,28},{16,24},{20,4},{24,16},{28,12},{1,9},{5... | collective-permute-start | bytes 589832 | tf_op jit(solution)/shard_map/ppermute | solution.py:46
  9.3 1.0 %expert.3 = (bf16[16,3072]{1,0:T(8,128)(2,1)S(1)}, bf16[16,3072]{1,0:T(8,128)(2,1)S(1)}) custom-call(bf16[3072,512]{1,0:T(8,128)(2,1)S(1)} %get-tuple-element.55.in_ref, bf16[256,3072]{1,0:T(8,128)(2,1)S(1)} %get-tuple-element.56.down_ref, bf16[32,3072]{1,0:T(8,128)(2,1)S(1)} %get-tuple-element.58.refs_0_), custom_call_target="tpu_custom_call" | custom-call | tf_op jit(solution)/shard_map/expert/pallas_call | solution.py:304
  10.3 1.1 %collective-permute-done.2.refs_0_ = bf16[32,3072]{1,0:T(8,128)(2,1)S(1)} collective-permute-done((bf16[32,3072]{1,0:T(8,128)(2,1)S(1)}, bf16[32,3072]{1,0:T(8,128)(2,1)S(1)}, u32[]{:S(2)}, u32[]{:S(2)}) %collective-permute-start.2) | collective-permute-done | bytes 196640 | tf_op jit(solution)/shard_map/ppermute | solution.py:46
  11.4 1.0 %expert.4 = (bf16[16,3072]{1,0:T(8,128)(2,1)S(1)}, bf16[16,3072]{1,0:T(8,128)(2,1)S(1)}) custom-call(bf16[3072,512]{1,0:T(8,128)(2,1)S(1)} %get-tuple-element.55.in_ref, bf16[256,3072]{1,0:T(8,128)(2,1)S(1)} %get-tuple-element.56.down_ref, bf16[32,3072]{1,0:T(8,128)(2,1)S(1)} %collective-permute-done.2.refs_0_, ...), custom_call_target="tpu_custom_call" | custom-call | tf_op jit(solution)/shard_map/expert/pallas_call | solution.py:304
  12.4 1.9 %collective-permute-start.4 = (bf16[16,3072]{1,0:T(8,128)(2,1)S(1)}, bf16[16,3072]{1,0:T(8,128)(2,1)S(1)}, u32[]{:S(2)}, u32[]{:S(2)}) collective-permute-start(bf16[16,3072]{1,0:T(8,128)(2,1)S(1)} %get-tuple-element.61), channel_id=1, source_target_pairs={{0,28},{4,24},{8,20},{12,16},{16,12},{20,8},{24,4},{28,0},{1,29},{... | collective-permute-start | bytes 294920 | tf_op jit(solution)/shard_map/ppermute | solution.py:46
  14.4 1.6 %collective-permute-start.3 = (bf16[16,3072]{1,0:T(8,128)(2,1)S(1)}, bf16[16,3072]{1,0:T(8,128)(2,1)S(1)}, u32[]{:S(2)}, u32[]{:S(2)}) collective-permute-start(bf16[16,3072]{1,0:T(8,128)(2,1)S(1)} %get-tuple-element.60.refs_2_), channel_id=1, source_target_pairs={{0,24},{4,28},{8,16},{12,20},{16,8},{20,12},{24,0},{28,4},{1,25},{... | collective-permute-start | bytes 294920 | tf_op jit(solution)/shard_map/ppermute | solution.py:46
  16.0 1.0 %expert.5 = (bf16[16,3072]{1,0:T(8,128)(2,1)S(1)}, bf16[16,3072]{1,0:T(8,128)(2,1)S(1)}, bf16[16,3072]{1,0:T(8,128)(2,1)S(1)}, bf16[16,3072]{1,0:T(8,128)(2,1)S(1)}) custom-call(bf16[3072,512]{1,0:T(8,128)(2,1)S(1)} %get-tuple-element.55.in_ref, bf16[256,3072]{1,0:T(8,128)(2,1)S(1)} %get-tuple-element.56.down_ref, ...), custom_call_target="tpu_custom_call" | custom-call | tf_op jit(solution)/shard_map/expert/pallas_call | solution.py:304
  17.0 1.4 %collective-permute-start.8 = (bf16[16,3072]{1,0:T(8,128)(2,1)S(1)}, bf16[16,3072]{1,0:T(8,128)(2,1)S(1)}, u32[]{:S(2)}, u32[]{:S(2)}) collective-permute-start(bf16[16,3072]{1,0:T(8,128)(2,1)S(1)} %get-tuple-element.65), channel_id=1, source_target_pairs={{0,8},{4,20},{8,0},{12,28},{16,24},{20,4},{24,16},{28,12},{1,9},{5... | collective-permute-start | bytes 294920 | tf_op jit(solution)/shard_map/ppermute | solution.py:46
  18.4 1.3 %collective-permute-start.9 = (bf16[16,3072]{1,0:T(8,128)(2,1)S(1)}, bf16[16,3072]{1,0:T(8,128)(2,1)S(1)}, u32[]{:S(2)}, u32[]{:S(2)}) collective-permute-start(bf16[16,3072]{1,0:T(8,128)(2,1)S(1)} %get-tuple-element.66), channel_id=1, source_target_pairs={{0,12},{4,16},{8,4},{12,24},{16,28},{20,0},{24,20},{28,8},{1,13},{... | collective-permute-start | bytes 294920 | tf_op jit(solution)/shard_map/ppermute | solution.py:46
  19.6 0.3 %collective-permute-start.10 = (bf16[16,3072]{1,0:T(8,128)(2,1)S(1)}, bf16[16,3072]{1,0:T(8,128)(2,1)S(1)}, u32[]{:S(2)}, u32[]{:S(2)}) collective-permute-start(bf16[16,3072]{1,0:T(8,128)(2,1)S(1)} %get-tuple-element.67), channel_id=1, source_target_pairs={{0,16},{4,12},{8,24},{12,4},{16,0},{20,28},{24,8},{28,20},{1,17},{... | collective-permute-start | bytes 294920 | tf_op jit(solution)/shard_map/ppermute | solution.py:46
  20.0 0.6 %collective-permute-start.11 = (bf16[16,3072]{1,0:T(8,128)(2,1)S(1)}, bf16[16,3072]{1,0:T(8,128)(2,1)S(1)}, u32[]{:S(2)}, u32[]{:S(2)}) collective-permute-start(bf16[16,3072]{1,0:T(8,128)(2,1)S(1)} %get-tuple-element.68), channel_id=1, source_target_pairs={{0,20},{4,8},{8,28},{12,0},{16,4},{20,24},{24,12},{28,16},{1,21},{... | collective-permute-start | bytes 294920 | tf_op jit(solution)/shard_map/ppermute | solution.py:46
  20.6 0.3 mix.1
  20.9 0.2 begin.1.begun_ref
  21.1 0.6 %collective-permute-done.8.refs_0_ = bf16[16,3072]{1,0:T(8,128)(2,1)S(1)} collective-permute-done((bf16[16,3072]{1,0:T(8,128)(2,1)S(1)}, bf16[16,3072]{1,0:T(8,128)(2,1)S(1)}, u32[]{:S(2)}, u32[]{:S(2)}) %collective-permute-start.8) | collective-permute-done | bytes 98336 | tf_op jit(solution)/shard_map/ppermute | solution.py:46
  21.7 1.3 %collective-permute-done.9.refs_1_ = bf16[16,3072]{1,0:T(8,128)(2,1)S(1)} collective-permute-done((bf16[16,3072]{1,0:T(8,128)(2,1)S(1)}, bf16[16,3072]{1,0:T(8,128)(2,1)S(1)}, u32[]{:S(2)}, u32[]{:S(2)}) %collective-permute-start.9) | collective-permute-done | bytes 98336 | tf_op jit(solution)/shard_map/ppermute | solution.py:46
  23.0 0.2 add_to.1.begun_ref
  23.3 1.0 %collective-permute-done.10.refs_0_ = bf16[16,3072]{1,0:T(8,128)(2,1)S(1)} collective-permute-done((bf16[16,3072]{1,0:T(8,128)(2,1)S(1)}, bf16[16,3072]{1,0:T(8,128)(2,1)S(1)}, u32[]{:S(2)}, u32[]{:S(2)}) %collective-permute-start.10) | collective-permute-done | bytes 98336 | tf_op jit(solution)/shard_map/ppermute | solution.py:46
  24.2 0.6 %collective-permute-done.11.refs_1_ = bf16[16,3072]{1,0:T(8,128)(2,1)S(1)} collective-permute-done((bf16[16,3072]{1,0:T(8,128)(2,1)S(1)}, bf16[16,3072]{1,0:T(8,128)(2,1)S(1)}, u32[]{:S(2)}, u32[]{:S(2)}) %collective-permute-start.11) | collective-permute-done | bytes 98336 | tf_op jit(solution)/shard_map/ppermute | solution.py:46
  24.9 0.3 close.1
  25.1 1.6 %collective-permute-start.12 = (bf16[32,768]{1,0:T(8,128)(2,1)S(1)}, bf16[32,768]{1,0:T(8,128)(2,1)S(1)}, u32[]{:S(2)}, u32[]{:S(2)}) collective-permute-start(bf16[32,768]{1,0:T(8,128)(2,1)S(1)} %get-tuple-element.70), channel_id=1, source_target_pairs={{0,1},{1,2},{2,3},{3,0},{4,5},{5,6},{6,7},{7,4},{8,9},{9,10},{10,1... | collective-permute-start | bytes 147464 | tf_op jit(solution)/shard_map/ppermute | solution.py:40
  26.8 2.6 %collective-permute-start.13 = (bf16[32,768]{1,0:T(8,128)(2,1)S(1)}, bf16[32,768]{1,0:T(8,128)(2,1)S(1)}, u32[]{:S(2)}, u32[]{:S(2)}) collective-permute-start(bf16[32,768]{1,0:T(8,128)(2,1)S(1)} %get-tuple-element.71), channel_id=1, source_target_pairs={{0,2},{1,3},{2,0},{3,1},{4,6},{5,7},{6,4},{7,5},{8,10},{9,11},{10,... | collective-permute-start | bytes 147464 | tf_op jit(solution)/shard_map/ppermute | solution.py:40
  29.4 1.3 %collective-permute-start.14 = (bf16[32,768]{1,0:T(8,128)(2,1)S(1)}, bf16[32,768]{1,0:T(8,128)(2,1)S(1)}, u32[]{:S(2)}, u32[]{:S(2)}) collective-permute-start(bf16[32,768]{1,0:T(8,128)(2,1)S(1)} %get-tuple-element.72), channel_id=1, source_target_pairs={{0,3},{1,0},{2,1},{3,2},{4,7},{5,4},{6,5},{7,6},{8,11},{9,8},{10,9... | collective-permute-start | bytes 147464 | tf_op jit(solution)/shard_map/ppermute | solution.py:40
  30.7 0.4 %collective-permute-done.12.refs_1_ = bf16[32,768]{1,0:T(8,128)(2,1)S(1)} collective-permute-done((bf16[32,768]{1,0:T(8,128)(2,1)S(1)}, bf16[32,768]{1,0:T(8,128)(2,1)S(1)}, u32[]{:S(2)}, u32[]{:S(2)}) %collective-permute-start.12) | collective-permute-done | bytes 49184 | tf_op jit(solution)/shard_map/ppermute | solution.py:40
  31.1 2.2 %collective-permute-done.13.refs_2_ = bf16[32,768]{1,0:T(8,128)(2,1)S(1)} collective-permute-done((bf16[32,768]{1,0:T(8,128)(2,1)S(1)}, bf16[32,768]{1,0:T(8,128)(2,1)S(1)}, u32[]{:S(2)}, u32[]{:S(2)}) %collective-permute-start.13) | collective-permute-done | bytes 49184 | tf_op jit(solution)/shard_map/ppermute | solution.py:40
  33.3 0.3 collective-permute-done.14.refs_3_
  33.7 0.6 %finish.1 = bf16[2,16,768]{2,1,0:T(8,128)(2,1)} custom-call(f32[32,768]{1,0:T(8,128)S(1)} %get-tuple-element.69.refs_0_, bf16[32,768]{1,0:T(8,128)(2,1)S(1)} %collective-permute-done.12.refs_1_, bf16[32,768]{1,0:T(8,128)(2,1)S(1)} %collective-permute-done.13.refs_2_, bf16[32,768]{1,0:T(8,128)(2,1)S(1)} %collective-permute-done.14.refs_3_), custom_call_target="tpu_custom_call" | custom-call | tf_op jit(solution)/shard_map/finish/pallas_call | solution.py:428
  (9 shorter events, 0.2 us)
Async XLA Ops:
  0.0 1.8 %collective-permute-start = (bf16[32,3072]{1,0:T(8,128)(2,1)}, bf16[32,3072]{1,0:T(8,128)(2,1)S(1)}, u32[]{:S(2)}, u32[]{:S(2)}) collective-permute-start(bf16[32,3072]{1,0:T(8,128)(2,1)} %bitcast.10), channel_id=1, source_target_pairs={{0,4},{4,0},{8,12},{12,8},{16,20},{20,16},{24,28},{28,24},{1,5},{5... | collective-permute-start | bytes 589832 | tf_op jit(solution)/shard_map/ppermute | solution.py:24
  0.5 1.4 %collective-permute-start.1 = (s32[2,2,16]{2,1,0:T(2,128)}, s32[2,2,16]{2,1,0:T(2,128)S(1)}, u32[]{:S(2)}, u32[]{:S(2)}) collective-permute-start(s32[2,2,16]{2,1,0:T(2,128)} %bitcast.14), channel_id=1, source_target_pairs={{0,4},{4,0},{8,12},{12,8},{16,20},{20,16},{24,28},{28,24},{1,5},{5... | collective-permute-start | bytes 776 | tf_op jit(solution)/shard_map/ppermute | solution.py:24
  2.2 9.2 %collective-permute-start.2 = (bf16[32,3072]{1,0:T(8,128)(2,1)S(1)}, bf16[32,3072]{1,0:T(8,128)(2,1)S(1)}, u32[]{:S(2)}, u32[]{:S(2)}) collective-permute-start(bf16[32,3072]{1,0:T(8,128)(2,1)S(1)} %get-tuple-element.57), channel_id=1, source_target_pairs={{0,24},{4,28},{8,16},{12,20},{16,8},{20,12},{24,0},{28,4},{1,25},{... | collective-permute-start | bytes 589832 | tf_op jit(solution)/shard_map/ppermute | solution.py:46
  8.6 7.3 %collective-permute-start.6 = (bf16[32,3072]{1,0:T(8,128)(2,1)S(1)}, bf16[32,3072]{1,0:T(8,128)(2,1)S(1)}, u32[]{:S(2)}, u32[]{:S(2)}) collective-permute-start(bf16[32,3072]{1,0:T(8,128)(2,1)S(1)} %get-tuple-element.63), channel_id=1, source_target_pairs={{0,8},{4,20},{8,0},{12,28},{16,24},{20,4},{24,16},{28,12},{1,9},{5... | collective-permute-start | bytes 589832 | tf_op jit(solution)/shard_map/ppermute | solution.py:46
  9.2 6.7 %collective-permute-start.7 = (bf16[32,3072]{1,0:T(8,128)(2,1)S(1)}, bf16[32,3072]{1,0:T(8,128)(2,1)S(1)}, u32[]{:S(2)}, u32[]{:S(2)}) collective-permute-start(bf16[32,3072]{1,0:T(8,128)(2,1)S(1)} %get-tuple-element.64), channel_id=1, source_target_pairs={{0,16},{4,12},{8,24},{12,4},{16,0},{20,28},{24,8},{28,20},{1,17},{... | collective-permute-start | bytes 589832 | tf_op jit(solution)/shard_map/ppermute | solution.py:46
  10.3 9.4 %collective-permute-start.5 = (bf16[16,3072]{1,0:T(8,128)(2,1)S(1)}, bf16[16,3072]{1,0:T(8,128)(2,1)S(1)}, u32[]{:S(2)}, u32[]{:S(2)}) collective-permute-start(bf16[16,3072]{1,0:T(8,128)(2,1)S(1)} %get-tuple-element.62), channel_id=1, source_target_pairs={{0,4},{4,0},{8,12},{12,8},{16,20},{20,16},{24,28},{28,24},{1,5},{5... | collective-permute-start | bytes 294920 | tf_op jit(solution)/shard_map/ppermute | solution.py:24
  12.4 7.5 %collective-permute-start.4 = (bf16[16,3072]{1,0:T(8,128)(2,1)S(1)}, bf16[16,3072]{1,0:T(8,128)(2,1)S(1)}, u32[]{:S(2)}, u32[]{:S(2)}) collective-permute-start(bf16[16,3072]{1,0:T(8,128)(2,1)S(1)} %get-tuple-element.61), channel_id=1, source_target_pairs={{0,28},{4,24},{8,20},{12,16},{16,12},{20,8},{24,4},{28,0},{1,29},{... | collective-permute-start | bytes 294920 | tf_op jit(solution)/shard_map/ppermute | solution.py:46
  14.4 6.5 %collective-permute-start.3 = (bf16[16,3072]{1,0:T(8,128)(2,1)S(1)}, bf16[16,3072]{1,0:T(8,128)(2,1)S(1)}, u32[]{:S(2)}, u32[]{:S(2)}) collective-permute-start(bf16[16,3072]{1,0:T(8,128)(2,1)S(1)} %get-tuple-element.60.refs_2_), channel_id=1, source_target_pairs={{0,24},{4,28},{8,16},{12,20},{16,8},{20,12},{24,0},{28,4},{1,25},{... | collective-permute-start | bytes 294920 | tf_op jit(solution)/shard_map/ppermute | solution.py:46
  17.0 4.7 %collective-permute-start.8 = (bf16[16,3072]{1,0:T(8,128)(2,1)S(1)}, bf16[16,3072]{1,0:T(8,128)(2,1)S(1)}, u32[]{:S(2)}, u32[]{:S(2)}) collective-permute-start(bf16[16,3072]{1,0:T(8,128)(2,1)S(1)} %get-tuple-element.65), channel_id=1, source_target_pairs={{0,8},{4,20},{8,0},{12,28},{16,24},{20,4},{24,16},{28,12},{1,9},{5... | collective-permute-start | bytes 294920 | tf_op jit(solution)/shard_map/ppermute | solution.py:46
  18.4 4.7 %collective-permute-start.9 = (bf16[16,3072]{1,0:T(8,128)(2,1)S(1)}, bf16[16,3072]{1,0:T(8,128)(2,1)S(1)}, u32[]{:S(2)}, u32[]{:S(2)}) collective-permute-start(bf16[16,3072]{1,0:T(8,128)(2,1)S(1)} %get-tuple-element.66), channel_id=1, source_target_pairs={{0,12},{4,16},{8,4},{12,24},{16,28},{20,0},{24,20},{28,8},{1,13},{... | collective-permute-start | bytes 294920 | tf_op jit(solution)/shard_map/ppermute | solution.py:46
  19.6 4.6 %collective-permute-start.10 = (bf16[16,3072]{1,0:T(8,128)(2,1)S(1)}, bf16[16,3072]{1,0:T(8,128)(2,1)S(1)}, u32[]{:S(2)}, u32[]{:S(2)}) collective-permute-start(bf16[16,3072]{1,0:T(8,128)(2,1)S(1)} %get-tuple-element.67), channel_id=1, source_target_pairs={{0,16},{4,12},{8,24},{12,4},{16,0},{20,28},{24,8},{28,20},{1,17},{... | collective-permute-start | bytes 294920 | tf_op jit(solution)/shard_map/ppermute | solution.py:46
  20.0 4.9 %collective-permute-start.11 = (bf16[16,3072]{1,0:T(8,128)(2,1)S(1)}, bf16[16,3072]{1,0:T(8,128)(2,1)S(1)}, u32[]{:S(2)}, u32[]{:S(2)}) collective-permute-start(bf16[16,3072]{1,0:T(8,128)(2,1)S(1)} %get-tuple-element.68), channel_id=1, source_target_pairs={{0,20},{4,8},{8,28},{12,0},{16,4},{20,24},{24,12},{28,16},{1,21},{... | collective-permute-start | bytes 294920 | tf_op jit(solution)/shard_map/ppermute | solution.py:46
  25.1 5.9 %collective-permute-start.12 = (bf16[32,768]{1,0:T(8,128)(2,1)S(1)}, bf16[32,768]{1,0:T(8,128)(2,1)S(1)}, u32[]{:S(2)}, u32[]{:S(2)}) collective-permute-start(bf16[32,768]{1,0:T(8,128)(2,1)S(1)} %get-tuple-element.70), channel_id=1, source_target_pairs={{0,1},{1,2},{2,3},{3,0},{4,5},{5,6},{6,7},{7,4},{8,9},{9,10},{10,1... | collective-permute-start | bytes 147464 | tf_op jit(solution)/shard_map/ppermute | solution.py:40
  26.8 6.6 %collective-permute-start.13 = (bf16[32,768]{1,0:T(8,128)(2,1)S(1)}, bf16[32,768]{1,0:T(8,128)(2,1)S(1)}, u32[]{:S(2)}, u32[]{:S(2)}) collective-permute-start(bf16[32,768]{1,0:T(8,128)(2,1)S(1)} %get-tuple-element.71), channel_id=1, source_target_pairs={{0,2},{1,3},{2,0},{3,1},{4,6},{5,7},{6,4},{7,5},{8,10},{9,11},{10,... | collective-permute-start | bytes 147464 | tf_op jit(solution)/shard_map/ppermute | solution.py:40
  29.4 4.3 %collective-permute-start.14 = (bf16[32,768]{1,0:T(8,128)(2,1)S(1)}, bf16[32,768]{1,0:T(8,128)(2,1)S(1)}, u32[]{:S(2)}, u32[]{:S(2)}) collective-permute-start(bf16[32,768]{1,0:T(8,128)(2,1)S(1)} %get-tuple-element.72), channel_id=1, source_target_pairs={{0,3},{1,0},{2,1},{3,2},{4,7},{5,4},{6,5},{7,6},{8,11},{9,8},{10,9... | collective-permute-start | bytes 147464 | tf_op jit(solution)/shard_map/ppermute | solution.py:40

commit v9 on v7

--- a/solution.py
+++ b/solution.py
@@ -10,7 +10,7 @@
 epsilon = 1e-05
 LANES = 128
 FIRST = (0,)
-INNER_STEPS = ((1, 2), (2, 1), (3, 3))
+INNER_STEPS = ((1, 1), (2, 2), (3, 3))
 TOKEN_COPIES = 4
 NT = (((1,), (1,)), ((), ()))
 VMEM = pl.BlockSpec(memory_space=pltpu.VMEM)
@@ -235,6 +235,31 @@
     )(section, normed, slots, named, router)
 
 
+def near_kernel(steps, per_expert, section_ref, *refs):
+    normed_refs, slots_refs, out_refs = refs[:2], refs[2:4], refs[5:]
+    for part in range(2):
+        packed = picked(
+            section_ref[0], slots_refs[part][...], normed_refs[part][...], steps, per_expert
+        )
+        each = packed.shape[0] // len(steps)
+        for place, out_ref in enumerate(out_refs):
+            out_ref[part * each : (part + 1) * each, :] = packed[
+                place * each : (place + 1) * each, :
+            ]
+
+
+def pack_near(section, normed, slots, steps, per_expert, after):
+    rows, width = normed[0].shape
+    return pl.pallas_call(
+        functools.partial(near_kernel, steps, per_expert),
+        out_shape=[shaped(rows, width, jnp.bfloat16)] * len(steps),
+        in_specs=[SMEM] + [VMEM] * 4 + [ANY],
+        out_specs=[VMEM] * len(steps),
+        compiler_params=PARAMS,
+        name="pack_near",
+    )(section, *normed, *slots, after)
+
+
 def load_kernel(count, steps, per_expert, section_ref, in_ref, *refs):
     sources, refs = refs[:count], refs[count:]
     normed_refs, slots_refs, refs = refs[:2], refs[2:4], refs[4:]
@@ -252,6 +277,8 @@
     for copy in copies + others:
         copy.start()
     for part, (normed_ref, slots_ref) in enumerate(zip(normed_refs, slots_refs)):
+        if not steps:
+            break
         packed = picked(section_ref[0], slots_ref[...], normed_ref[...], steps, per_expert)
         each = packed.shape[0] // len(steps)
         for place, out_ref in enumerate(out_refs):
@@ -452,14 +479,17 @@
         section, other, other_named, gain, halves, first_steps, per_expert, experts
     )
     first_blocks = [visit(value, step, 0) for value, step in zip(messages, first)]
-    turned_in, router_rows, down, *messages = load_weights(
+    turned_in, router_rows, down = load_weights(
         section,
         expert_in[0].reshape(2 * hidden, width),
         (router.T, expert_out[0]),
         (normed, other_normed),
         (slots, other_slots),
-        tuple(second),
+        (),
         per_expert,
+    )
+    messages = pack_near(
+        section, (normed, other_normed), (slots, other_slots), tuple(second), per_expert, down
     )
     second_blocks = [visit(value, step, 0) for value, step in zip(messages, second)]
 
@@ -478,7 +508,9 @@
     here, beside = run_expert([message], turned_in, down, 2)
     beside = trade(beside, "section", 1)
     first_results = run_expert(first_blocks, turned_in, down, 2, (here,))
-    second_results = run_expert(second_blocks, turned_in, down, 2, (first_results[0],))
+    second_results = run_expert(
+        second_blocks, turned_in, down, 2, (first_results[0], beside)
+    )
     begun = begin(early_weights, [*send_back(first_results, first), here, beside])
     split = close(
         late_weights,

time: 34.4 us -> 34.6 us (level)
  transfers between devices with their start and end apart: 15 -> 15, of which waited for: 8 -> 9; matrix products, arithmetic and copies ran while one was open for 0% -> 0% of each run, Pallas kernels for 21% -> 22%
where the time goes in v9:
time: 34.6 us; the launch traced here: 34.4 us
  starting transfers between devices  17.8 us (51%)
  Pallas kernels  8.84 us (26%)
  waiting for transfers between devices  7.7 us (22%)
    ppermute x9, starting transfers between devices, visit(): return lax.ppermute(value, 'section', pairs)  11.7 us
    ppermute x3, starting transfers between devices, turn(): return lax.ppermute(value, ('section', 'inner'), pairs)  5.57 us
    ppermute x9, waiting for transfers between devices, visit(): return lax.ppermute(value, 'section', pairs)  4.73 us
    pallas_call x3, Pallas kernels, run_expert(): pl.pallas_call(functools.partial(expert_kernel, count, len(after)), out_s...  2.99 us
    ppermute x3, waiting for transfers between devices, turn(): return lax.ppermute(value, ('section', 'inner'), pairs)  2.93 us
    pallas_call x1, Pallas kernels, load_weights(): pl.pallas_call(functools.partial(load_kernel, count, steps, per_expert),...  2.43 us
    pallas_call x1, Pallas kernels, own_part(): pl.pallas_call(functools.partial(own_kernel, steps, per_expert), out_shap...  1.26 us
  transfers between devices with their start and end apart: 15, of which 9 were waited for; matrix products, arithmetic and copies ran while one was open for 0% of the time, Pallas kernels for 22%

profile of v9, /device:TPU:0, one launch (start us, length us, event | category | flops | bytes accessed | tf_op | source)
XLA Modules:
  0.0 34.4 jit_solution(530673749370026369)
XLA Ops:
  0.0 0.5 %collective-permute-start = (bf16[32,3072]{1,0:T(8,128)(2,1)}, bf16[32,3072]{1,0:T(8,128)(2,1)S(1)}, u32[]{:S(2)}, u32[]{:S(2)}) collective-permute-start(bf16[32,3072]{1,0:T(8,128)(2,1)} %bitcast.10), channel_id=1, source_target_pairs={{0,4},{4,0},{8,12},{12,8},{16,20},{20,16},{24,28},{28,24},{1,5},{5... | collective-permute-start | bytes 589832 | tf_op jit(solution)/shard_map/ppermute | solution.py:25
  0.5 0.1 collective-permute-start.1
  0.5 1.3 %own_part.1 = (bf16[16,3072]{1,0:T(8,128)(2,1)S(1)}, bf16[16,3072]{1,0:T(8,128)(2,1)S(1)}, bf16[32,3072]{1,0:T(8,128)(2,1)S(1)}, f32[1,3072]{1,0:T(1,128)S(1)}, ...) custom-call(s32[1]{0:T(128)} %bitcast.1.section_ref, bf16[32,3072]{1,0:T(8,128)(2,1)} %bitcast.11, ...), custom_call_target="tpu_custom_call" | custom-call | tf_op jit(solution)/shard_map/own_part/pallas_call | solution.py:144
  1.8 0.4 %other_part.1 = (bf16[32,3072]{1,0:T(8,128)(2,1)S(1)}, bf16[32,3072]{1,0:T(8,128)(2,1)S(1)}, bf16[32,3072]{1,0:T(8,128)(2,1)S(1)}, f32[8,32]{1,0:T(8,128)S(1)}) custom-call(s32[1]{0:T(128)} %bitcast.1.section_ref, bf16[32,3072]{1,0:T(8,128)(2,1)S(1)} %collective-permute-done.other_ref, s32[2,2,16]{2,1,0:T(2,128)S(1)} %collective-permute-done.1.named_ref, ...), custom_call_target="tpu_custom_call" | custom-call | tf_op jit(solution)/shard_map/other_part/pallas_call | solution.py:173
  2.2 3.9 %collective-permute-start.2 = (bf16[32,3072]{1,0:T(8,128)(2,1)S(1)}, bf16[32,3072]{1,0:T(8,128)(2,1)S(1)}, u32[]{:S(2)}, u32[]{:S(2)}) collective-permute-start(bf16[32,3072]{1,0:T(8,128)(2,1)S(1)} %get-tuple-element.49), channel_id=1, source_target_pairs={{0,24},{4,28},{8,16},{12,20},{16,8},{20,12},{24,0},{28,4},{1,25},{... | collective-permute-start | bytes 589832 | tf_op jit(solution)/shard_map/ppermute | solution.py:51
  6.2 2.4 %load_weights.1 = (bf16[3072,512]{1,0:T(8,128)(2,1)S(1)}, bf16[8,3072]{1,0:T(8,128)(2,1)S(1)}, bf16[256,3072]{1,0:T(8,128)(2,1)S(1)}) custom-call(s32[1]{0:T(128)} %bitcast.1.section_ref, bf16[512,3072]{1,0:T(8,128)(2,1)} %bitcast.8, bf16[8,3072]{1,0:T(8,128)(2,1)} %bitcast.12, bf16[256,3072]{1,0:T(8,128)(2,1)} %bitcast.9, ...), custom_call_target="tpu_custom_call" | custom-call | tf_op jit(solution)/shard_map/load_weights/pallas_call | solution.py:303
  8.6 0.3 pack_near.1
  8.9 0.6 %collective-permute-start.6 = (bf16[32,3072]{1,0:T(8,128)(2,1)S(1)}, bf16[32,3072]{1,0:T(8,128)(2,1)S(1)}, u32[]{:S(2)}, u32[]{:S(2)}) collective-permute-start(bf16[32,3072]{1,0:T(8,128)(2,1)S(1)} %get-tuple-element.55), channel_id=1, source_target_pairs={{0,8},{4,20},{8,0},{12,28},{16,24},{20,4},{24,16},{28,12},{1,9},{5... | collective-permute-start | bytes 589832 | tf_op jit(solution)/shard_map/ppermute | solution.py:51
  9.5 1.0 %expert.3 = (bf16[16,3072]{1,0:T(8,128)(2,1)S(1)}, bf16[16,3072]{1,0:T(8,128)(2,1)S(1)}) custom-call(bf16[3072,512]{1,0:T(8,128)(2,1)S(1)} %get-tuple-element.47.in_ref, bf16[256,3072]{1,0:T(8,128)(2,1)S(1)} %get-tuple-element.48.down_ref.refs_4_, bf16[32,3072]{1,0:T(8,128)(2,1)S(1)} %get-tuple-element.50.refs_0_), custom_call_target="tpu_custom_call" | custom-call | tf_op jit(solution)/shard_map/expert/pallas_call | solution.py:334
  10.6 0.9 %collective-permute-done.2.refs_0_ = bf16[32,3072]{1,0:T(8,128)(2,1)S(1)} collective-permute-done((bf16[32,3072]{1,0:T(8,128)(2,1)S(1)}, bf16[32,3072]{1,0:T(8,128)(2,1)S(1)}, u32[]{:S(2)}, u32[]{:S(2)}) %collective-permute-start.2) | collective-permute-done | bytes 196640 | tf_op jit(solution)/shard_map/ppermute | solution.py:51
  11.4 1.0 %expert.4 = (bf16[16,3072]{1,0:T(8,128)(2,1)S(1)}, bf16[16,3072]{1,0:T(8,128)(2,1)S(1)}) custom-call(bf16[3072,512]{1,0:T(8,128)(2,1)S(1)} %get-tuple-element.47.in_ref, bf16[256,3072]{1,0:T(8,128)(2,1)S(1)} %get-tuple-element.48.down_ref.refs_4_, bf16[32,3072]{1,0:T(8,128)(2,1)S(1)} %collective-permute-done.2.refs_0_, ...), custom_call_target="tpu_custom_call" | custom-call | tf_op jit(solution)/shard_map/expert/pallas_call | solution.py:334
  12.4 2.2 %collective-permute-start.4 = (bf16[16,3072]{1,0:T(8,128)(2,1)S(1)}, bf16[16,3072]{1,0:T(8,128)(2,1)S(1)}, u32[]{:S(2)}, u32[]{:S(2)}) collective-permute-start(bf16[16,3072]{1,0:T(8,128)(2,1)S(1)} %get-tuple-element.53), channel_id=1, source_target_pairs={{0,28},{4,24},{8,20},{12,16},{16,12},{20,8},{24,4},{28,0},{1,29},{... | collective-permute-start | bytes 294920 | tf_op jit(solution)/shard_map/ppermute | solution.py:51
  14.6 1.3 %collective-permute-start.3 = (bf16[16,3072]{1,0:T(8,128)(2,1)S(1)}, bf16[16,3072]{1,0:T(8,128)(2,1)S(1)}, u32[]{:S(2)}, u32[]{:S(2)}) collective-permute-start(bf16[16,3072]{1,0:T(8,128)(2,1)S(1)} %get-tuple-element.52.refs_2_), channel_id=1, source_target_pairs={{0,24},{4,28},{8,16},{12,20},{16,8},{20,12},{24,0},{28,4},{1,25},{... | collective-permute-start | bytes 294920 | tf_op jit(solution)/shard_map/ppermute | solution.py:51
  15.9 1.0 %expert.5 = (bf16[16,3072]{1,0:T(8,128)(2,1)S(1)}, bf16[16,3072]{1,0:T(8,128)(2,1)S(1)}, bf16[16,3072]{1,0:T(8,128)(2,1)S(1)}, bf16[16,3072]{1,0:T(8,128)(2,1)S(1)}) custom-call(bf16[3072,512]{1,0:T(8,128)(2,1)S(1)} %get-tuple-element.47.in_ref, bf16[256,3072]{1,0:T(8,128)(2,1)S(1)} %get-tuple-element.48.down_ref.refs_4_, ...), custom_call_target="tpu_custom_call" | custom-call | tf_op jit(solution)/shard_map/expert/pallas_call | solution.py:334
  17.0 1.4 %collective-permute-start.8 = (bf16[16,3072]{1,0:T(8,128)(2,1)S(1)}, bf16[16,3072]{1,0:T(8,128)(2,1)S(1)}, u32[]{:S(2)}, u32[]{:S(2)}) collective-permute-start(bf16[16,3072]{1,0:T(8,128)(2,1)S(1)} %get-tuple-element.57), channel_id=1, source_target_pairs={{0,8},{4,20},{8,0},{12,28},{16,24},{20,4},{24,16},{28,12},{1,9},{5... | collective-permute-start | bytes 294920 | tf_op jit(solution)/shard_map/ppermute | solution.py:51
  18.3 1.3 %collective-permute-start.9 = (bf16[16,3072]{1,0:T(8,128)(2,1)S(1)}, bf16[16,3072]{1,0:T(8,128)(2,1)S(1)}, u32[]{:S(2)}, u32[]{:S(2)}) collective-permute-start(bf16[16,3072]{1,0:T(8,128)(2,1)S(1)} %get-tuple-element.58), channel_id=1, source_target_pairs={{0,12},{4,16},{8,4},{12,24},{16,28},{20,0},{24,20},{28,8},{1,13},{... | collective-permute-start | bytes 294920 | tf_op jit(solution)/shard_map/ppermute | solution.py:51
  19.6 0.3 %collective-permute-start.10 = (bf16[16,3072]{1,0:T(8,128)(2,1)S(1)}, bf16[16,3072]{1,0:T(8,128)(2,1)S(1)}, u32[]{:S(2)}, u32[]{:S(2)}) collective-permute-start(bf16[16,3072]{1,0:T(8,128)(2,1)S(1)} %get-tuple-element.59), channel_id=1, source_target_pairs={{0,16},{4,12},{8,24},{12,4},{16,0},{20,28},{24,8},{28,20},{1,17},{... | collective-permute-start | bytes 294920 | tf_op jit(solution)/shard_map/ppermute | solution.py:51
  19.9 0.6 %collective-permute-start.11 = (bf16[16,3072]{1,0:T(8,128)(2,1)S(1)}, bf16[16,3072]{1,0:T(8,128)(2,1)S(1)}, u32[]{:S(2)}, u32[]{:S(2)}) collective-permute-start(bf16[16,3072]{1,0:T(8,128)(2,1)S(1)} %get-tuple-element.60), channel_id=1, source_target_pairs={{0,20},{4,8},{8,28},{12,0},{16,4},{20,24},{24,12},{28,16},{1,21},{... | collective-permute-start | bytes 294920 | tf_op jit(solution)/shard_map/ppermute | solution.py:51
  20.5 0.4 %mix.1 = (bf16[32,128]{1,0:T(8,128)(2,1)S(1)}, bf16[32,128]{1,0:T(8,128)(2,1)S(1)}) custom-call(s32[1]{0:T(128)} %bitcast.1.section_ref, bf16[32,3072]{1,0:T(8,128)(2,1)S(1)} %get-tuple-element.36.refs_2_.normed_ref.refs_0_, f32[8,32]{1,0:T(8,128)S(1)} %get-tuple-element.37.refs_4_.slots_ref.refs_2_, f32[2,32]{1,0:T(2,128)S(1)} %get-tuple-element.38.named_ref, ...), custom_call_target="tpu_custom_call" | custom-call | tf_op jit(solution)/shard_map/mix/pallas_call | solution.py:228
  21.0 0.2 begin.1.begun_ref
  21.2 0.6 %collective-permute-done.8.refs_0_ = bf16[16,3072]{1,0:T(8,128)(2,1)S(1)} collective-permute-done((bf16[16,3072]{1,0:T(8,128)(2,1)S(1)}, bf16[16,3072]{1,0:T(8,128)(2,1)S(1)}, u32[]{:S(2)}, u32[]{:S(2)}) %collective-permute-start.8) | collective-permute-done | bytes 98336 | tf_op jit(solution)/shard_map/ppermute | solution.py:51
  21.8 1.6 %collective-permute-done.9.refs_1_ = bf16[16,3072]{1,0:T(8,128)(2,1)S(1)} collective-permute-done((bf16[16,3072]{1,0:T(8,128)(2,1)S(1)}, bf16[16,3072]{1,0:T(8,128)(2,1)S(1)}, u32[]{:S(2)}, u32[]{:S(2)}) %collective-permute-start.9) | collective-permute-done | bytes 98336 | tf_op jit(solution)/shard_map/ppermute | solution.py:51
  23.4 0.9 %collective-permute-done.10.refs_2_ = bf16[16,3072]{1,0:T(8,128)(2,1)S(1)} collective-permute-done((bf16[16,3072]{1,0:T(8,128)(2,1)S(1)}, bf16[16,3072]{1,0:T(8,128)(2,1)S(1)}, u32[]{:S(2)}, u32[]{:S(2)}) %collective-permute-start.10) | collective-permute-done | bytes 98336 | tf_op jit(solution)/shard_map/ppermute | solution.py:51
  24.3 0.7 %collective-permute-done.11.refs_3_ = bf16[16,3072]{1,0:T(8,128)(2,1)S(1)} collective-permute-done((bf16[16,3072]{1,0:T(8,128)(2,1)S(1)}, bf16[16,3072]{1,0:T(8,128)(2,1)S(1)}, u32[]{:S(2)}, u32[]{:S(2)}) %collective-permute-start.11) | collective-permute-done | bytes 98336 | tf_op jit(solution)/shard_map/ppermute | solution.py:51
  25.0 0.3 close.1
  25.3 1.6 %collective-permute-start.12 = (bf16[32,768]{1,0:T(8,128)(2,1)S(1)}, bf16[32,768]{1,0:T(8,128)(2,1)S(1)}, u32[]{:S(2)}, u32[]{:S(2)}) collective-permute-start(bf16[32,768]{1,0:T(8,128)(2,1)S(1)} %get-tuple-element.62), channel_id=1, source_target_pairs={{0,1},{1,2},{2,3},{3,0},{4,5},{5,6},{6,7},{7,4},{8,9},{9,10},{10,1... | collective-permute-start | bytes 147464 | tf_op jit(solution)/shard_map/ppermute | solution.py:45
  26.9 2.6 %collective-permute-start.13 = (bf16[32,768]{1,0:T(8,128)(2,1)S(1)}, bf16[32,768]{1,0:T(8,128)(2,1)S(1)}, u32[]{:S(2)}, u32[]{:S(2)}) collective-permute-start(bf16[32,768]{1,0:T(8,128)(2,1)S(1)} %get-tuple-element.63), channel_id=1, source_target_pairs={{0,2},{1,3},{2,0},{3,1},{4,6},{5,7},{6,4},{7,5},{8,10},{9,11},{10,... | collective-permute-start | bytes 147464 | tf_op jit(solution)/shard_map/ppermute | solution.py:45
  29.5 1.4 %collective-permute-start.14 = (bf16[32,768]{1,0:T(8,128)(2,1)S(1)}, bf16[32,768]{1,0:T(8,128)(2,1)S(1)}, u32[]{:S(2)}, u32[]{:S(2)}) collective-permute-start(bf16[32,768]{1,0:T(8,128)(2,1)S(1)} %get-tuple-element.64), channel_id=1, source_target_pairs={{0,3},{1,0},{2,1},{3,2},{4,7},{5,4},{6,5},{7,6},{8,11},{9,8},{10,9... | collective-permute-start | bytes 147464 | tf_op jit(solution)/shard_map/ppermute | solution.py:45
  30.8 0.4 %collective-permute-done.12.refs_1_ = bf16[32,768]{1,0:T(8,128)(2,1)S(1)} collective-permute-done((bf16[32,768]{1,0:T(8,128)(2,1)S(1)}, bf16[32,768]{1,0:T(8,128)(2,1)S(1)}, u32[]{:S(2)}, u32[]{:S(2)}) %collective-permute-start.12) | collective-permute-done | bytes 49184 | tf_op jit(solution)/shard_map/ppermute | solution.py:45
  31.2 2.2 %collective-permute-done.13.refs_2_ = bf16[32,768]{1,0:T(8,128)(2,1)S(1)} collective-permute-done((bf16[32,768]{1,0:T(8,128)(2,1)S(1)}, bf16[32,768]{1,0:T(8,128)(2,1)S(1)}, u32[]{:S(2)}, u32[]{:S(2)}) %collective-permute-start.13) | collective-permute-done | bytes 49184 | tf_op jit(solution)/shard_map/ppermute | solution.py:45
  33.4 0.3 collective-permute-done.14.refs_3_
  33.8 0.6 %finish.1 = bf16[2,16,768]{2,1,0:T(8,128)(2,1)} custom-call(f32[32,768]{1,0:T(8,128)S(1)} %get-tuple-element.61.refs_0_, bf16[32,768]{1,0:T(8,128)(2,1)S(1)} %collective-permute-done.12.refs_1_, bf16[32,768]{1,0:T(8,128)(2,1)S(1)} %collective-permute-done.13.refs_2_, bf16[32,768]{1,0:T(8,128)(2,1)S(1)} %collective-permute-done.14.refs_3_), custom_call_target="tpu_custom_call" | custom-call | tf_op jit(solution)/shard_map/finish/pallas_call | solution.py:440
  (9 shorter events, 0.2 us)
Async XLA Ops:
  0.0 1.8 %collective-permute-start = (bf16[32,3072]{1,0:T(8,128)(2,1)}, bf16[32,3072]{1,0:T(8,128)(2,1)S(1)}, u32[]{:S(2)}, u32[]{:S(2)}) collective-permute-start(bf16[32,3072]{1,0:T(8,128)(2,1)} %bitcast.10), channel_id=1, source_target_pairs={{0,4},{4,0},{8,12},{12,8},{16,20},{20,16},{24,28},{28,24},{1,5},{5... | collective-permute-start | bytes 589832 | tf_op jit(solution)/shard_map/ppermute | solution.py:25
  0.5 1.4 %collective-permute-start.1 = (s32[2,2,16]{2,1,0:T(2,128)}, s32[2,2,16]{2,1,0:T(2,128)S(1)}, u32[]{:S(2)}, u32[]{:S(2)}) collective-permute-start(s32[2,2,16]{2,1,0:T(2,128)} %bitcast.14), channel_id=1, source_target_pairs={{0,4},{4,0},{8,12},{12,8},{16,20},{20,16},{24,28},{28,24},{1,5},{5... | collective-permute-start | bytes 776 | tf_op jit(solution)/shard_map/ppermute | solution.py:25
  2.2 9.2 %collective-permute-start.2 = (bf16[32,3072]{1,0:T(8,128)(2,1)S(1)}, bf16[32,3072]{1,0:T(8,128)(2,1)S(1)}, u32[]{:S(2)}, u32[]{:S(2)}) collective-permute-start(bf16[32,3072]{1,0:T(8,128)(2,1)S(1)} %get-tuple-element.49), channel_id=1, source_target_pairs={{0,24},{4,28},{8,16},{12,20},{16,8},{20,12},{24,0},{28,4},{1,25},{... | collective-permute-start | bytes 589832 | tf_op jit(solution)/shard_map/ppermute | solution.py:51
  8.9 7.1 %collective-permute-start.6 = (bf16[32,3072]{1,0:T(8,128)(2,1)S(1)}, bf16[32,3072]{1,0:T(8,128)(2,1)S(1)}, u32[]{:S(2)}, u32[]{:S(2)}) collective-permute-start(bf16[32,3072]{1,0:T(8,128)(2,1)S(1)} %get-tuple-element.55), channel_id=1, source_target_pairs={{0,8},{4,20},{8,0},{12,28},{16,24},{20,4},{24,16},{28,12},{1,9},{5... | collective-permute-start | bytes 589832 | tf_op jit(solution)/shard_map/ppermute | solution.py:51
  9.4 6.5 %collective-permute-start.7 = (bf16[32,3072]{1,0:T(8,128)(2,1)S(1)}, bf16[32,3072]{1,0:T(8,128)(2,1)S(1)}, u32[]{:S(2)}, u32[]{:S(2)}) collective-permute-start(bf16[32,3072]{1,0:T(8,128)(2,1)S(1)} %get-tuple-element.56), channel_id=1, source_target_pairs={{0,16},{4,12},{8,24},{12,4},{16,0},{20,28},{24,8},{28,20},{1,17},{... | collective-permute-start | bytes 589832 | tf_op jit(solution)/shard_map/ppermute | solution.py:51
  10.5 5.4 %collective-permute-start.5 = (bf16[16,3072]{1,0:T(8,128)(2,1)S(1)}, bf16[16,3072]{1,0:T(8,128)(2,1)S(1)}, u32[]{:S(2)}, u32[]{:S(2)}) collective-permute-start(bf16[16,3072]{1,0:T(8,128)(2,1)S(1)} %get-tuple-element.54), channel_id=1, source_target_pairs={{0,4},{4,0},{8,12},{12,8},{16,20},{20,16},{24,28},{28,24},{1,5},{5... | collective-permute-start | bytes 294920 | tf_op jit(solution)/shard_map/ppermute | solution.py:25
  12.4 7.5 %collective-permute-start.4 = (bf16[16,3072]{1,0:T(8,128)(2,1)S(1)}, bf16[16,3072]{1,0:T(8,128)(2,1)S(1)}, u32[]{:S(2)}, u32[]{:S(2)}) collective-permute-start(bf16[16,3072]{1,0:T(8,128)(2,1)S(1)} %get-tuple-element.53), channel_id=1, source_target_pairs={{0,28},{4,24},{8,20},{12,16},{16,12},{20,8},{24,4},{28,0},{1,29},{... | collective-permute-start | bytes 294920 | tf_op jit(solution)/shard_map/ppermute | solution.py:51
  14.6 6.4 %collective-permute-start.3 = (bf16[16,3072]{1,0:T(8,128)(2,1)S(1)}, bf16[16,3072]{1,0:T(8,128)(2,1)S(1)}, u32[]{:S(2)}, u32[]{:S(2)}) collective-permute-start(bf16[16,3072]{1,0:T(8,128)(2,1)S(1)} %get-tuple-element.52.refs_2_), channel_id=1, source_target_pairs={{0,24},{4,28},{8,16},{12,20},{16,8},{20,12},{24,0},{28,4},{1,25},{... | collective-permute-start | bytes 294920 | tf_op jit(solution)/shard_map/ppermute | solution.py:51
  17.0 4.9 %collective-permute-start.8 = (bf16[16,3072]{1,0:T(8,128)(2,1)S(1)}, bf16[16,3072]{1,0:T(8,128)(2,1)S(1)}, u32[]{:S(2)}, u32[]{:S(2)}) collective-permute-start(bf16[16,3072]{1,0:T(8,128)(2,1)S(1)} %get-tuple-element.57), channel_id=1, source_target_pairs={{0,8},{4,20},{8,0},{12,28},{16,24},{20,4},{24,16},{28,12},{1,9},{5... | collective-permute-start | bytes 294920 | tf_op jit(solution)/shard_map/ppermute | solution.py:51
  18.3 5.1 %collective-permute-start.9 = (bf16[16,3072]{1,0:T(8,128)(2,1)S(1)}, bf16[16,3072]{1,0:T(8,128)(2,1)S(1)}, u32[]{:S(2)}, u32[]{:S(2)}) collective-permute-start(bf16[16,3072]{1,0:T(8,128)(2,1)S(1)} %get-tuple-element.58), channel_id=1, source_target_pairs={{0,12},{4,16},{8,4},{12,24},{16,28},{20,0},{24,20},{28,8},{1,13},{... | collective-permute-start | bytes 294920 | tf_op jit(solution)/shard_map/ppermute | solution.py:51
  19.6 4.7 %collective-permute-start.10 = (bf16[16,3072]{1,0:T(8,128)(2,1)S(1)}, bf16[16,3072]{1,0:T(8,128)(2,1)S(1)}, u32[]{:S(2)}, u32[]{:S(2)}) collective-permute-start(bf16[16,3072]{1,0:T(8,128)(2,1)S(1)} %get-tuple-element.59), channel_id=1, source_target_pairs={{0,16},{4,12},{8,24},{12,4},{16,0},{20,28},{24,8},{28,20},{1,17},{... | collective-permute-start | bytes 294920 | tf_op jit(solution)/shard_map/ppermute | solution.py:51
  19.9 5.0 %collective-permute-start.11 = (bf16[16,3072]{1,0:T(8,128)(2,1)S(1)}, bf16[16,3072]{1,0:T(8,128)(2,1)S(1)}, u32[]{:S(2)}, u32[]{:S(2)}) collective-permute-start(bf16[16,3072]{1,0:T(8,128)(2,1)S(1)} %get-tuple-element.60), channel_id=1, source_target_pairs={{0,20},{4,8},{8,28},{12,0},{16,4},{20,24},{24,12},{28,16},{1,21},{... | collective-permute-start | bytes 294920 | tf_op jit(solution)/shard_map/ppermute | solution.py:51
  25.3 5.9 %collective-permute-start.12 = (bf16[32,768]{1,0:T(8,128)(2,1)S(1)}, bf16[32,768]{1,0:T(8,128)(2,1)S(1)}, u32[]{:S(2)}, u32[]{:S(2)}) collective-permute-start(bf16[32,768]{1,0:T(8,128)(2,1)S(1)} %get-tuple-element.62), channel_id=1, source_target_pairs={{0,1},{1,2},{2,3},{3,0},{4,5},{5,6},{6,7},{7,4},{8,9},{9,10},{10,1... | collective-permute-start | bytes 147464 | tf_op jit(solution)/shard_map/ppermute | solution.py:45
  26.9 6.5 %collective-permute-start.13 = (bf16[32,768]{1,0:T(8,128)(2,1)S(1)}, bf16[32,768]{1,0:T(8,128)(2,1)S(1)}, u32[]{:S(2)}, u32[]{:S(2)}) collective-permute-start(bf16[32,768]{1,0:T(8,128)(2,1)S(1)} %get-tuple-element.63), channel_id=1, source_target_pairs={{0,2},{1,3},{2,0},{3,1},{4,6},{5,7},{6,4},{7,5},{8,10},{9,11},{10,... | collective-permute-start | bytes 147464 | tf_op jit(solution)/shard_map/ppermute | solution.py:45
  29.5 4.3 %collective-permute-start.14 = (bf16[32,768]{1,0:T(8,128)(2,1)S(1)}, bf16[32,768]{1,0:T(8,128)(2,1)S(1)}, u32[]{:S(2)}, u32[]{:S(2)}) collective-permute-start(bf16[32,768]{1,0:T(8,128)(2,1)S(1)} %get-tuple-element.64), channel_id=1, source_target_pairs={{0,3},{1,0},{2,1},{3,2},{4,7},{5,4},{6,5},{7,6},{8,11},{9,8},{10,9... | collective-permute-start | bytes 147464 | tf_op jit(solution)/shard_map/ppermute | solution.py:45
